TPU v7x, 256 devices: a whole 4x4x8 slice. The times are simulated.
256 devices in a mesh: dom: 64 (over x, y_lo, z), rep: 4 (over y_hi, core).
Axes of the slice: x: 4, y: 4 (y_hi: 2, y_lo: 2; y = y_hi * 2 + y_lo), z: 8, core: 2. Of those that a mesh axis runs over, the one named last changes fastest.
Arguments:
- left_embedding: float32 [16384, 400], P('dom'), may hold values from -1.8 to 1.8
- left_state: float32 [16384], P('dom'), may hold values from 0.01 to 1
- right_embedding: float32 [16384, 400], P('dom'), may hold values from -1.8 to 1.8
- right_state: float32 [16384], P('dom'), may hold values from 0.01 to 1
- relation: float32 [1536, 400], replicated, may hold values from -4 to 4
- sources: int32 [64, 2048], P('dom', 'rep'), may hold values from 0 to 255
- relation_ids: int32 [64, 2048], P('dom', 'rep'), may hold values from 0 to 1535, as said below
- destinations: int32 [64, 2048], P('dom', 'rep'), may hold values from 0 to 255
- negatives_left: int32 [64, 4, 1000], P('dom', 'rep'), may hold values from 0 to 255
- negatives_right: int32 [64, 4, 1000], P('dom', 'rep'), may hold values from 0 to 255
- edge_counts: int32 [64], P('dom'), may hold values from 682 to 2048, as said below
Outputs:
- left_next: float32 [16384, 400], P('dom')
- left_state_next: float32 [16384], P('dom')
- right_next: float32 [16384, 400], P('dom')
- right_state_next: float32 [16384], P('dom')
- relation_grad: float32 [1536, 400], replicated
Inputs may be any that keep to these rules, and one draw needn't show every extreme that they name: `relation_ids`: integers of 0 to 1535. The live edges of a bucket are its first edge_counts slots; some bucket is full.
All inputs are finite; a program needn't handle non-finite values.
Results may differ from a plain program's by a relative error of at most 0.0003.
Values sent between devices are 32-bit elements; how exact they have to be, the bound alone decides.
No kernel may reach another device: no remote copies, remote signals or barrier semaphores. Data moves between devices by JAX's collectives and lax.ppermute only.
A program may use at most 64 MiB of HBM per device.

v0:
```python
import jax
import jax.numpy as jnp
from jax import lax
from jax.sharding import PartitionSpec as P

MARGIN = 0.1
LEARN_RATE = 0.1
HIGHEST = lax.Precision.HIGHEST


def shifted(shard, axis, by):
    peers = lax.axis_size(axis)
    return lax.ppermute(shard, axis, [(i, (i + by) % peers) for i in range(peers)])


def complex_product(vectors, weights):
    half_width = vectors.shape[-1] // 2
    vec_real, vec_imag = (vectors[:, :half_width], vectors[:, half_width:])
    weight_real, weight_imag = (weights[:, :half_width], weights[:, half_width:])
    return jnp.concatenate(
        [
            vec_real * weight_real - vec_imag * weight_imag,
            vec_real * weight_imag + vec_imag * weight_real,
        ],
        axis=1,
    )


def complex_adjoint(vectors, weights):
    half_width = vectors.shape[-1] // 2
    vec_real, vec_imag = (vectors[:, :half_width], vectors[:, half_width:])
    weight_real, weight_imag = (weights[:, :half_width], weights[:, half_width:])
    return jnp.concatenate(
        [
            vec_real * weight_real + vec_imag * weight_imag,
            vec_imag * weight_real - vec_real * weight_imag,
        ],
        axis=1,
    )


def batch_loss(
    left_rows,
    right_rows,
    relation,
    sources,
    relation_ids,
    destinations,
    negatives_left,
    negatives_right,
    edge_mask,
):
    weights = relation[relation_ids]
    targets = right_rows[destinations]
    queries = complex_product(left_rows[sources], weights)
    probes = complex_adjoint(targets, weights)
    positive = jnp.sum(queries * targets, axis=1)
    contract = (((1,), (1,)), ((), ()))
    score_right = lax.dot_general(
        queries,
        right_rows[negatives_right],
        contract,
        precision=HIGHEST,
        preferred_element_type=jnp.float32,
    )
    score_left = lax.dot_general(
        probes,
        left_rows[negatives_left],
        contract,
        precision=HIGHEST,
        preferred_element_type=jnp.float32,
    )
    hinge_right = jnp.mean(jax.nn.softplus(MARGIN - positive[:, None] + score_right), axis=1)
    hinge_left = jnp.mean(jax.nn.softplus(MARGIN - positive[:, None] + score_left), axis=1)
    return jnp.sum((hinge_right + hinge_left) * edge_mask)


def adagrad_rows(embedding, state, gradient):
    new_state = state + jnp.mean(gradient * gradient, axis=1)
    return (embedding - LEARN_RATE * gradient / jnp.sqrt(new_state)[:, None], new_state)


def body(
    left_embedding,
    left_state,
    right_embedding,
    right_state,
    relation,
    sources,
    relation_ids,
    destinations,
    negatives_left,
    negatives_right,
    edge_counts,
):
    batch_number = negatives_left.shape[1]
    edge_slots = sources.shape[1]
    batch_size = edge_slots // batch_number
    slot_ids = lax.axis_index("rep") * edge_slots + jnp.arange(edge_slots, dtype=jnp.int32)
    edge_mask = (slot_ids < edge_counts[0]).astype(jnp.float32)
    number = 0
    edge_span = slice(number * batch_size, (number + 1) * batch_size)

    def run_batch(unused, edge_span=edge_span, number=number):

        def loss_of(left_param, right_param, relation_param):
            return batch_loss(
                left_param,
                right_param,
                relation_param,
                sources[0, edge_span],
                relation_ids[0, edge_span],
                destinations[0, edge_span],
                negatives_left[0, number],
                negatives_right[0, number],
                edge_mask,
            )

        loss_sum, pullback = jax.vjp(loss_of, left_embedding, right_embedding, relation)
        return pullback(jnp.ones((), jnp.float32))

    def skip_batch(unused):
        return (
            jnp.zeros_like(left_embedding),
            jnp.zeros_like(right_embedding),
            jnp.zeros_like(relation),
        )

    batch_left, batch_right, batch_relation = lax.cond(
        jnp.sum(edge_mask) > 0, run_batch, skip_batch, 0
    )
    summed_left, summed_right = lax.psum((batch_left, batch_right), "rep")
    left_next, left_state_next = adagrad_rows(left_embedding, left_state, summed_left)
    right_new, right_state_new = adagrad_rows(right_embedding, right_state, summed_right)
    right_next, right_state_next = shifted((right_new, right_state_new), "dom", -1)
    relation_grad = lax.psum(batch_relation, ("dom", "rep"))
    return (left_next, left_state_next, right_next, right_state_next, relation_grad)


def solution(mesh):
    in_specs = (
        P("dom", None),
        P("dom"),
        P("dom", None),
        P("dom"),
        P(),
        P("dom", "rep"),
        P("dom", "rep"),
        P("dom", "rep"),
        P("dom", "rep", None),
        P("dom", "rep", None),
        P("dom"),
    )
    out_specs = (P("dom", None), P("dom"), P("dom", None), P("dom"), P())
    return jax.shard_map(body, mesh=mesh, in_specs=in_specs, out_specs=out_specs, check_vma=False)
```

profile of v0, /device:TPU:1, one launch (start us, length us, event | category | flops | bytes accessed | tf_op | source)
XLA Modules:
  0.0 452.0 jit_solution(4521073793230996050)
XLA Ops:
  9.1 107.5 %conditional.1 = (f32[256,400]{1,0:T(8,128)}, f32[256,400]{1,0:T(8,128)}, f32[1536,400]{1,0:T(8,128)}) conditional(s32[]{:T(128)} %convert_element_type.7, () %tuple.16, (s32[1,1,1000]{2,1,0:T(1,128)}, f32[512]{0:T(512)S(1)}, s32[1,512]{1,0:T(1,128)}, f32[256,400]{0,1:T(8,128)}, s32[1,512]{1,0:T(1,128)}, /*index=5*/f32[1536,400]{0,1:T(8,128)}, ...), branch_computations={%region_1.0_spmd, %region_2.11_spmd} | conditional | flops 14769046528 | bytes 137890752 | solution.py:129
  11.1 4.9 %gather_fusion.3 = f32[1000,400]{1,0:T(8,128)} fusion(f32[256,400]{1,0:T(8,128)S(1)} %copy.49, s32[1024]{0:T(1024)S(1)} %pad_clamp_fusion.1), kind=kCustom, calls=%fused_computation.3 | custom fusion | bytes 3204000 | tf_op jit(solution)/shard_map/cond/branch_1_fun/jvp()/gather | solution.py:68
  15.9 3.4 copy.50
  19.4 3.9 gather_fusion.1
  27.6 2.2 gather_fusion
  34.6 5.0 %fusion.29 = (f32[512]{0:T(512)S(1)}, f32[512,1000]{0,1:T(8,128)S(1)}) fusion(f32[1000,400]{1,0:T(8,128)S(1)} %copy-done, f32[512,200]{0,1:T(8,128)S(1)} %get-tuple-element.83, f32[512,200]{0,1:T(8,128)S(1)} %get-tuple-element.82, f32[512]{0:T(512)S(1)} %broadcast_subtract_fusion, f32[512]{0:T(512)S(1)} %broadcast_multiply_fusion), kind=kOutput, calls=%fused_computation.84 | convolution fusion | flops 2464972288 | bytes 4473344 | tf_op jit(solution)/shard_map/cond/branch_1_fun/jvp()/dot_general | solution.py:66
  41.0 4.7 %fusion.8 = f32[1000,400]{1,0:T(8,128)} fusion(f32[512,1000]{0,1:T(8,128)S(1)} %get-tuple-element.99, f32[512,200]{0,1:T(8,128)S(1)} %get-tuple-element.83, f32[512,200]{0,1:T(8,128)S(1)} %get-tuple-element.82), kind=kOutput, calls=%fused_computation.31 | convolution fusion | flops 2457804800 | bytes 4467200 | tf_op jit(solution)/shard_map/cond/branch_1_fun/transpose(jvp())/dot_general | solution.py:66
  45.6 8.2 %scatter_custom_fusion = f32[256,400]{1,0:T(8,128)} fusion(s32[1000]{0:T(1024)S(1)} %bitcast.29, f32[1000,400]{1,0:T(8,128)} %fusion.8, f32[]{:T(128)} %constant.12.clone), kind=kCustom, calls=%fused_computation.51 | custom fusion | flops 400000 | bytes 410112 | tf_op jit(solution)/shard_map/cond/branch_1_fun/transpose(jvp())/scatter-add | solution.py:68
  53.8 6.5 %fusion.30 = f32[512,400]{0,1:T(8,128)} fusion(f32[512,1000]{0,1:T(8,128)} %copy-done.1, f32[1000,400]{1,0:T(8,128)S(1)} %copy-done), kind=kOutput, calls=%fused_computation.85 | convolution fusion | flops 2457600000 | bytes 4467200 | tf_op jit(solution)/shard_map/cond/branch_1_fun/transpose(jvp())/dot_general | solution.py:66
  60.4 5.1 %gather_fusion.4 = f32[1000,400]{1,0:T(8,128)} fusion(f32[256,400]{1,0:T(8,128)S(1)} %copy.51, s32[1024]{0:T(1024)S(1)} %pad_clamp_fusion), kind=kCustom, calls=%fused_computation.4 | custom fusion | bytes 3204000 | tf_op jit(solution)/shard_map/cond/branch_1_fun/jvp()/gather | solution.py:61
  65.5 6.9 %fusion.28 = (f32[512]{0:T(512)S(1)}, f32[512,1000]{0,1:T(8,128)S(1)}) fusion(f32[1000,400]{1,0:T(8,128)} %gather_fusion.4, f32[512,200]{0,1:T(8,128)S(1)} %copy-done.6, f32[512,200]{0,1:T(8,128)} %copy-done.7, f32[512]{0:T(512)S(1)} %broadcast_subtract_fusion, f32[512]{0:T(512)S(1)} %broadcast_multiply_fusion), kind=kOutput, calls=%fused_computation.83 | convolution fusion | flops 2464972288 | bytes 4473344 | tf_op jit(solution)/shard_map/cond/branch_1_fun/jvp()/dot_general | solution.py:59
  72.4 4.1 convolution_add_fusion
  79.2 2.5 copy.45
  81.7 5.3 %scatter_custom_fusion.1 = f32[256,400]{1,0:T(8,128)} fusion(s32[512]{0:T(512)S(1)} %bitcast.31, f32[512,400]{1,0:T(8,128)} %copy.45, f32[]{:T(128)} %constant.12.clone), kind=kCustom, calls=%fused_computation.49 | custom fusion | flops 204800 | bytes 410112 | tf_op jit(solution)/shard_map/cond/branch_1_fun/transpose(jvp())/scatter-add | solution.py:55
  89.1 4.6 %fusion.9 = f32[1000,400]{1,0:T(8,128)} fusion(f32[512,1000]{0,1:T(8,128)S(1)} %get-tuple-element.97, f32[512,200]{0,1:T(8,128)S(1)} %copy-done.6, f32[512,200]{0,1:T(8,128)S(1)} %copy-done.8), kind=kOutput, calls=%fused_computation.44 | convolution fusion | flops 2457804800 | bytes 4467200 | tf_op jit(solution)/shard_map/cond/branch_1_fun/transpose(jvp())/dot_general | solution.py:59
  93.7 8.0 %scatter_custom_fusion.2 = f32[256,400]{1,0:T(8,128)} fusion(s32[1000]{0:T(1024)S(1)} %bitcast.27, f32[1000,400]{1,0:T(8,128)} %fusion.9, f32[]{:T(128)} %constant.12.clone), kind=kCustom, calls=%fused_computation.47 | custom fusion | flops 400000 | bytes 410112 | tf_op jit(solution)/shard_map/cond/branch_1_fun/transpose(jvp())/scatter-add | solution.py:61
  104.3 4.7 %scatter_custom_fusion.3 = f32[256,400]{1,0:T(8,128)S(1)} fusion(s32[512]{0:T(512)S(1)} %bitcast.35, f32[512,400]{1,0:T(8,128)} %copy.47, f32[]{:T(128)} %constant.12.clone), kind=kCustom, calls=%fused_computation.45 | custom fusion | flops 204800 | bytes 410112 | tf_op jit(solution)/shard_map/cond/branch_1_fun/transpose(jvp())/scatter-add | solution.py:54
  110.8 5.4 %scatter_custom_fusion.4 = f32[1536,400]{1,0:T(8,128)} fusion(s32[512]{0:T(512)S(1)} %bitcast.33, f32[512,400]{1,0:T(8,128)S(1)} %copy.48, f32[]{:T(128)} %constant.12.clone), kind=kCustom, calls=%fused_computation.22 | custom fusion | flops 204800 | bytes 2457604 | tf_op jit(solution)/shard_map/cond/branch_1_fun/transpose(jvp())/scatter-add | solution.py:53
  120.7 3.4 copy.54
  124.1 49.9 %all-reduce.14.cloned.1.call-done = (f32[256,400]{0,1:T(8,128)}, f32[256,400]{0,1:T(8,128)}) async-done(((f32[256,400]{0,1:T(8,128)}, f32[256,400]{0,1:T(8,128)}), (f32[256,400]{0,1:T(8,128)}, f32[256,400]{0,1:T(8,128)})) %all-reduce.14.cloned.1.call-update) | async-done | bytes 819216 | tf_op jit(solution)/shard_map/psum | solution.py:132
  176.2 5.3 %collective-permute-start = (f32[256,400]{0,1:T(8,128)S(1)}, f32[256,400]{0,1:T(8,128)S(1)}, u32[]{:S(2)}, u32[]{:S(2)}) collective-permute-start(f32[256,400]{0,1:T(8,128)S(1)} %divide_subtract_fusion), channel_id=1, source_target_pairs={{0,252},{4,0},{8,4},{12,8},{16,12},{20,16},{24,20},{28,24},{32,28}... | collective-permute-start | bytes 1228808 | tf_op jit(solution)/shard_map/ppermute | solution.py:13
  185.0 5.2 %collective-permute-done.1 = f32[256]{0:T(256)S(1)} collective-permute-done((f32[256]{0:T(256)S(1)}, f32[256]{0:T(256)S(1)}, u32[]{:S(2)}, u32[]{:S(2)}) %collective-permute-start.1) | collective-permute-done | bytes 1056 | tf_op jit(solution)/shard_map/ppermute | solution.py:13
  190.2 250.2 %all-reduce.12.cloned.1.call-done = f32[1536,400]{0,1:T(8,128)} async-done(((f32[1536,400]{0,1:T(8,128)}), f32[1536,400]{0,1:T(8,128)}) %all-reduce.12.cloned.1.call-update) | async-done | bytes 2457616 | tf_op jit(solution)/shard_map/psum | solution.py:136
  441.7 3.3 copy.75
  (104 shorter events, 33.0 us)
Async XLA Ops:
  7.2 166.9 %all-reduce.14.cloned.1.call-start = ((), (), s32[]{:S(2)}) async-start(), calls=%async_computation.1 | async-start | bytes 1638400 | tf_op jit(solution)/shard_map/psum | solution.py:132
  15.9 3.4 copy-start.23
  15.9 3.4 copy-start.24
  23.3 2.1 copy-start.18
  31.9 2.7 copy-start
  60.4 5.1 %copy-start.6 = (f32[512,200]{0,1:T(8,128)S(1)}, f32[512,200]{0,1:T(8,128)}, u32[]{:S(2)}) copy-start(f32[512,200]{0,1:T(8,128)} %copy-done.5) | copy-start | bytes 1228804 | tf_op jit(solution)/shard_map/cond
  65.5 6.9 %copy-start.2 = (f32[1000,400]{1,0:T(8,128)S(1)}, f32[1000,400]{1,0:T(8,128)}, u32[]{:S(2)}) copy-start(f32[1000,400]{1,0:T(8,128)} %gather_fusion.4) | copy-start | bytes 4800004 | tf_op jit(solution)/shard_map/cond
  72.4 4.2 copy-start.11
  72.4 4.2 copy-start.12
  72.4 4.2 copy-start.13
  79.2 9.9 %copy-start.8 = (f32[512,200]{0,1:T(8,128)S(1)}, f32[512,200]{0,1:T(8,128)}, u32[]{:S(2)}) copy-start(f32[512,200]{0,1:T(8,128)} %copy-done.7) | copy-start | bytes 1228804 | tf_op jit(solution)/shard_map/cond
  89.1 12.7 %copy-start.20 = (f32[512,200]{0,1:T(8,128)S(1)}, f32[512,200]{0,1:T(8,128)}, u32[]{:S(2)}) copy-start(f32[512,200]{0,1:T(8,128)} %get-tuple-element.90) | copy-start | bytes 1228804 | tf_op jit(solution)/shard_map/cond
  103.0 6.0 %copy-start.14 = (f32[256,400]{1,0:T(8,128)S(1)}, f32[256,400]{1,0:T(8,128)}, u32[]{:S(2)}) copy-start(f32[256,400]{1,0:T(8,128)} %scatter_custom_fusion.2) | copy-start | bytes 1228804 | tf_op jit(solution)/shard_map/cond
  103.0 6.9 %copy-start.4 = (f32[512,400]{0,1:T(8,128)S(1)}, f32[512,400]{0,1:T(8,128)}, u32[]{:S(2)}) copy-start(f32[512,400]{0,1:T(8,128)} %copy-done.3) | copy-start | bytes 2457604 | tf_op jit(solution)/shard_map/cond
  103.0 6.9 %copy-start.9 = (f32[512,200]{0,1:T(8,128)S(1)}, f32[512,200]{0,1:T(8,128)}, u32[]{:S(2)}) copy-start(f32[512,200]{0,1:T(8,128)} %copy.59) | copy-start | bytes 1228804 | tf_op jit(solution)/shard_map/cond
  103.0 6.9 %copy-start.10 = (f32[512,200]{0,1:T(8,128)S(1)}, f32[512,200]{0,1:T(8,128)}, u32[]{:S(2)}) copy-start(f32[512,200]{0,1:T(8,128)} %copy.57) | copy-start | bytes 1228804 | tf_op jit(solution)/shard_map/cond
  120.6 319.8 %all-reduce.12.cloned.1.call-start = ((), (), s32[]{:S(2)}) async-start(), calls=%async_computation | async-start | bytes 4915200 | tf_op jit(solution)/shard_map/psum | solution.py:136
  124.0 51.1 %copy-start.25 = (f32[256]{0:T(256)S(1)}, f32[256]{0:T(256)}, u32[]{:S(2)}) copy-start(f32[256]{0:T(256)} %param.16) | copy-start | bytes 3076
  124.0 51.1 %copy-start.17 = (f32[256,400]{0,1:T(8,128)S(1)}, f32[256,400]{0,1:T(8,128)}, u32[]{:S(2)}) copy-start(f32[256,400]{0,1:T(8,128)} %param.15) | copy-start | bytes 1228804
  124.0 59.6 %copy-start.26 = (f32[256]{0:T(256)S(1)}, f32[256]{0:T(256)}, u32[]{:S(2)}) copy-start(f32[256]{0:T(256)} %param.14) | copy-start | bytes 3076
  124.0 60.2 %copy-start.19 = (f32[256,400]{0,1:T(8,128)S(1)}, f32[256,400]{0,1:T(8,128)}, u32[]{:S(2)}) copy-start(f32[256,400]{0,1:T(8,128)} %param.13) | copy-start | bytes 1228804
  174.0 10.2 %copy-start.21 = (f32[256,400]{0,1:T(8,128)S(1)}, f32[256,400]{0,1:T(8,128)}, u32[]{:S(2)}) copy-start(f32[256,400]{0,1:T(8,128)} %get-tuple-element.68) | copy-start | bytes 1228804
  176.2 14.0 %collective-permute-start = (f32[256,400]{0,1:T(8,128)S(1)}, f32[256,400]{0,1:T(8,128)S(1)}, u32[]{:S(2)}, u32[]{:S(2)}) collective-permute-start(f32[256,400]{0,1:T(8,128)S(1)} %divide_subtract_fusion), channel_id=1, source_target_pairs={{0,252},{4,0},{8,4},{12,8},{16,12},{20,16},{24,20},{28,24},{32,28}... | collective-permute-start | bytes 1228808 | tf_op jit(solution)/shard_map/ppermute | solution.py:13
  181.5 8.7 %collective-permute-start.1 = (f32[256]{0:T(256)S(1)}, f32[256]{0:T(256)S(1)}, u32[]{:S(2)}, u32[]{:S(2)}) collective-permute-start(f32[256]{0:T(256)S(1)} %get-tuple-element.71), channel_id=1, source_target_pairs={{0,252},{4,0},{8,4},{12,8},{16,12},{20,16},{24,20},{28,24},{32,28}... | collective-permute-start | bytes 3080 | tf_op jit(solution)/shard_map/ppermute | solution.py:13
  (7 other events, 8.9 us)
Sparse Core Ops, SparseCore 0:
  120.7 53.2 all-reduce.13
  180.1 260.3 all-reduce.11
where the time goes:
time: 458 us; the launch traced here: 452 us
  waiting for transfers between devices  305 us (67%)
  other arithmetic  46.6 us (10%)
  local copies, waits for them, and re-layouts  45.3 us (10%)
  matrix products  31.9 us (7%)
  between operations  15.5 us (3%)
  starting transfers between devices  6.43 us (1%)
    psum x1, waiting for transfers between devices, body(): relation_grad = lax.psum(batch_relation, ('dom', 'rep'))  250 us
    psum x1, waiting for transfers between devices, body(): summed_left, summed_right = lax.psum((batch_left, batch_right), 'rep')  49.9 us
    dot_general x3, matrix products, batch_loss(): lax.dot_general(probes, left_rows[negatives_left], contract, precision=HI...  16.2 us
    dot_general x3, matrix products, batch_loss(): lax.dot_general(queries, right_rows[negatives_right], contract, precision...  15.7 us
  transfers between devices with their start and end apart: 4, of which 3 were waited for; matrix products, arithmetic and copies ran while one was open for 2% of the time, Pallas kernels for 0%

commit v1 on v0

v1 whole, which is shorter than its diff:
```python
import jax
import jax.numpy as jnp
from jax import lax
from jax.sharding import PartitionSpec as P
from jax.experimental import pallas as pl
from jax.experimental.pallas import tpu as pltpu

MARGIN = 0.1
LEARN_RATE = 0.1
F32 = jnp.float32
BF16 = jnp.bfloat16
NN = (((1,), (0,)), ((), ()))
NT = (((1,), (1,)), ((), ()))


def parts(value):
    high = value.astype(BF16)
    return high, (value - high.astype(F32)).astype(BF16)


def dot(a, b, dims):
    return lax.dot_general(a, b, dims, preferred_element_type=F32)


def dot_picked(value, picks, dims):
    high, low = parts(value)
    return dot(high, picks, dims) + dot(low, picks, dims)


def dot_split(a, b, dims):
    return dot(a[0], b[0], dims) + (dot(a[0], b[1], dims) + dot(a[1], b[0], dims))


def product(v, w):
    return v[0] * w[0] - v[1] * w[1], v[0] * w[1] + v[1] * w[0]


def adjoint(v, w):
    return v[0] * w[0] + v[1] * w[1], v[1] * w[0] - v[0] * w[1]


def halves(x):
    half = x.shape[0] // 2
    return x[:half], x[half:]


def one_hot(ids, rows):
    return (lax.broadcasted_iota(jnp.int32, (rows, ids.shape[1]), 0) == ids).astype(F32)


CORES, X_SIZE, Y_SIZE, Z_SIZE = 2, 4, 4, 8
DEVICES = CORES * X_SIZE * Y_SIZE * Z_SIZE
LANES = 128
VMEM_LIMIT = 56 * 1024 * 1024


def place(dom, rep):
    return rep % 2, dom // 16, (rep // 2) * 2 + (dom // 8) % 2, dom % 8


def device(core, x, y, z):
    return ((x * 2 + y % 2) * 8 + z) * 4 + (y // 2) * 2 + core


def send(value, target):
    pairs = []
    for n in range(DEVICES):
        pairs.append((n, device(*target(*place(n // 4, n % 4)))))
    return lax.ppermute(value, ("dom", "rep"), pairs)


def to_core(value):
    return send(value, lambda core, x, y, z: (1 - core, x, y, z))


def to_x(value, step):
    return send(value, lambda core, x, y, z: (core, (x + step) % X_SIZE, y, z))


def to_y(value, step):
    return send(value, lambda core, x, y, z: (core, x, (y + step) % Y_SIZE, z))


def to_z(value, bit):
    return send(value, lambda core, x, y, z: (core, x, y, z ^ bit))


def to_bucket_before(value):
    pairs = []
    for n in range(DEVICES):
        pairs.append((n, (n - 4) % DEVICES))
    return lax.ppermute(value, ("dom", "rep"), pairs)


def piece_rows(total):
    block = total // LANES // (CORES * X_SIZE)
    piece = -(-block // (8 * Y_SIZE)) * 8
    return block, piece


def spans(width, types):
    block, piece = piece_rows(width * types)
    pad = piece * Y_SIZE - block
    found = []
    for k in range(types // LANES):
        row, end = k * width, (k + 1) * width
        while row < end:
            stop = min(end, (row // block + 1) * block)
            found.append((k, row - k * width, stop - row, row + (row // block) * pad))
            row = stop
    return found


def piece_at(half, x, y, r, s, piece):
    block = half * X_SIZE + (x + r) % X_SIZE
    return pl.multiple_of((block * Y_SIZE + (y + s) % Y_SIZE) * piece, 8)


def grad_kernel(place_ref, counts_ref, left_ref, right_ref, rel_ref, src_ref, rid_ref, dst_ref, negl_ref, negr_ref,
                rel_send_ref, rel_keep_ref, lr_send_ref, lr_keep_ref, rows_ref):
    slots = src_ref.shape[1]
    rows = left_ref.shape[1]
    types = rel_ref.shape[1]
    negatives = negl_ref.shape[1]
    left, right = left_ref[...], right_ref[...]
    left_parts, right_parts = parts(left), parts(right)
    pick_src = one_hot(src_ref[...], rows).astype(BF16)
    pick_dst = one_hot(dst_ref[...], rows).astype(BF16)
    pick_rel = one_hot(rid_ref[...], types).astype(BF16)
    source = dot(left_parts[0], pick_src, NN) + dot(left_parts[1], pick_src, NN)
    target = dot(right_parts[0], pick_dst, NN) + dot(right_parts[1], pick_dst, NN)
    weight = dot_picked(rel_ref[...], pick_rel, NN)
    s, t, w = halves(source), halves(target), halves(weight)
    q = jnp.concatenate(product(s, w), axis=0)
    p = jnp.concatenate(adjoint(t, w), axis=0)
    positive = jnp.sum(q * target, axis=0, keepdims=True)
    q_parts, p_parts = parts(q), parts(p)
    right_rows, left_rows = parts(right.T), parts(left.T)
    count_right = jnp.sum(one_hot(negr_ref[...], rows), axis=1, keepdims=True)
    count_left = jnp.sum(one_hot(negl_ref[...], rows), axis=1, keepdims=True)
    slot = lax.broadcasted_iota(jnp.int32, (1, slots), 1)
    live = (slot + place_ref[3] * slots < counts_ref[0]).astype(F32) * (1.0 / negatives)
    offset = MARGIN - positive
    g_right = jax.nn.sigmoid(offset + dot_split(right_rows, q_parts, NN)) * count_right * live
    g_left = jax.nn.sigmoid(offset + dot_split(left_rows, p_parts, NN)) * count_left * live
    d_pos = -(jnp.sum(g_right, axis=0, keepdims=True) + jnp.sum(g_left, axis=0, keepdims=True))
    gr_parts, gl_parts = parts(g_right), parts(g_left)
    d_q = dot_split(right_parts, gr_parts, NN) + d_pos * target
    d_p = dot_split(left_parts, gl_parts, NN)
    dq, dp = halves(d_q), halves(d_p)
    a, b = adjoint(dq, s), adjoint(dp, t)
    d_w = jnp.concatenate([a[0] + b[0], a[1] - b[1]], axis=0)
    d_relation = dot_picked(d_w, pick_rel, NT)
    width = d_relation.shape[0]
    core, x, y = place_ref[0], place_ref[1], place_ref[2]
    block, piece = piece_rows(width * types)
    pad = piece * Y_SIZE - block
    if pad:
        for k in range(CORES * X_SIZE):
            rows_ref[(k + 1) * (block + pad) - pad:(k + 1) * (block + pad), :] = jnp.zeros((pad, LANES), F32)
    for k, start, size, row in spans(width, types):
        rows_ref[row:row + size, :] = d_relation[start:start + size, k * LANES:(k + 1) * LANES]
    for out_ref, half in ((rel_send_ref, 1 - core), (rel_keep_ref, core)):
        for r in range(X_SIZE):
            for s in range(Y_SIZE):
                to = (r * Y_SIZE + s) * piece
                out_ref[to:to + piece, :] = rows_ref[pl.ds(piece_at(half, x, y, r, s, piece), piece), :]
    d_s = jnp.concatenate(adjoint(dq, w), axis=0)
    d_left = dot_split(p_parts, gl_parts, NT) + dot_picked(d_s, pick_src, NT)
    d_t = jnp.concatenate(product(dp, w), axis=0) + d_pos * q
    d_right = dot_split(q_parts, gr_parts, NT) + dot_picked(d_t, pick_dst, NT)
    first = core == 0
    half = rows // CORES
    for at, grad in ((0, d_left), (width, d_right)):
        low, high = grad[:, :half], grad[:, half:]
        lr_keep_ref[at:at + width, :] = jnp.where(first, low, high)
        lr_send_ref[at:at + width, :] = jnp.where(first, high, low)


SCALAR, WHOLE = pl.BlockSpec(memory_space=pltpu.SMEM), pl.BlockSpec(memory_space=pltpu.VMEM)


def call(kernel, scalars, arrays, shapes, scratch=()):
    return pl.pallas_call(
        kernel,
        out_shape=[jax.ShapeDtypeStruct(shape, F32) for shape in shapes],
        in_specs=[SCALAR] * len(scalars) + [WHOLE] * len(arrays),
        out_specs=[WHOLE] * len(shapes),
        scratch_shapes=[pltpu.VMEM(shape, F32) for shape in scratch],
        compiler_params=pltpu.CompilerParams(vmem_limit_bytes=VMEM_LIMIT),
    )(*scalars, *arrays)


def adagrad_kernel(place_ref, kept_ref, got_ref, left_ref, right_ref, left_state_ref, right_state_ref, new_left_ref, new_right_ref):
    width = left_ref.shape[0]
    first = place_ref[0] == 0
    for at, rows_ref, state_ref, out_ref in (
        (0, left_ref, left_state_ref, new_left_ref),
        (width, right_ref, right_state_ref, new_right_ref),
    ):
        half = rows_ref.shape[1] // CORES
        gradient = kept_ref[at:at + width, :] + got_ref[at:at + width, :]
        embedding = jnp.where(first, rows_ref[:, :half], rows_ref[:, half:])
        state = jnp.where(first, state_ref[:, :half], state_ref[:, half:])
        new_state = state + jnp.sum(gradient * gradient, axis=0, keepdims=True) * (1.0 / width)
        out_ref[:width, :] = embedding - gradient * (LEARN_RATE / jnp.sqrt(new_state))
        out_ref[width:, :] = jnp.broadcast_to(new_state, (8, half))


def join_kernel(place_ref, own_left_ref, other_left_ref, own_right_ref, other_right_ref, left_ref, left_state_ref, right_ref, right_state_ref):
    first = place_ref[0] == 0
    width = left_ref.shape[0]
    half = own_left_ref.shape[1]
    for own_ref, other_ref, rows_ref, state_ref in (
        (own_left_ref, other_left_ref, left_ref, left_state_ref),
        (own_right_ref, other_right_ref, right_ref, right_state_ref),
    ):
        own, other = own_ref[...], other_ref[...]
        for at, value in ((0, jnp.where(first, own, other)), (half, jnp.where(first, other, own))):
            rows_ref[:, at:at + half] = value[:width]
            state_ref[:, at:at + half] = value[width:width + 1]


def relation_kernel(place_ref, own_ref, other_ref, out_ref, rows_ref):
    core, x, y = place_ref[0], place_ref[1], place_ref[2]
    width, types = out_ref.shape
    piece = piece_rows(width * types)[1]
    for in_ref, half in ((own_ref, core), (other_ref, 1 - core)):
        for r in range(X_SIZE):
            for s in range(Y_SIZE):
                at = (r * Y_SIZE + s) * piece
                rows_ref[pl.ds(piece_at(half, x, y, r, s, piece), piece), :] = in_ref[at:at + piece, :]
    for k, start, size, row in spans(width, types):
        out_ref[start:start + size, k * LANES:(k + 1) * LANES] = rows_ref[row:row + size, :]


def scatter(pieces, move):
    return sum([move(pieces[r], r) for r in range(1, len(pieces))], pieces[0])


def gather(own, count, move):
    return jnp.concatenate([own] + [move(own, (count - r) % count) for r in range(1, count)], axis=0)


def body(left_embedding, left_state, right_embedding, right_state, relation, sources, relation_ids, destinations, negatives_left, negatives_right, edge_counts):
    left, right, relation = left_embedding.T, right_embedding.T, relation.T
    width, types = relation.shape
    rows = left.shape[1]
    rep = lax.axis_index("rep")
    core, x, y, _ = place(lax.axis_index("dom"), rep)
    where = jnp.stack([core, x, y, rep]).astype(jnp.int32)
    piece = piece_rows(width * types)[1]
    block = piece * Y_SIZE
    half = (block * X_SIZE, LANES)
    lr_half = (2 * width, rows // CORES)
    rel_send, rel_keep, lr_send, lr_keep = call(
        grad_kernel,
        [where, edge_counts],
        [left, right, relation, sources, relation_ids, destinations, negatives_left[0], negatives_right[0]],
        [half, half, lr_half, lr_half],
        [(CORES * half[0], LANES)],
    )
    rel_got = to_core(rel_send)
    lr_got = to_core(lr_send)

    blocks = []
    for r in range(X_SIZE):
        blocks.append(rel_keep[r * block:(r + 1) * block] + rel_got[r * block:(r + 1) * block])
    mine = scatter(blocks, to_x)
    pieces = []
    for r in range(Y_SIZE):
        pieces.append(mine[r * piece:(r + 1) * piece])
    mine = scatter(pieces, to_y)

    lr_sum = lr_keep + lr_got
    lr_other = to_y(lr_sum, 2)
    packed = (width + 8, rows // CORES)
    new_left, new_right = call(
        adagrad_kernel,
        [where],
        [lr_sum, lr_other, left, right, left_state[None], right_state[None]],
        [packed, packed],
    )
    new_right = to_bucket_before(new_right)
    left_next, left_state_next, right_next, right_state_next = call(
        join_kernel,
        [where],
        [new_left, to_core(new_left), new_right, to_core(new_right)],
        [(width, rows), (1, rows), (width, rows), (1, rows)],
    )

    for bit in (1, 2, 4):
        mine = mine + to_z(mine, bit)
    mine = gather(mine, Y_SIZE, to_y)
    mine = gather(mine, X_SIZE, to_x)
    relation_grad, = call(relation_kernel, [where], [mine, to_core(mine)], [(width, types)], [(CORES * half[0], LANES)])
    return left_next.T, left_state_next[0], right_next.T, right_state_next[0], relation_grad.T


def solution(mesh):
    in_specs = (
        P("dom", None),
        P("dom"),
        P("dom", None),
        P("dom"),
        P(),
        P("dom", "rep"),
        P("dom", "rep"),
        P("dom", "rep"),
        P("dom", "rep", None),
        P("dom", "rep", None),
        P("dom"),
    )
    out_specs = (P("dom", None), P("dom"), P("dom", None), P("dom"), P())
    return jax.shard_map(body, mesh=mesh, in_specs=in_specs, out_specs=out_specs, check_vma=False)
```

time: 458 us -> 128 us (0.28); the launches traced: 452 us -> 128 us
  waiting for transfers between devices: 305 us -> 58.3 us
  other arithmetic: 46.6 us -> 3.07 us
  local copies, waits for them, and re-layouts: 45.3 us -> 2.59 us
  starting transfers between devices: 6.43 us -> 44.1 us
  matrix products: 31.9 us -> 0 us
  Pallas kernels: 0 us -> 18.3 us
  between operations: 15.5 us -> 1.46 us
    psum x2 -> x0, waiting for transfers between devices: 300 us -> none  [the longest x1 250 us: body(): relation_grad = lax.psum(batch_relation, ('dom', 'rep'))]
    ppermute x2 -> x22, waiting for transfers between devices: 5.19 us -> 58.3 us  [the longest x21 56.2 us: send(): return lax.ppermute(value, ('dom', 'rep'), pairs)]
    ppermute x2 -> x22, starting transfers between devices: 6.35 us -> 44.1 us  [the longest x21 39.8 us: send(): return lax.ppermute(value, ('dom', 'rep'), pairs)]
    dot_general x6 -> x0, matrix products: 31.9 us -> none  [the longest x3 16.2 us: batch_loss(): lax.dot_general(probes, left_rows[negatives_left], contract, precision=HI...]
    scatter-add x5 -> x0, other arithmetic: 31.6 us -> none  [the longest x1 8.2 us: batch_loss(): left_rows[negatives_left]]
    pallas_call x0 -> x4, Pallas kernels: none -> 18.3 us  [call(): pl.pallas_call(kernel, out_shape=[jax.ShapeDtypeStruct(shape, F32) for sh...]
    gather x6 -> x0, local copies, waits for them, and re-layouts: 18 us -> none  [the longest x1 5.07 us: batch_loss(): right_rows[negatives_right]]
    cond x51 -> x0, local copies, waits for them, and re-layouts: 13.3 us -> none  [the longest x3 7.29 us: body(): lax.cond(jnp.sum(edge_mask) > 0, run_batch, skip_batch, 0)]
  transfers between devices with their start and end apart: 4 -> 22, of which waited for: 3 -> 20; matrix products, arithmetic and copies ran while one was open for 2% -> 0% of each run, Pallas kernels for 0% -> 3%
where the time goes in v1:
time: 128 us
  waiting for transfers between devices  58.3 us (46%)
  starting transfers between devices  44.1 us (34%)
  Pallas kernels  18.3 us (14%)
  other arithmetic  3.07 us (2%)
  local copies, waits for them, and re-layouts  2.59 us (2%)
  between operations  1.46 us (1%)
    ppermute x21, waiting for transfers between devices, send(): return lax.ppermute(value, ('dom', 'rep'), pairs)  56.2 us
    ppermute x21, starting transfers between devices, send(): return lax.ppermute(value, ('dom', 'rep'), pairs)  39.8 us
    pallas_call x4, Pallas kernels, call(): pl.pallas_call(kernel, out_shape=[jax.ShapeDtypeStruct(shape, F32) for sh...  18.3 us
    ppermute x1, starting transfers between devices, to_bucket_before(): return lax.ppermute(value, ('dom', 'rep'), pairs)  4.37 us
  transfers between devices with their start and end apart: 22, of which 20 were waited for; matrix products, arithmetic and copies ran while one was open for 0% of the time, Pallas kernels for 3%

profile of v1, /device:TPU:1, one launch (start us, length us, event | category | flops | bytes accessed | tf_op | source)
XLA Modules:
  0.0 127.8 jit_solution(6277435828814709322)
XLA Ops:
  2.0 10.2 %shard_map.146 = (f32[2432,128]{1,0:T(8,128)}, f32[2432,128]{1,0:T(8,128)}, f32[800,128]{1,0:T(8,128)}, f32[800,128]{1,0:T(8,128)}) custom-call(s32[4]{0:T(128)} %pad_add_fusion.place_ref, s32[1]{0:T(128)S(6)} %copy.22.counts_ref, f32[400,256]{1,0:T(8,128)} %bitcast.18, f32[400,256]{1,0:T(8,128)} %bitcast.20, f32[400,1536]{1,0:T(8,128)} %bitcast.17, ...), custom_call_target="tpu_custom_call" | custom-call | tf_op jit(solution)/shard_map/pallas_call | solution.py:184
  12.2 3.2 %collective-permute-start.5 = (f32[2432,128]{1,0:T(8,128)}, f32[2432,128]{1,0:T(8,128)S(1)}, u32[]{:S(2)}, u32[]{:S(2)}) collective-permute-start(f32[2432,128]{1,0:T(8,128)} %get-tuple-element.24), channel_id=1, source_target_pairs={{0,1},{1,0},{2,3},{3,2},{4,5},{5,4},{6,7},{7,6},{8,9},{9,8},{10,11... | collective-permute-start | bytes 3735560 | tf_op jit(solution)/shard_map/ppermute | solution.py:69
  15.5 2.8 %collective-permute-done.5 = f32[2432,128]{1,0:T(8,128)S(1)} collective-permute-done((f32[2432,128]{1,0:T(8,128)}, f32[2432,128]{1,0:T(8,128)S(1)}, u32[]{:S(2)}, u32[]{:S(2)}) %collective-permute-start.5) | collective-permute-done | bytes 1245216 | tf_op jit(solution)/shard_map/ppermute | solution.py:69
  19.6 1.9 %collective-permute-start.7 = (f32[608,128]{1,0:T(8,128)S(1)}, f32[608,128]{1,0:T(8,128)S(1)}, u32[]{:S(2)}, u32[]{:S(2)}) collective-permute-start(f32[608,128]{1,0:T(8,128)S(1)} %get-tuple-element.29), channel_id=1, source_target_pairs={{0,128},{1,129},{2,130},{3,131},{4,132},{5,133},{6,134},{7,135},{8... | collective-permute-start | bytes 933896 | tf_op jit(solution)/shard_map/ppermute | solution.py:69
  22.6 7.5 %collective-permute-done.6 = f32[608,128]{1,0:T(8,128)S(1)} collective-permute-done((f32[608,128]{1,0:T(8,128)S(1)}, f32[608,128]{1,0:T(8,128)S(1)}, u32[]{:S(2)}, u32[]{:S(2)}) %collective-permute-start.6) | collective-permute-done | bytes 311328 | tf_op jit(solution)/shard_map/ppermute | solution.py:69
  30.1 5.2 %collective-permute-done.7 = f32[608,128]{1,0:T(8,128)S(1)} collective-permute-done((f32[608,128]{1,0:T(8,128)S(1)}, f32[608,128]{1,0:T(8,128)S(1)}, u32[]{:S(2)}, u32[]{:S(2)}) %collective-permute-start.7) | collective-permute-done | bytes 311328 | tf_op jit(solution)/shard_map/ppermute | solution.py:69
  37.4 2.0 %collective-permute-start.10 = (f32[152,128]{1,0:T(8,128)S(1)}, f32[152,128]{1,0:T(8,128)S(1)}, u32[]{:S(2)}, u32[]{:S(2)}) collective-permute-start(f32[152,128]{1,0:T(8,128)S(1)} %get-tuple-element.32), channel_id=1, source_target_pairs={{0,2},{1,3},{2,0},{3,1},{4,6},{5,7},{6,4},{7,5},{8,10},{9,11},{10,... | collective-permute-start | bytes 233480 | tf_op jit(solution)/shard_map/ppermute | solution.py:69
  42.9 2.3 %collective-permute-done.9 = f32[152,128]{1,0:T(8,128)S(1)} collective-permute-done((f32[152,128]{1,0:T(8,128)S(1)}, f32[152,128]{1,0:T(8,128)S(1)}, u32[]{:S(2)}, u32[]{:S(2)}) %collective-permute-start.9) | collective-permute-done | bytes 77856 | tf_op jit(solution)/shard_map/ppermute | solution.py:69
  46.3 2.2 %collective-permute-done.12 = f32[152,128]{1,0:T(8,128)S(1)} collective-permute-done((f32[152,128]{1,0:T(8,128)S(1)}, f32[152,128]{1,0:T(8,128)S(1)}, u32[]{:S(2)}, u32[]{:S(2)}) %collective-permute-start.12) | collective-permute-done | bytes 77856 | tf_op jit(solution)/shard_map/ppermute | solution.py:69
  48.6 2.6 %collective-permute-start.13 = (f32[152,128]{1,0:T(8,128)S(1)}, f32[152,128]{1,0:T(8,128)S(1)}, u32[]{:S(2)}, u32[]{:S(2)}) collective-permute-start(f32[152,128]{1,0:T(8,128)S(1)} %add.69), channel_id=1, source_target_pairs={{0,8},{1,9},{2,10},{3,11},{4,12},{5,13},{6,14},{7,15},{8,0},{9,1},... | collective-permute-start | bytes 233480 | tf_op jit(solution)/shard_map/ppermute | solution.py:69
  53.0 6.8 %collective-permute-start.14 = (f32[152,128]{1,0:T(8,128)S(1)}, f32[152,128]{1,0:T(8,128)S(1)}, u32[]{:S(2)}, u32[]{:S(2)}) collective-permute-start(f32[152,128]{1,0:T(8,128)S(1)} %add.70), channel_id=1, source_target_pairs={{0,16},{1,17},{2,18},{3,19},{4,20},{5,21},{6,22},{7,23},{8,24},{9,... | collective-permute-start | bytes 233480 | tf_op jit(solution)/shard_map/ppermute | solution.py:69
  65.0 3.1 %collective-permute-done.16 = f32[152,128]{1,0:T(8,128)S(1)} collective-permute-done((f32[152,128]{1,0:T(8,128)S(1)}, f32[152,128]{1,0:T(8,128)S(1)}, u32[]{:S(2)}, u32[]{:S(2)}) %collective-permute-start.16) | collective-permute-done | bytes 77856 | tf_op jit(solution)/shard_map/ppermute | solution.py:69
  69.3 2.8 %collective-permute-start.18 = (f32[608,128]{1,0:T(8,128)S(1)}, f32[608,128]{1,0:T(8,128)S(1)}, u32[]{:S(2)}, u32[]{:S(2)}) collective-permute-start(f32[608,128]{1,0:T(8,128)S(1)} %pad_maximum_fusion), channel_id=1, source_target_pairs={{0,192},{1,193},{2,194},{3,195},{4,196},{5,197},{6,198},{7,199},{8... | collective-permute-start | bytes 933896 | tf_op jit(solution)/shard_map/ppermute | solution.py:69
  72.8 6.5 %collective-permute-done.18 = f32[608,128]{1,0:T(8,128)S(1)} collective-permute-done((f32[608,128]{1,0:T(8,128)S(1)}, f32[608,128]{1,0:T(8,128)S(1)}, u32[]{:S(2)}, u32[]{:S(2)}) %collective-permute-start.18) | collective-permute-done | bytes 311328 | tf_op jit(solution)/shard_map/ppermute | solution.py:69
  79.5 3.0 %collective-permute-done.20 = f32[608,128]{1,0:T(8,128)S(1)} collective-permute-done((f32[608,128]{1,0:T(8,128)S(1)}, f32[608,128]{1,0:T(8,128)S(1)}, u32[]{:S(2)}, u32[]{:S(2)}) %collective-permute-start.20) | collective-permute-done | bytes 311328 | tf_op jit(solution)/shard_map/ppermute | solution.py:69
  82.5 8.1 %collective-permute-start.21 = (f32[2432,128]{1,0:T(8,128)S(1)}, f32[2432,128]{1,0:T(8,128)S(1)}, u32[]{:S(2)}, u32[]{:S(2)}) collective-permute-start(f32[2432,128]{1,0:T(8,128)S(1)} %constant_dynamic-update-slice_fusion.own_ref), channel_id=1, source_target_pairs={{0,1},{1,0},{2,3},{3,2},{4,5},{5,4},{6,7},{7,6},{8,9},{9,8},{10,11... | collective-permute-start | bytes 3735560 | tf_op jit(solution)/shard_map/ppermute | solution.py:69
  90.7 3.0 %collective-permute-done = f32[800,128]{1,0:T(8,128)S(1)} collective-permute-done((f32[800,128]{1,0:T(8,128)S(1)}, f32[800,128]{1,0:T(8,128)S(1)}, u32[]{:S(2)}, u32[]{:S(2)}) %collective-permute-start) | collective-permute-done | bytes 409632 | tf_op jit(solution)/shard_map/ppermute | solution.py:69
  94.8 11.3 %collective-permute-done.1.got_ref = f32[800,128]{1,0:T(8,128)S(1)} collective-permute-done((f32[800,128]{1,0:T(8,128)S(1)}, f32[800,128]{1,0:T(8,128)S(1)}, u32[]{:S(2)}, u32[]{:S(2)}) %collective-permute-start.1) | collective-permute-done | bytes 409632 | tf_op jit(solution)/shard_map/ppermute | solution.py:69
  106.8 2.2 %shard_map.147 = (f32[408,128]{1,0:T(8,128)}, f32[408,128]{1,0:T(8,128)}) custom-call(s32[4]{0:T(128)} %pad_add_fusion.place_ref, f32[800,128]{1,0:T(8,128)} %copy-done, f32[800,128]{1,0:T(8,128)} %copy-done.4, f32[400,256]{1,0:T(8,128)} %bitcast.19, f32[400,256]{1,0:T(8,128)} %bitcast.21, f32[1,256]{1,0:T(1,128)} %bitcast.24, f32[1,256]{1,0:T(1,128)} %bitcast.25), custom_call_target="tpu_custom_call" | custom-call | tf_op jit(solution)/shard_map/pallas_call | solution.py:184
  109.1 4.4 %collective-permute-start.3 = (f32[408,128]{1,0:T(8,128)}, f32[408,128]{1,0:T(8,128)S(1)}, u32[]{:S(2)}, u32[]{:S(2)}) collective-permute-start(f32[408,128]{1,0:T(8,128)} %get-tuple-element.18), channel_id=1, source_target_pairs={{0,252},{1,253},{2,254},{3,255},{4,0},{5,1},{6,2},{7,3},{8,4},{9,5... | collective-permute-start | bytes 626696 | tf_op jit(solution)/shard_map/ppermute | solution.py:92
  114.9 2.1 %collective-permute-done.3.own_right_ref = f32[408,128]{1,0:T(8,128)S(1)} collective-permute-done((f32[408,128]{1,0:T(8,128)}, f32[408,128]{1,0:T(8,128)S(1)}, u32[]{:S(2)}, u32[]{:S(2)}) %collective-permute-start.3) | collective-permute-done | bytes 208928 | tf_op jit(solution)/shard_map/ppermute | solution.py:92
  117.0 2.1 %collective-permute-start.4 = (f32[408,128]{1,0:T(8,128)S(1)}, f32[408,128]{1,0:T(8,128)S(1)}, u32[]{:S(2)}, u32[]{:S(2)}) collective-permute-start(f32[408,128]{1,0:T(8,128)S(1)} %collective-permute-done.3.own_right_ref), channel_id=1, source_target_pairs={{0,1},{1,0},{2,3},{3,2},{4,5},{5,4},{6,7},{7,6},{8,9},{9,8},{10,11... | collective-permute-start | bytes 626696 | tf_op jit(solution)/shard_map/ppermute | solution.py:69
  120.9 2.2 %shard_map.148 = (f32[400,256]{1,0:T(8,128)}, f32[1,256]{1,0:T(1,128)}, f32[400,256]{1,0:T(8,128)}, f32[1,256]{1,0:T(1,128)}) custom-call(s32[4]{0:T(128)} %pad_add_fusion.place_ref, f32[408,128]{1,0:T(8,128)} %get-tuple-element.17.own_left_ref, f32[408,128]{1,0:T(8,128)} %copy-done.6, f32[408,128]{1,0:T(8,128)} %copy-done.5, f32[408,128]{1,0:T(8,128)} %copy-done.7), custom_call_target="tpu_custom_call" | custom-call | tf_op jit(solution)/shard_map/pallas_call | solution.py:184
  124.2 3.6 %shard_map.149 = f32[400,1536]{1,0:T(8,128)} custom-call(s32[4]{0:T(128)} %pad_add_fusion.place_ref, f32[2432,128]{1,0:T(8,128)} %copy-done.1, f32[2432,128]{1,0:T(8,128)} %copy-done.2), custom_call_target="tpu_custom_call" | custom-call | tf_op jit(solution)/shard_map/pallas_call | solution.py:184
  (58 shorter events, 25.1 us)
Async XLA Ops:
  12.2 6.0 %collective-permute-start.5 = (f32[2432,128]{1,0:T(8,128)}, f32[2432,128]{1,0:T(8,128)S(1)}, u32[]{:S(2)}, u32[]{:S(2)}) collective-permute-start(f32[2432,128]{1,0:T(8,128)} %get-tuple-element.24), channel_id=1, source_target_pairs={{0,1},{1,0},{2,3},{3,2},{4,5},{5,4},{6,7},{7,6},{8,9},{9,8},{10,11... | collective-permute-start | bytes 3735560 | tf_op jit(solution)/shard_map/ppermute | solution.py:69
  19.5 10.6 %collective-permute-start.6 = (f32[608,128]{1,0:T(8,128)S(1)}, f32[608,128]{1,0:T(8,128)S(1)}, u32[]{:S(2)}, u32[]{:S(2)}) collective-permute-start(f32[608,128]{1,0:T(8,128)S(1)} %get-tuple-element.27), channel_id=1, source_target_pairs={{0,64},{1,65},{2,66},{3,67},{4,68},{5,69},{6,70},{7,71},{8,72},{9,... | collective-permute-start | bytes 933896 | tf_op jit(solution)/shard_map/ppermute | solution.py:69
  19.6 15.7 %collective-permute-start.7 = (f32[608,128]{1,0:T(8,128)S(1)}, f32[608,128]{1,0:T(8,128)S(1)}, u32[]{:S(2)}, u32[]{:S(2)}) collective-permute-start(f32[608,128]{1,0:T(8,128)S(1)} %get-tuple-element.29), channel_id=1, source_target_pairs={{0,128},{1,129},{2,130},{3,131},{4,132},{5,133},{6,134},{7,135},{8... | collective-permute-start | bytes 933896 | tf_op jit(solution)/shard_map/ppermute | solution.py:69
  21.5 14.8 %collective-permute-start.8 = (f32[608,128]{1,0:T(8,128)S(1)}, f32[608,128]{1,0:T(8,128)S(1)}, u32[]{:S(2)}, u32[]{:S(2)}) collective-permute-start(f32[608,128]{1,0:T(8,128)S(1)} %get-tuple-element.28), channel_id=1, source_target_pairs={{0,192},{1,193},{2,194},{3,195},{4,196},{5,197},{6,198},{7,199},{8... | collective-permute-start | bytes 933896 | tf_op jit(solution)/shard_map/ppermute | solution.py:69
  37.4 4.8 %collective-permute-start.10 = (f32[152,128]{1,0:T(8,128)S(1)}, f32[152,128]{1,0:T(8,128)S(1)}, u32[]{:S(2)}, u32[]{:S(2)}) collective-permute-start(f32[152,128]{1,0:T(8,128)S(1)} %get-tuple-element.32), channel_id=1, source_target_pairs={{0,2},{1,3},{2,0},{3,1},{4,6},{5,7},{6,4},{7,5},{8,10},{9,11},{10,... | collective-permute-start | bytes 233480 | tf_op jit(solution)/shard_map/ppermute | solution.py:69
  39.3 3.5 %collective-permute-start.11 = (f32[152,128]{1,0:T(8,128)S(1)}, f32[152,128]{1,0:T(8,128)S(1)}, u32[]{:S(2)}, u32[]{:S(2)}) collective-permute-start(f32[152,128]{1,0:T(8,128)S(1)} %get-tuple-element.31), channel_id=1, source_target_pairs={{0,34},{1,35},{2,32},{3,33},{4,38},{5,39},{6,36},{7,37},{8,42},{9,... | collective-permute-start | bytes 233480 | tf_op jit(solution)/shard_map/ppermute | solution.py:69
  40.1 5.1 %collective-permute-start.9 = (f32[152,128]{1,0:T(8,128)S(1)}, f32[152,128]{1,0:T(8,128)S(1)}, u32[]{:S(2)}, u32[]{:S(2)}) collective-permute-start(f32[152,128]{1,0:T(8,128)S(1)} %get-tuple-element.30), channel_id=1, source_target_pairs={{0,32},{1,33},{2,34},{3,35},{4,36},{5,37},{6,38},{7,39},{8,40},{9,... | collective-permute-start | bytes 233480 | tf_op jit(solution)/shard_map/ppermute | solution.py:69
  45.2 3.3 %collective-permute-start.12 = (f32[152,128]{1,0:T(8,128)S(1)}, f32[152,128]{1,0:T(8,128)S(1)}, u32[]{:S(2)}, u32[]{:S(2)}) collective-permute-start(f32[152,128]{1,0:T(8,128)S(1)} %fusion.4), channel_id=1, source_target_pairs={{0,4},{1,5},{2,6},{3,7},{4,0},{5,1},{6,2},{7,3},{8,12},{9,13},{10,... | collective-permute-start | bytes 233480 | tf_op jit(solution)/shard_map/ppermute | solution.py:69
  48.6 4.4 %collective-permute-start.13 = (f32[152,128]{1,0:T(8,128)S(1)}, f32[152,128]{1,0:T(8,128)S(1)}, u32[]{:S(2)}, u32[]{:S(2)}) collective-permute-start(f32[152,128]{1,0:T(8,128)S(1)} %add.69), channel_id=1, source_target_pairs={{0,8},{1,9},{2,10},{3,11},{4,12},{5,13},{6,14},{7,15},{8,0},{9,1},... | collective-permute-start | bytes 233480 | tf_op jit(solution)/shard_map/ppermute | solution.py:69
  53.0 8.7 %collective-permute-start.14 = (f32[152,128]{1,0:T(8,128)S(1)}, f32[152,128]{1,0:T(8,128)S(1)}, u32[]{:S(2)}, u32[]{:S(2)}) collective-permute-start(f32[152,128]{1,0:T(8,128)S(1)} %add.70), channel_id=1, source_target_pairs={{0,16},{1,17},{2,18},{3,19},{4,20},{5,21},{6,22},{7,23},{8,24},{9,... | collective-permute-start | bytes 233480 | tf_op jit(solution)/shard_map/ppermute | solution.py:69
  61.7 3.3 %collective-permute-start.15 = (f32[152,128]{1,0:T(8,128)S(1)}, f32[152,128]{1,0:T(8,128)S(1)}, u32[]{:S(2)}, u32[]{:S(2)}) collective-permute-start(f32[152,128]{1,0:T(8,128)S(1)} %get-tuple-element.26), channel_id=1, source_target_pairs={{0,34},{1,35},{2,32},{3,33},{4,38},{5,39},{6,36},{7,37},{8,42},{9,... | collective-permute-start | bytes 233480 | tf_op jit(solution)/shard_map/ppermute | solution.py:69
  63.3 4.8 %collective-permute-start.16 = (f32[152,128]{1,0:T(8,128)S(1)}, f32[152,128]{1,0:T(8,128)S(1)}, u32[]{:S(2)}, u32[]{:S(2)}) collective-permute-start(f32[152,128]{1,0:T(8,128)S(1)} %get-tuple-element.26), channel_id=1, source_target_pairs={{0,2},{1,3},{2,0},{3,1},{4,6},{5,7},{6,4},{7,5},{8,10},{9,11},{10,... | collective-permute-start | bytes 233480 | tf_op jit(solution)/shard_map/ppermute | solution.py:69
  64.7 4.5 %collective-permute-start.17 = (f32[152,128]{1,0:T(8,128)S(1)}, f32[152,128]{1,0:T(8,128)S(1)}, u32[]{:S(2)}, u32[]{:S(2)}) collective-permute-start(f32[152,128]{1,0:T(8,128)S(1)} %get-tuple-element.26), channel_id=1, source_target_pairs={{0,32},{1,33},{2,34},{3,35},{4,36},{5,37},{6,38},{7,39},{8,40},{9,... | collective-permute-start | bytes 233480 | tf_op jit(solution)/shard_map/ppermute | solution.py:69
  69.2 24.5 %copy-start.3 = (f32[800,128]{1,0:T(8,128)S(1)}, f32[800,128]{1,0:T(8,128)}, u32[]{:S(2)}) copy-start(f32[800,128]{1,0:T(8,128)} %get-tuple-element.15) | copy-start | bytes 1228804
  69.3 10.0 %collective-permute-start.18 = (f32[608,128]{1,0:T(8,128)S(1)}, f32[608,128]{1,0:T(8,128)S(1)}, u32[]{:S(2)}, u32[]{:S(2)}) collective-permute-start(f32[608,128]{1,0:T(8,128)S(1)} %pad_maximum_fusion), channel_id=1, source_target_pairs={{0,192},{1,193},{2,194},{3,195},{4,196},{5,197},{6,198},{7,199},{8... | collective-permute-start | bytes 933896 | tf_op jit(solution)/shard_map/ppermute | solution.py:69
  72.1 7.4 %collective-permute-start.19 = (f32[608,128]{1,0:T(8,128)S(1)}, f32[608,128]{1,0:T(8,128)S(1)}, u32[]{:S(2)}, u32[]{:S(2)}) collective-permute-start(f32[608,128]{1,0:T(8,128)S(1)} %pad_maximum_fusion), channel_id=1, source_target_pairs={{0,128},{1,129},{2,130},{3,131},{4,132},{5,133},{6,134},{7,135},{8... | collective-permute-start | bytes 933896 | tf_op jit(solution)/shard_map/ppermute | solution.py:69
  72.2 10.3 %collective-permute-start.20 = (f32[608,128]{1,0:T(8,128)S(1)}, f32[608,128]{1,0:T(8,128)S(1)}, u32[]{:S(2)}, u32[]{:S(2)}) collective-permute-start(f32[608,128]{1,0:T(8,128)S(1)} %pad_maximum_fusion), channel_id=1, source_target_pairs={{0,64},{1,65},{2,66},{3,67},{4,68},{5,69},{6,70},{7,71},{8,72},{9,... | collective-permute-start | bytes 933896 | tf_op jit(solution)/shard_map/ppermute | solution.py:69
  82.5 40.6 %copy-start.1 = (f32[2432,128]{1,0:T(8,128)}, f32[2432,128]{1,0:T(8,128)S(1)}, u32[]{:S(2)}) copy-start(f32[2432,128]{1,0:T(8,128)S(1)} %constant_dynamic-update-slice_fusion.own_ref) | copy-start | bytes 3735556
  82.5 40.6 %collective-permute-start.21 = (f32[2432,128]{1,0:T(8,128)S(1)}, f32[2432,128]{1,0:T(8,128)S(1)}, u32[]{:S(2)}, u32[]{:S(2)}) collective-permute-start(f32[2432,128]{1,0:T(8,128)S(1)} %constant_dynamic-update-slice_fusion.own_ref), channel_id=1, source_target_pairs={{0,1},{1,0},{2,3},{3,2},{4,5},{5,4},{6,7},{7,6},{8,9},{9,8},{10,11... | collective-permute-start | bytes 3735560 | tf_op jit(solution)/shard_map/ppermute | solution.py:69
  90.6 3.2 %collective-permute-start = (f32[800,128]{1,0:T(8,128)S(1)}, f32[800,128]{1,0:T(8,128)S(1)}, u32[]{:S(2)}, u32[]{:S(2)}) collective-permute-start(f32[800,128]{1,0:T(8,128)S(1)} %copy-done.8), channel_id=1, source_target_pairs={{0,1},{1,0},{2,3},{3,2},{4,5},{5,4},{6,7},{7,6},{8,9},{9,8},{10,11... | collective-permute-start | bytes 1228808 | tf_op jit(solution)/shard_map/ppermute | solution.py:69
  93.8 12.3 %collective-permute-start.1 = (f32[800,128]{1,0:T(8,128)S(1)}, f32[800,128]{1,0:T(8,128)S(1)}, u32[]{:S(2)}, u32[]{:S(2)}) collective-permute-start(f32[800,128]{1,0:T(8,128)S(1)} %add.58.kept_ref), channel_id=1, source_target_pairs={{0,2},{1,3},{2,0},{3,1},{4,6},{5,7},{6,4},{7,5},{8,10},{9,11},{10,... | collective-permute-start | bytes 1228808 | tf_op jit(solution)/shard_map/ppermute | solution.py:69
  109.1 7.9 %collective-permute-start.3 = (f32[408,128]{1,0:T(8,128)}, f32[408,128]{1,0:T(8,128)S(1)}, u32[]{:S(2)}, u32[]{:S(2)}) collective-permute-start(f32[408,128]{1,0:T(8,128)} %get-tuple-element.18), channel_id=1, source_target_pairs={{0,252},{1,253},{2,254},{3,255},{4,0},{5,1},{6,2},{7,3},{8,4},{9,5... | collective-permute-start | bytes 626696 | tf_op jit(solution)/shard_map/ppermute | solution.py:92
  113.5 5.7 %collective-permute-start.2 = (f32[408,128]{1,0:T(8,128)}, f32[408,128]{1,0:T(8,128)S(1)}, u32[]{:S(2)}, u32[]{:S(2)}) collective-permute-start(f32[408,128]{1,0:T(8,128)} %get-tuple-element.17.own_left_ref), channel_id=1, source_target_pairs={{0,1},{1,0},{2,3},{3,2},{4,5},{5,4},{6,7},{7,6},{8,9},{9,8},{10,11... | collective-permute-start | bytes 626696 | tf_op jit(solution)/shard_map/ppermute | solution.py:69
  117.0 3.2 %collective-permute-start.4 = (f32[408,128]{1,0:T(8,128)S(1)}, f32[408,128]{1,0:T(8,128)S(1)}, u32[]{:S(2)}, u32[]{:S(2)}) collective-permute-start(f32[408,128]{1,0:T(8,128)S(1)} %collective-permute-done.3.own_right_ref), channel_id=1, source_target_pairs={{0,1},{1,0},{2,3},{3,2},{4,5},{5,4},{6,7},{7,6},{8,9},{9,8},{10,11... | collective-permute-start | bytes 626696 | tf_op jit(solution)/shard_map/ppermute | solution.py:69
  (7 other events, 40.4 us)

commit v2 on v1

v2 whole, which is shorter than its diff:
```python
import functools

import jax
import jax.numpy as jnp
from jax import lax
from jax.sharding import PartitionSpec as P
from jax.experimental import pallas as pl
from jax.experimental.pallas import tpu as pltpu

MARGIN = 0.1
LEARN_RATE = 0.1
F32 = jnp.float32
BF16 = jnp.bfloat16
NN = (((1,), (0,)), ((), ()))
NT = (((1,), (1,)), ((), ()))


def parts(value):
    high = value.astype(BF16)
    return high, (value - high.astype(F32)).astype(BF16)


def dot(a, b, dims):
    return lax.dot_general(a, b, dims, preferred_element_type=F32)


def dot_picked(value, picks, dims):
    rows = value.shape[0]
    both = dot(jnp.concatenate(parts(value), axis=0), picks, dims)
    return both[:rows] + both[rows:]


def dot_split(a, b, dims):
    rows = a[0].shape[0]
    both = dot(jnp.concatenate(a, axis=0), b[0], dims)
    return both[:rows] + (dot(a[0], b[1], dims) + both[rows:])


def product(v, w):
    return v[0] * w[0] - v[1] * w[1], v[0] * w[1] + v[1] * w[0]


def adjoint(v, w):
    return v[0] * w[0] + v[1] * w[1], v[1] * w[0] - v[0] * w[1]


def halves(x):
    half = x.shape[0] // 2
    return x[:half], x[half:]


def one_hot(ids, rows):
    return (lax.broadcasted_iota(jnp.int32, (rows, ids.shape[1]), 0) == ids).astype(F32)


CORES, X_SIZE, Y_SIZE, Z_SIZE = 2, 4, 4, 8
DEVICES = CORES * X_SIZE * Y_SIZE * Z_SIZE
LANES = 128
VMEM_LIMIT = 32 * 1024 * 1024


def place(dom, rep):
    return rep % 2, dom // 16, (rep // 2) * 2 + (dom // 8) % 2, dom % 8


def here():
    return place(lax.axis_index("dom"), lax.axis_index("rep"))


def device(core, x, y, z):
    return ((x * 2 + y % 2) * 8 + z) * 4 + (y // 2) * 2 + core


def send(value, target):
    pairs = []
    for n in range(DEVICES):
        pairs.append((n, device(*target(*place(n // 4, n % 4)))))
    return lax.ppermute(value, ("dom", "rep"), pairs)


def to_core(value):
    return send(value, lambda core, x, y, z: (1 - core, x, y, z))


def to_first(value, step):
    return send(
        value,
        lambda core, x, y, z: (core, x, (y + step) % Y_SIZE, z) if core else (core, (x + step) % X_SIZE, y, z),
    )


def to_second(value, step):
    return send(
        value,
        lambda core, x, y, z: (core, (x + step) % X_SIZE, y, z) if core else (core, x, (y + step) % Y_SIZE, z),
    )


def to_y(value, step):
    return send(value, lambda core, x, y, z: (core, x, (y + step) % Y_SIZE, z))


def to_z(value, target):
    return send(value, lambda core, x, y, z: (core, x, y, target(z) % Z_SIZE))


def to_bucket_before(value):
    pairs = []
    for n in range(DEVICES):
        pairs.append((n, (n - 4) % DEVICES))
    return lax.ppermute(value, ("dom", "rep"), pairs)


def piece_rows(total):
    block = total // LANES // (CORES * X_SIZE)
    piece = -(-block // (8 * Y_SIZE)) * 8
    return block, piece


def block_spans(width, types, parity):
    block, piece = piece_rows(width * types)
    found = []
    for k, start, size, row in spans(width, types):
        if row // (piece * Y_SIZE) == parity:
            found.append((k, start, size, row))
    return found


def spans(width, types):
    block, piece = piece_rows(width * types)
    pad = piece * Y_SIZE - block
    found = []
    for k in range(types // LANES):
        row, end = k * width, (k + 1) * width
        while row < end:
            stop = min(end, (row // block + 1) * block)
            found.append((k, row - k * width, stop - row, row + (row // block) * pad))
            row = stop
    return found


def piece_at(half, x, y, r, s, piece):
    first, second = jnp.where(half == 0, x, y), jnp.where(half == 0, y, x)
    block = half * X_SIZE + (first + r) % X_SIZE
    return pl.multiple_of((block * Y_SIZE + (second + s) % Y_SIZE) * piece, 8)


def grad_kernel(counts_ref, left_ref, right_ref, rel_ref, src_ref, rid_ref, dst_ref, negl_ref, negr_ref, *refs):
    send_refs, keep_refs = refs[:X_SIZE], refs[X_SIZE:2 * X_SIZE]
    q_ref, p_ref, gr_ref, gl_ref, ds_ref, dt_ref, rows_ref, near_left_ref, near_right_ref, near_rel_ref, sems = refs[2 * X_SIZE:]
    core, x, y, _ = here()
    fetches = []
    for n, pair in enumerate(((left_ref, near_left_ref), (right_ref, near_right_ref), (rel_ref, near_rel_ref))):
        fetches.append(pltpu.make_async_copy(*pair, sems.at[n]))
    for fetch in fetches:
        fetch.start()
    slots = src_ref.shape[1]
    rows = left_ref.shape[1]
    types = rel_ref.shape[1]
    negatives = negl_ref.shape[1]
    count_right = jnp.sum(one_hot(negr_ref[...], rows), axis=1, keepdims=True)
    count_left = jnp.sum(one_hot(negl_ref[...], rows), axis=1, keepdims=True)
    pick_src = one_hot(src_ref[...], rows).astype(BF16)
    pick_dst = one_hot(dst_ref[...], rows).astype(BF16)
    pick_rel = one_hot(rid_ref[...], types).astype(BF16)
    fetches[0].wait()
    left = near_left_ref[...]
    source = dot_picked(left, pick_src, NN)
    left_parts, left_rows = parts(left), parts(left.T)
    fetches[1].wait()
    right = near_right_ref[...]
    target = dot_picked(right, pick_dst, NN)
    right_parts, right_rows = parts(right), parts(right.T)
    fetches[2].wait()
    weight = dot_picked(near_rel_ref[...], pick_rel, NN)
    s, t, w = halves(source), halves(target), halves(weight)
    q = jnp.concatenate(product(s, w), axis=0)
    p = jnp.concatenate(adjoint(t, w), axis=0)
    positive = jnp.sum(q * target, axis=0, keepdims=True)
    q_parts, p_parts = parts(q), parts(p)
    slot = lax.broadcasted_iota(jnp.int32, (1, slots), 1)
    live = (slot + lax.axis_index("rep") * slots < counts_ref[0]).astype(F32) * (1.0 / negatives)
    offset = MARGIN - positive
    g_right = jax.nn.sigmoid(offset + dot_split(right_rows, q_parts, NN)) * count_right * live
    g_left = jax.nn.sigmoid(offset + dot_split(left_rows, p_parts, NN)) * count_left * live
    d_pos = -(jnp.sum(g_right, axis=0, keepdims=True) + jnp.sum(g_left, axis=0, keepdims=True))
    gr_parts, gl_parts = parts(g_right), parts(g_left)
    d_q = dot_split(right_parts, gr_parts, NN) + d_pos * target
    d_p = dot_split(left_parts, gl_parts, NN)
    dq, dp = halves(d_q), halves(d_p)
    a, b = adjoint(dq, s), adjoint(dp, t)
    d_w = jnp.concatenate([a[0] + b[0], a[1] - b[1]], axis=0)
    d_relation = dot_picked(d_w, pick_rel, NT)
    width = d_relation.shape[0]
    block, piece = piece_rows(width * types)
    pad = piece * Y_SIZE - block
    if pad:
        for k in range(CORES * X_SIZE):
            rows_ref[(k + 1) * (block + pad) - pad:(k + 1) * (block + pad), :] = jnp.zeros((pad, LANES), F32)
    for k, start, size, row in spans(width, types):
        rows_ref[row:row + size, :] = d_relation[start:start + size, k * LANES:(k + 1) * LANES]
    for out_refs, half in ((send_refs, 1 - core), (keep_refs, core)):
        for r in range(X_SIZE):
            for s in range(Y_SIZE):
                out_refs[r][s * piece:(s + 1) * piece, :] = rows_ref[pl.ds(piece_at(half, x, y, r, s, piece), piece), :]
    q_ref[...], p_ref[...] = q, p
    gr_ref[...], gl_ref[...] = g_right, g_left
    ds_ref[...] = jnp.concatenate(adjoint(dq, w), axis=0)
    dt_ref[...] = jnp.concatenate(product(dp, w), axis=0) + d_pos * q


def rows_kernel(src_ref, dst_ref, q_ref, p_ref, gr_ref, gl_ref, ds_ref, dt_ref, send_ref, keep_ref):
    width = q_ref.shape[0]
    rows = gr_ref.shape[0]
    half = rows // CORES
    first = here()[0] == 0
    for at, ids_ref, edge_ref, score_ref, picked_ref in (
        (0, src_ref, p_ref, gl_ref, ds_ref),
        (width, dst_ref, q_ref, gr_ref, dt_ref),
    ):
        picks = one_hot(ids_ref[...], rows).astype(BF16)
        grad = dot_split(parts(edge_ref[...]), parts(score_ref[...]), NT) + dot_picked(picked_ref[...], picks, NT)
        low, high = grad[:, :half], grad[:, half:]
        keep_ref[at:at + width, :] = jnp.where(first, low, high)
        send_ref[at:at + width, :] = jnp.where(first, high, low)


WHOLE = pl.BlockSpec(memory_space=pltpu.VMEM)


def near(value):
    return pltpu.with_memory_space_constraint(value, pltpu.VMEM)


def far(value):
    return pltpu.with_memory_space_constraint(value, pltpu.HBM)


def call(kernel, specs, arrays, shapes, scratch=(), own=True):
    return pl.pallas_call(
        kernel,
        out_shape=[pltpu.VMEM(shape, F32) if own else jax.ShapeDtypeStruct(shape, F32) for shape in shapes],
        in_specs=list(specs) + [WHOLE] * (len(arrays) - len(specs)),
        out_specs=[WHOLE] * len(shapes),
        scratch_shapes=list(scratch),
        compiler_params=pltpu.CompilerParams(vmem_limit_bytes=VMEM_LIMIT),
    )(*arrays)


def adagrad_kernel(kept_ref, got_ref, left_ref, right_ref, left_state_ref, right_state_ref, new_left_ref, new_right_ref):
    width = left_ref.shape[0]
    first = here()[0] == 0
    for at, rows_ref, state_ref, out_ref in (
        (0, left_ref, left_state_ref, new_left_ref),
        (width, right_ref, right_state_ref, new_right_ref),
    ):
        half = rows_ref.shape[1] // CORES
        gradient = kept_ref[at:at + width, :] + got_ref[at:at + width, :]
        embedding = jnp.where(first, rows_ref[:, :half], rows_ref[:, half:])
        state = jnp.where(first, state_ref[:, :half], state_ref[:, half:])
        new_state = state + jnp.sum(gradient * gradient, axis=0, keepdims=True) * (1.0 / width)
        out_ref[:width, :] = embedding - gradient * (LEARN_RATE / jnp.sqrt(new_state))
        out_ref[width:, :] = jnp.broadcast_to(new_state, (8, half))


def join_kernel(own_left_ref, other_left_ref, own_right_ref, other_right_ref, left_ref, left_state_ref, right_ref, right_state_ref):
    first = here()[0] == 0
    width = left_ref.shape[0]
    half = own_left_ref.shape[1]
    for own_ref, other_ref, rows_ref, state_ref in (
        (own_left_ref, other_left_ref, left_ref, left_state_ref),
        (own_right_ref, other_right_ref, right_ref, right_state_ref),
    ):
        own, other = own_ref[...], other_ref[...]
        for at, value in ((0, jnp.where(first, own, other)), (half, jnp.where(first, other, own))):
            rows_ref[:, at:at + half] = value[:width]
            state_ref[:, at:at + half] = value[width:width + 1]


def relation_kernel(steps, *refs):
    count = 2 * len(steps)
    in_refs, (out_ref, rows_ref, sems) = refs[-3 - count:-3], refs[-3:]
    core, x, y, _ = here()
    width, types = out_ref.shape
    block, piece = piece_rows(width * types)
    lanes_each = block * LANES // width
    for n, in_ref in enumerate(in_refs):
        half = core if n % 2 == 0 else 1 - core
        second = jnp.where(half == 0, y, x)
        for s in range(Y_SIZE):
            to = pl.multiple_of((second + s) % Y_SIZE * piece, 8)
            rows_ref[n, pl.ds(to, piece), :] = in_ref[s * piece:(s + 1) * piece, :]
    for begin in (True, False):
        for n in range(count):
            half = core if n % 2 == 0 else 1 - core
            first = (jnp.where(half == 0, x, y) + steps[n // 2]) % X_SIZE
            for low in range(2):

                @pl.when(first % 2 == low)
                def _():
                    at = 0
                    for i, (k, start, size, _) in enumerate(block_spans(width, types, low)):
                        lane = (half * X_SIZE + first - low) * lanes_each + k * LANES
                        copy = pltpu.make_async_copy(
                            rows_ref.at[n, pl.ds(at, size), :],
                            out_ref.at[pl.ds(start, size), pl.ds(pl.multiple_of(lane, LANES), LANES)],
                            sems.at[n, i],
                        )
                        if begin:
                            copy.start()
                        else:
                            copy.wait()
                        at += size


def put_relation(steps, blocks, sofar, width, types):
    piece = piece_rows(width * types)[1]
    anywhere = pl.BlockSpec(memory_space=pl.ANY)
    before = [] if sofar is None else [sofar]
    count = len(blocks)
    return pl.pallas_call(
        functools.partial(relation_kernel, steps),
        out_shape=jax.ShapeDtypeStruct((width, types), F32),
        in_specs=[anywhere] * len(before) + [WHOLE] * count,
        out_specs=anywhere,
        scratch_shapes=[pltpu.VMEM((count, piece * Y_SIZE, LANES), F32), pltpu.SemaphoreType.DMA((count, 2))],
        input_output_aliases={0: 0} if before else {},
        compiler_params=pltpu.CompilerParams(vmem_limit_bytes=VMEM_LIMIT),
    )(*before, *[near(value) for value in blocks])


def scatter(pieces, move):
    return sum([move(pieces[r], r) for r in (2, 1, 3)], pieces[0])


def gather(own, count, move):
    got = {r: move(own, (count - r) % count) for r in (2, 3, 1)}
    return [own] + [got[r] for r in range(1, count)]


def after(value, *others):
    return lax.optimization_barrier((value, *others))


def body(left_embedding, left_state, right_embedding, right_state, relation, sources, relation_ids, destinations, negatives_left, negatives_right, edge_counts):
    left, right, relation = left_embedding.T, right_embedding.T, relation.T
    width, types = relation.shape
    rows = left.shape[1]
    edges = sources.shape[1]
    piece = piece_rows(width * types)[1]
    block = (piece * Y_SIZE, LANES)
    scalar = pl.BlockSpec(memory_space=pltpu.SMEM)
    found = call(
        grad_kernel,
        [scalar] + [pl.BlockSpec(memory_space=pl.ANY)] * 3,
        [edge_counts] + [far(value) for value in (left, right, relation, sources, relation_ids, destinations, negatives_left[0], negatives_right[0])],
        [block] * (2 * X_SIZE) + [(width, edges)] * 2 + [(rows, edges)] * 2 + [(width, edges)] * 2,
        [pltpu.VMEM((CORES * X_SIZE * block[0], LANES), F32), pltpu.VMEM(left.shape, F32), pltpu.VMEM(right.shape, F32), pltpu.VMEM(relation.shape, F32), pltpu.SemaphoreType.DMA((3,))],
    )
    rel_send, rel_keep, saved = found[:X_SIZE], found[X_SIZE:2 * X_SIZE], found[2 * X_SIZE:]

    blocks = {}
    for r in (2, 1, 3, 0):
        blocks[r] = rel_keep[r] + to_core(rel_send[r])
    blocks[3], *saved = after(blocks[3], *saved)
    mine = scatter([blocks[r] for r in range(X_SIZE)], to_first)

    lr_half = (2 * width, rows // CORES)
    lr_send, lr_keep = call(rows_kernel, [], [far(sources), far(destinations)] + [near(value) for value in saved], [lr_half, lr_half])
    lr_sum = lr_keep + to_core(lr_send)

    pieces = []
    for r in range(Y_SIZE):
        pieces.append(mine[r * piece:(r + 1) * piece])
    mine = scatter(pieces, to_second)

    mine = mine + to_z(mine, lambda z: z ^ 1)
    mine, lr_sum = after(mine, lr_sum)
    lr_other = to_y(lr_sum, 2)
    opposite = to_z(mine, lambda z: z ^ 5)
    opposite, lr_sum, lr_other = after(opposite, lr_sum, lr_other)
    packed = (width + 8, rows // CORES)
    new_left, new_right = call(
        adagrad_kernel,
        [],
        [near(lr_sum), near(lr_other)] + [far(value) for value in (left, right, left_state[None], right_state[None])],
        [packed, packed],
    )
    new_right = to_bucket_before(new_right)
    other_left = to_core(new_left)
    mine = (mine + opposite) + (to_z(mine, lambda z: z + 2) + to_z(mine, lambda z: z - 2))

    mine = jnp.concatenate(gather(mine, Y_SIZE, to_second), axis=0)
    mine, new_left, other_left, new_right = after(mine, new_left, other_left, new_right)
    own = gather(mine, X_SIZE, to_first)
    own[2], new_right = after(own[2], new_right)
    left_next, left_state_next, right_next, right_state_next = call(
        join_kernel,
        [],
        [near(value) for value in (new_left, other_left, new_right, to_core(new_right))],
        [(width, rows), (1, rows), (width, rows), (1, rows)],
        own=False,
    )
    relation_grad = put_relation((0, 2), [own[0], to_core(own[0]), own[2], to_core(own[2])], None, width, types)
    last = own[1]
    last, relation_grad, left_next, left_state_next, right_next, right_state_next = after(
        last, relation_grad, left_next, left_state_next, right_next, right_state_next
    )
    relation_grad = put_relation((3,), [own[3], to_core(own[3])], relation_grad, width, types)
    relation_grad = put_relation((1,), [last, to_core(last)], relation_grad, width, types)
    return left_next.T, left_state_next[0], right_next.T, right_state_next[0], relation_grad.T


def solution(mesh):
    in_specs = (
        P("dom", None),
        P("dom"),
        P("dom", None),
        P("dom"),
        P(),
        P("dom", "rep"),
        P("dom", "rep"),
        P("dom", "rep"),
        P("dom", "rep", None),
        P("dom", "rep", None),
        P("dom"),
    )
    out_specs = (P("dom", None), P("dom"), P("dom", None), P("dom"), P())
    return jax.shard_map(body, mesh=mesh, in_specs=in_specs, out_specs=out_specs, check_vma=False)
```

time: 128 us -> 84 us (0.66)
  waiting for transfers between devices: 58.3 us -> 18.2 us
  starting transfers between devices: 44.1 us -> 48.4 us
  Pallas kernels: 18.3 us -> 15.3 us
  other arithmetic: 3.07 us -> 0.29 us
  local copies, waits for them, and re-layouts: 2.59 us -> 0.02 us
    ppermute x21 -> x28, waiting for transfers between devices: 56.2 us -> 18.2 us  [send(): return lax.ppermute(value, ('dom', 'rep'), pairs)]
    ppermute x21 -> x28, starting transfers between devices: 39.8 us -> 45.1 us  [send(): return lax.ppermute(value, ('dom', 'rep'), pairs)]
    pallas_call x4 -> x7, Pallas kernels: 18.3 us -> 15.3 us  [the longest x4 12.1 us: call(): pl.pallas_call(kernel, out_shape=[pltpu.VMEM(shape, F32) if own else jax....]
    unnamed x23 -> x0, local copies, waits for them, and re-layouts: 2.55 us -> none
    add x6 -> x8, other arithmetic: 2.38 us -> 0.27 us  [the longest x3 0.1 us: body(): blocks[r] = rel_keep[r] + to_core(rel_send[r])]
    ppermute x1, waiting for transfers between devices: 2.09 us -> 0.01 us  [to_bucket_before(): return lax.ppermute(value, ('dom', 'rep'), pairs)]
  transfers between devices with their start and end apart: 22 -> 29, of which waited for: 20 -> 14; matrix products, arithmetic and copies ran while one was open for 0% -> 0% of each run, Pallas kernels for 3% -> 8%
where the time goes in v2:
time: 84 us; the launch traced here: 83.8 us
  starting transfers between devices  48.4 us (58%)
  waiting for transfers between devices  18.2 us (22%)
  Pallas kernels  15.3 us (18%)
  between operations  1.56 us (2%)
    ppermute x28, starting transfers between devices, send(): return lax.ppermute(value, ('dom', 'rep'), pairs)  45.1 us
    ppermute x28, waiting for transfers between devices, send(): return lax.ppermute(value, ('dom', 'rep'), pairs)  18.2 us
    pallas_call x4, Pallas kernels, call(): pl.pallas_call(kernel, out_shape=[pltpu.VMEM(shape, F32) if own else jax....  12.1 us
    ppermute x1, starting transfers between devices, to_bucket_before(): return lax.ppermute(value, ('dom', 'rep'), pairs)  3.3 us
    pallas_call x3, Pallas kernels, put_relation(): pl.pallas_call(functools.partial(relation_kernel, steps), out_shape=jax.S...  3.19 us
  transfers between devices with their start and end apart: 29, of which 14 were waited for; matrix products, arithmetic and copies ran while one was open for 0% of the time, Pallas kernels for 8%

profile of v2, /device:TPU:1, one launch (start us, length us, event | category | flops | bytes accessed | tf_op | source)
XLA Modules:
  0.0 83.8 jit_solution(17574396472371405875)
XLA Ops:
  1.3 7.9 %shard_map.146 = (f32[608,128]{1,0:T(8,128)S(1)}, f32[608,128]{1,0:T(8,128)S(1)}, f32[608,128]{1,0:T(8,128)S(1)}, f32[608,128]{1,0:T(8,128)S(1)}, f32[608,128]{1...) custom-call(s32[1]{0:T(128)S(6)} %copy.20.counts_ref, ...), custom_call_target="tpu_custom_call" | custom-call | tf_op jit(solution)/shard_map/pallas_call | solution.py:240
  9.2 3.3 %collective-permute-start.1 = (f32[608,128]{1,0:T(8,128)S(1)}, f32[608,128]{1,0:T(8,128)S(1)}, u32[]{:S(2)}, u32[]{:S(2)}) collective-permute-start(f32[608,128]{1,0:T(8,128)S(1)} %get-tuple-element.54), channel_id=1, source_target_pairs={{0,1},{1,0},{2,3},{3,2},{4,5},{5,4},{6,7},{7,6},{8,9},{9,8},{10,11... | collective-permute-start | bytes 933896 | tf_op jit(solution)/shard_map/ppermute | solution.py:78
  15.6 2.4 %collective-permute-start.6 = (f32[608,128]{1,0:T(8,128)S(1)}, f32[608,128]{1,0:T(8,128)S(1)}, u32[]{:S(2)}, u32[]{:S(2)}) collective-permute-start(f32[608,128]{1,0:T(8,128)S(1)} %add.50), channel_id=1, source_target_pairs={{0,192},{1,35},{2,194},{3,33},{4,196},{5,39},{6,198},{7,37},{8,200... | collective-permute-start | bytes 933896 | tf_op jit(solution)/shard_map/ppermute | solution.py:78
  18.0 2.0 %shard_map.147 = (f32[800,128]{1,0:T(8,128)S(1)}, f32[800,128]{1,0:T(8,128)S(1)}) custom-call(s32[1,512]{1,0:T(1,128)} %src_ref.3, s32[1,512]{1,0:T(1,128)} %dst_ref.3, f32[400,512]{1,0:T(8,128)S(1)} %get-tuple-element.66.q_ref, f32[400,512]{1,0:T(8,128)S(1)} %get-tuple-element.67.p_ref, f32[256,512]{1,0:T(8,128)S(1)} %get-tuple-element.68.gr_ref, ...), custom_call_target="tpu_custom_call" | custom-call | tf_op jit(solution)/shard_map/pallas_call | solution.py:240
  20.0 1.3 %collective-permute-start.11 = (f32[800,128]{1,0:T(8,128)S(1)}, f32[800,128]{1,0:T(8,128)S(1)}, u32[]{:S(2)}, u32[]{:S(2)}) collective-permute-start(f32[800,128]{1,0:T(8,128)S(1)} %get-tuple-element.73), channel_id=1, source_target_pairs={{0,1},{1,0},{2,3},{3,2},{4,5},{5,4},{6,7},{7,6},{8,9},{9,8},{10,11... | collective-permute-start | bytes 1228808 | tf_op jit(solution)/shard_map/ppermute | solution.py:78
  21.5 3.3 %collective-permute-done.4 = f32[608,128]{1,0:T(8,128)S(1)} collective-permute-done((f32[608,128]{1,0:T(8,128)S(1)}, f32[608,128]{1,0:T(8,128)S(1)}, u32[]{:S(2)}, u32[]{:S(2)}) %collective-permute-start.4) | collective-permute-done | bytes 311328 | tf_op jit(solution)/shard_map/ppermute | solution.py:78
  24.9 1.4 %collective-permute-start.7 = (f32[152,128]{1,0:T(8,128)S(1)}, f32[152,128]{1,0:T(8,128)S(1)}, u32[]{:S(2)}, u32[]{:S(2)}) collective-permute-start(f32[152,128]{1,0:T(8,128)S(1)} %get-tuple-element.97), channel_id=1, source_target_pairs={{0,2},{1,129},{2,0},{3,131},{4,6},{5,133},{6,4},{7,135},{8,10},{9,... | collective-permute-start | bytes 233480 | tf_op jit(solution)/shard_map/ppermute | solution.py:78
  27.8 1.9 %collective-permute-done.7 = f32[152,128]{1,0:T(8,128)S(1)} collective-permute-done((f32[152,128]{1,0:T(8,128)S(1)}, f32[152,128]{1,0:T(8,128)S(1)}, u32[]{:S(2)}, u32[]{:S(2)}) %collective-permute-start.7) | collective-permute-done | bytes 77856 | tf_op jit(solution)/shard_map/ppermute | solution.py:78
  29.7 2.0 %collective-permute-done.8 = f32[152,128]{1,0:T(8,128)S(1)} collective-permute-done((f32[152,128]{1,0:T(8,128)S(1)}, f32[152,128]{1,0:T(8,128)S(1)}, u32[]{:S(2)}, u32[]{:S(2)}) %collective-permute-start.8) | collective-permute-done | bytes 77856 | tf_op jit(solution)/shard_map/ppermute | solution.py:78
  31.7 1.6 %collective-permute-start.10 = (f32[152,128]{1,0:T(8,128)S(1)}, f32[152,128]{1,0:T(8,128)S(1)}, u32[]{:S(2)}, u32[]{:S(2)}) collective-permute-start(f32[152,128]{1,0:T(8,128)S(1)} %fusion.1), channel_id=1, source_target_pairs={{0,4},{1,5},{2,6},{3,7},{4,0},{5,1},{6,2},{7,3},{8,12},{9,13},{10,... | collective-permute-start | bytes 233480 | tf_op jit(solution)/shard_map/ppermute | solution.py:78
  33.4 1.7 %collective-permute-done.10 = f32[152,128]{1,0:T(8,128)S(1)} collective-permute-done((f32[152,128]{1,0:T(8,128)S(1)}, f32[152,128]{1,0:T(8,128)S(1)}, u32[]{:S(2)}, u32[]{:S(2)}) %collective-permute-start.10) | collective-permute-done | bytes 77856 | tf_op jit(solution)/shard_map/ppermute | solution.py:78
  35.2 2.0 %collective-permute-start.13 = (f32[800,128]{1,0:T(8,128)S(1)}, f32[800,128]{1,0:T(8,128)S(1)}, u32[]{:S(2)}, u32[]{:S(2)}) collective-permute-start(f32[800,128]{1,0:T(8,128)S(1)} %add.56.kept_ref), channel_id=1, source_target_pairs={{0,2},{1,3},{2,0},{3,1},{4,6},{5,7},{6,4},{7,5},{8,10},{9,11},{10,... | collective-permute-start | bytes 1228808 | tf_op jit(solution)/shard_map/ppermute | solution.py:78
  37.2 6.3 %collective-permute-start.12 = (f32[152,128]{1,0:T(8,128)S(1)}, f32[152,128]{1,0:T(8,128)S(1)}, u32[]{:S(2)}, u32[]{:S(2)}) collective-permute-start(f32[152,128]{1,0:T(8,128)S(1)} %add.55), channel_id=1, source_target_pairs={{0,20},{1,21},{2,22},{3,23},{4,16},{5,17},{6,18},{7,19},{8,28},{9,... | collective-permute-start | bytes 233480 | tf_op jit(solution)/shard_map/ppermute | solution.py:78
  43.8 2.1 %collective-permute-start.14 = (f32[152,128]{1,0:T(8,128)S(1)}, f32[152,128]{1,0:T(8,128)S(1)}, u32[]{:S(2)}, u32[]{:S(2)}) collective-permute-start(f32[152,128]{1,0:T(8,128)S(1)} %add.55), channel_id=1, source_target_pairs={{0,8},{1,9},{2,10},{3,11},{4,12},{5,13},{6,14},{7,15},{8,16},{9,17... | collective-permute-start | bytes 233480 | tf_op jit(solution)/shard_map/ppermute | solution.py:78
  46.4 1.3 %shard_map.148 = (f32[408,128]{1,0:T(8,128)S(1)}, f32[408,128]{1,0:T(8,128)S(1)}) custom-call(f32[800,128]{1,0:T(8,128)S(1)} %add.56.kept_ref, f32[800,128]{1,0:T(8,128)S(1)} %collective-permute-done.13.got_ref, f32[400,256]{1,0:T(8,128)} %bitcast.15, f32[400,256]{1,0:T(8,128)} %bitcast.17, f32[1,256]{1,0:T(1,128)} %bitcast.20, f32[1,256]{1,0:T(1,128)} %bitcast.21), custom_call_target="tpu_custom_call" | custom-call | tf_op jit(solution)/shard_map/pallas_call | solution.py:240
  47.7 3.3 %collective-permute-start.20 = (f32[408,128]{1,0:T(8,128)S(1)}, f32[408,128]{1,0:T(8,128)S(1)}, u32[]{:S(2)}, u32[]{:S(2)}) collective-permute-start(f32[408,128]{1,0:T(8,128)S(1)} %get-tuple-element.80), channel_id=1, source_target_pairs={{0,252},{1,253},{2,254},{3,255},{4,0},{5,1},{6,2},{7,3},{8,4},{9,5... | collective-permute-start | bytes 626696 | tf_op jit(solution)/shard_map/ppermute | solution.py:111
  51.0 6.1 %collective-permute-start.19 = (f32[408,128]{1,0:T(8,128)S(1)}, f32[408,128]{1,0:T(8,128)S(1)}, u32[]{:S(2)}, u32[]{:S(2)}) collective-permute-start(f32[408,128]{1,0:T(8,128)S(1)} %get-tuple-element.84.own_left_ref), channel_id=1, source_target_pairs={{0,1},{1,0},{2,3},{3,2},{4,5},{5,4},{6,7},{7,6},{8,9},{9,8},{10,11... | collective-permute-start | bytes 626696 | tf_op jit(solution)/shard_map/ppermute | solution.py:78
  58.3 2.0 %collective-permute-start.16 = (f32[152,128]{1,0:T(8,128)S(1)}, f32[152,128]{1,0:T(8,128)S(1)}, u32[]{:S(2)}, u32[]{:S(2)}) collective-permute-start(f32[152,128]{1,0:T(8,128)S(1)} %add_add_fusion.1), channel_id=1, source_target_pairs={{0,34},{1,193},{2,32},{3,195},{4,38},{5,197},{6,36},{7,199},{8,42}... | collective-permute-start | bytes 233480 | tf_op jit(solution)/shard_map/ppermute | solution.py:78
  60.3 1.6 %collective-permute-done.18 = f32[152,128]{1,0:T(8,128)S(1)} collective-permute-done((f32[152,128]{1,0:T(8,128)S(1)}, f32[152,128]{1,0:T(8,128)S(1)}, u32[]{:S(2)}, u32[]{:S(2)}) %collective-permute-start.18) | collective-permute-done | bytes 77856 | tf_op jit(solution)/shard_map/ppermute | solution.py:78
  63.4 3.2 %collective-permute-start.23 = (f32[608,128]{1,0:T(8,128)S(1)}, f32[608,128]{1,0:T(8,128)S(1)}, u32[]{:S(2)}, u32[]{:S(2)}) collective-permute-start(f32[608,128]{1,0:T(8,128)S(1)} %pad_maximum_fusion.refs_0_), channel_id=1, source_target_pairs={{0,128},{1,3},{2,130},{3,1},{4,132},{5,7},{6,134},{7,5},{8,136},{9... | collective-permute-start | bytes 933896 | tf_op jit(solution)/shard_map/ppermute | solution.py:78
  66.7 1.4 %collective-permute-start.22 = (f32[608,128]{1,0:T(8,128)S(1)}, f32[608,128]{1,0:T(8,128)S(1)}, u32[]{:S(2)}, u32[]{:S(2)}) collective-permute-start(f32[608,128]{1,0:T(8,128)S(1)} %pad_maximum_fusion.refs_0_), channel_id=1, source_target_pairs={{0,1},{1,0},{2,3},{3,2},{4,5},{5,4},{6,7},{7,6},{8,9},{9,8},{10,11... | collective-permute-start | bytes 933896 | tf_op jit(solution)/shard_map/ppermute | solution.py:78
  68.1 3.2 %collective-permute-done.23.refs_2_ = f32[608,128]{1,0:T(8,128)S(1)} collective-permute-done((f32[608,128]{1,0:T(8,128)S(1)}, f32[608,128]{1,0:T(8,128)S(1)}, u32[]{:S(2)}, u32[]{:S(2)}) %collective-permute-start.23) | collective-permute-done | bytes 311328 | tf_op jit(solution)/shard_map/ppermute | solution.py:78
  71.2 2.7 %collective-permute-start.24 = (f32[608,128]{1,0:T(8,128)S(1)}, f32[608,128]{1,0:T(8,128)S(1)}, u32[]{:S(2)}, u32[]{:S(2)}) collective-permute-start(f32[608,128]{1,0:T(8,128)S(1)} %collective-permute-done.23.refs_2_), channel_id=1, source_target_pairs={{0,1},{1,0},{2,3},{3,2},{4,5},{5,4},{6,7},{7,6},{8,9},{9,8},{10,11... | collective-permute-start | bytes 933896 | tf_op jit(solution)/shard_map/ppermute | solution.py:78
  73.9 3.3 %collective-permute-start.21 = (f32[608,128]{1,0:T(8,128)S(1)}, f32[608,128]{1,0:T(8,128)S(1)}, u32[]{:S(2)}, u32[]{:S(2)}) collective-permute-start(f32[608,128]{1,0:T(8,128)S(1)} %pad_maximum_fusion.refs_0_), channel_id=1, source_target_pairs={{0,192},{1,35},{2,194},{3,33},{4,196},{5,39},{6,198},{7,37},{8,200... | collective-permute-start | bytes 933896 | tf_op jit(solution)/shard_map/ppermute | solution.py:78
  (51 shorter events, 14.8 us)
Async XLA Ops:
  9.2 4.6 %collective-permute-start.1 = (f32[608,128]{1,0:T(8,128)S(1)}, f32[608,128]{1,0:T(8,128)S(1)}, u32[]{:S(2)}, u32[]{:S(2)}) collective-permute-start(f32[608,128]{1,0:T(8,128)S(1)} %get-tuple-element.54), channel_id=1, source_target_pairs={{0,1},{1,0},{2,3},{3,2},{4,5},{5,4},{6,7},{7,6},{8,9},{9,8},{10,11... | collective-permute-start | bytes 933896 | tf_op jit(solution)/shard_map/ppermute | solution.py:78
  13.1 8.2 %collective-permute-start = (f32[608,128]{1,0:T(8,128)S(1)}, f32[608,128]{1,0:T(8,128)S(1)}, u32[]{:S(2)}, u32[]{:S(2)}) collective-permute-start(f32[608,128]{1,0:T(8,128)S(1)} %get-tuple-element.52), channel_id=1, source_target_pairs={{0,1},{1,0},{2,3},{3,2},{4,5},{5,4},{6,7},{7,6},{8,9},{9,8},{10,11... | collective-permute-start | bytes 933896 | tf_op jit(solution)/shard_map/ppermute | solution.py:78
  13.8 7.7 %collective-permute-start.2 = (f32[608,128]{1,0:T(8,128)S(1)}, f32[608,128]{1,0:T(8,128)S(1)}, u32[]{:S(2)}, u32[]{:S(2)}) collective-permute-start(f32[608,128]{1,0:T(8,128)S(1)} %add.46), channel_id=1, source_target_pairs={{0,128},{1,3},{2,130},{3,1},{4,132},{5,7},{6,134},{7,5},{8,136},{9... | collective-permute-start | bytes 933896 | tf_op jit(solution)/shard_map/ppermute | solution.py:78
  15.1 9.7 %collective-permute-start.4 = (f32[608,128]{1,0:T(8,128)S(1)}, f32[608,128]{1,0:T(8,128)S(1)}, u32[]{:S(2)}, u32[]{:S(2)}) collective-permute-start(f32[608,128]{1,0:T(8,128)S(1)} %add.48), channel_id=1, source_target_pairs={{0,64},{1,33},{2,66},{3,35},{4,68},{5,37},{6,70},{7,39},{8,72},{9,... | collective-permute-start | bytes 933896 | tf_op jit(solution)/shard_map/ppermute | solution.py:78
  15.6 9.1 %collective-permute-start.6 = (f32[608,128]{1,0:T(8,128)S(1)}, f32[608,128]{1,0:T(8,128)S(1)}, u32[]{:S(2)}, u32[]{:S(2)}) collective-permute-start(f32[608,128]{1,0:T(8,128)S(1)} %add.50), channel_id=1, source_target_pairs={{0,192},{1,35},{2,194},{3,33},{4,196},{5,39},{6,198},{7,37},{8,200... | collective-permute-start | bytes 933896 | tf_op jit(solution)/shard_map/ppermute | solution.py:78
  20.0 13.4 %collective-permute-start.11 = (f32[800,128]{1,0:T(8,128)S(1)}, f32[800,128]{1,0:T(8,128)S(1)}, u32[]{:S(2)}, u32[]{:S(2)}) collective-permute-start(f32[800,128]{1,0:T(8,128)S(1)} %get-tuple-element.73), channel_id=1, source_target_pairs={{0,1},{1,0},{2,3},{3,2},{4,5},{5,4},{6,7},{7,6},{8,9},{9,8},{10,11... | collective-permute-start | bytes 1228808 | tf_op jit(solution)/shard_map/ppermute | solution.py:78
  24.9 4.8 %collective-permute-start.7 = (f32[152,128]{1,0:T(8,128)S(1)}, f32[152,128]{1,0:T(8,128)S(1)}, u32[]{:S(2)}, u32[]{:S(2)}) collective-permute-start(f32[152,128]{1,0:T(8,128)S(1)} %get-tuple-element.97), channel_id=1, source_target_pairs={{0,2},{1,129},{2,0},{3,131},{4,6},{5,133},{6,4},{7,135},{8,10},{9,... | collective-permute-start | bytes 233480 | tf_op jit(solution)/shard_map/ppermute | solution.py:78
  27.2 4.5 %collective-permute-start.8 = (f32[152,128]{1,0:T(8,128)S(1)}, f32[152,128]{1,0:T(8,128)S(1)}, u32[]{:S(2)}, u32[]{:S(2)}) collective-permute-start(f32[152,128]{1,0:T(8,128)S(1)} %get-tuple-element.99), channel_id=1, source_target_pairs={{0,32},{1,65},{2,34},{3,67},{4,36},{5,69},{6,38},{7,71},{8,40},{9,... | collective-permute-start | bytes 233480 | tf_op jit(solution)/shard_map/ppermute | solution.py:78
  31.7 3.4 %collective-permute-start.10 = (f32[152,128]{1,0:T(8,128)S(1)}, f32[152,128]{1,0:T(8,128)S(1)}, u32[]{:S(2)}, u32[]{:S(2)}) collective-permute-start(f32[152,128]{1,0:T(8,128)S(1)} %fusion.1), channel_id=1, source_target_pairs={{0,4},{1,5},{2,6},{3,7},{4,0},{5,1},{6,2},{7,3},{8,12},{9,13},{10,... | collective-permute-start | bytes 233480 | tf_op jit(solution)/shard_map/ppermute | solution.py:78
  35.2 11.2 %collective-permute-start.13 = (f32[800,128]{1,0:T(8,128)S(1)}, f32[800,128]{1,0:T(8,128)S(1)}, u32[]{:S(2)}, u32[]{:S(2)}) collective-permute-start(f32[800,128]{1,0:T(8,128)S(1)} %add.56.kept_ref), channel_id=1, source_target_pairs={{0,2},{1,3},{2,0},{3,1},{4,6},{5,7},{6,4},{7,5},{8,10},{9,11},{10,... | collective-permute-start | bytes 1228808 | tf_op jit(solution)/shard_map/ppermute | solution.py:78
  37.2 9.2 %collective-permute-start.12 = (f32[152,128]{1,0:T(8,128)S(1)}, f32[152,128]{1,0:T(8,128)S(1)}, u32[]{:S(2)}, u32[]{:S(2)}) collective-permute-start(f32[152,128]{1,0:T(8,128)S(1)} %add.55), channel_id=1, source_target_pairs={{0,20},{1,21},{2,22},{3,23},{4,16},{5,17},{6,18},{7,19},{8,28},{9,... | collective-permute-start | bytes 233480 | tf_op jit(solution)/shard_map/ppermute | solution.py:78
  43.5 13.6 %collective-permute-start.15 = (f32[152,128]{1,0:T(8,128)S(1)}, f32[152,128]{1,0:T(8,128)S(1)}, u32[]{:S(2)}, u32[]{:S(2)}) collective-permute-start(f32[152,128]{1,0:T(8,128)S(1)} %add.55), channel_id=1, source_target_pairs={{0,24},{1,25},{2,26},{3,27},{4,28},{5,29},{6,30},{7,31},{8,0},{9,1... | collective-permute-start | bytes 233480 | tf_op jit(solution)/shard_map/ppermute | solution.py:78
  43.8 13.4 %collective-permute-start.14 = (f32[152,128]{1,0:T(8,128)S(1)}, f32[152,128]{1,0:T(8,128)S(1)}, u32[]{:S(2)}, u32[]{:S(2)}) collective-permute-start(f32[152,128]{1,0:T(8,128)S(1)} %add.55), channel_id=1, source_target_pairs={{0,8},{1,9},{2,10},{3,11},{4,12},{5,13},{6,14},{7,15},{8,16},{9,17... | collective-permute-start | bytes 233480 | tf_op jit(solution)/shard_map/ppermute | solution.py:78
  47.7 15.7 %collective-permute-start.20 = (f32[408,128]{1,0:T(8,128)S(1)}, f32[408,128]{1,0:T(8,128)S(1)}, u32[]{:S(2)}, u32[]{:S(2)}) collective-permute-start(f32[408,128]{1,0:T(8,128)S(1)} %get-tuple-element.80), channel_id=1, source_target_pairs={{0,252},{1,253},{2,254},{3,255},{4,0},{5,1},{6,2},{7,3},{8,4},{9,5... | collective-permute-start | bytes 626696 | tf_op jit(solution)/shard_map/ppermute | solution.py:111
  51.0 12.4 %collective-permute-start.19 = (f32[408,128]{1,0:T(8,128)S(1)}, f32[408,128]{1,0:T(8,128)S(1)}, u32[]{:S(2)}, u32[]{:S(2)}) collective-permute-start(f32[408,128]{1,0:T(8,128)S(1)} %get-tuple-element.84.own_left_ref), channel_id=1, source_target_pairs={{0,1},{1,0},{2,3},{3,2},{4,5},{5,4},{6,7},{7,6},{8,9},{9,8},{10,11... | collective-permute-start | bytes 626696 | tf_op jit(solution)/shard_map/ppermute | solution.py:78
  57.1 4.8 %collective-permute-start.18 = (f32[152,128]{1,0:T(8,128)S(1)}, f32[152,128]{1,0:T(8,128)S(1)}, u32[]{:S(2)}, u32[]{:S(2)}) collective-permute-start(f32[152,128]{1,0:T(8,128)S(1)} %add_add_fusion.1), channel_id=1, source_target_pairs={{0,32},{1,65},{2,34},{3,67},{4,36},{5,69},{6,38},{7,71},{8,40},{9,... | collective-permute-start | bytes 233480 | tf_op jit(solution)/shard_map/ppermute | solution.py:78
  57.8 5.0 %collective-permute-start.17 = (f32[152,128]{1,0:T(8,128)S(1)}, f32[152,128]{1,0:T(8,128)S(1)}, u32[]{:S(2)}, u32[]{:S(2)}) collective-permute-start(f32[152,128]{1,0:T(8,128)S(1)} %add_add_fusion.1), channel_id=1, source_target_pairs={{0,2},{1,129},{2,0},{3,131},{4,6},{5,133},{6,4},{7,135},{8,10},{9,... | collective-permute-start | bytes 233480 | tf_op jit(solution)/shard_map/ppermute | solution.py:78
  58.3 5.1 %collective-permute-start.16 = (f32[152,128]{1,0:T(8,128)S(1)}, f32[152,128]{1,0:T(8,128)S(1)}, u32[]{:S(2)}, u32[]{:S(2)}) collective-permute-start(f32[152,128]{1,0:T(8,128)S(1)} %add_add_fusion.1), channel_id=1, source_target_pairs={{0,34},{1,193},{2,32},{3,195},{4,38},{5,197},{6,36},{7,199},{8,42}... | collective-permute-start | bytes 233480 | tf_op jit(solution)/shard_map/ppermute | solution.py:78
  63.4 7.8 %collective-permute-start.23 = (f32[608,128]{1,0:T(8,128)S(1)}, f32[608,128]{1,0:T(8,128)S(1)}, u32[]{:S(2)}, u32[]{:S(2)}) collective-permute-start(f32[608,128]{1,0:T(8,128)S(1)} %pad_maximum_fusion.refs_0_), channel_id=1, source_target_pairs={{0,128},{1,3},{2,130},{3,1},{4,132},{5,7},{6,134},{7,5},{8,136},{9... | collective-permute-start | bytes 933896 | tf_op jit(solution)/shard_map/ppermute | solution.py:78
  66.6 10.6 %collective-permute-start.26 = (f32[608,128]{1,0:T(8,128)S(1)}, f32[608,128]{1,0:T(8,128)S(1)}, u32[]{:S(2)}, u32[]{:S(2)}) collective-permute-start(f32[608,128]{1,0:T(8,128)S(1)} %pad_maximum_fusion.refs_0_), channel_id=1, source_target_pairs={{0,64},{1,33},{2,66},{3,35},{4,68},{5,37},{6,70},{7,39},{8,72},{9,... | collective-permute-start | bytes 933896 | tf_op jit(solution)/shard_map/ppermute | solution.py:78
  66.7 13.0 %collective-permute-start.22 = (f32[608,128]{1,0:T(8,128)S(1)}, f32[608,128]{1,0:T(8,128)S(1)}, u32[]{:S(2)}, u32[]{:S(2)}) collective-permute-start(f32[608,128]{1,0:T(8,128)S(1)} %pad_maximum_fusion.refs_0_), channel_id=1, source_target_pairs={{0,1},{1,0},{2,3},{3,2},{4,5},{5,4},{6,7},{7,6},{8,9},{9,8},{10,11... | collective-permute-start | bytes 933896 | tf_op jit(solution)/shard_map/ppermute | solution.py:78
  71.2 8.4 %collective-permute-start.24 = (f32[608,128]{1,0:T(8,128)S(1)}, f32[608,128]{1,0:T(8,128)S(1)}, u32[]{:S(2)}, u32[]{:S(2)}) collective-permute-start(f32[608,128]{1,0:T(8,128)S(1)} %collective-permute-done.23.refs_2_), channel_id=1, source_target_pairs={{0,1},{1,0},{2,3},{3,2},{4,5},{5,4},{6,7},{7,6},{8,9},{9,8},{10,11... | collective-permute-start | bytes 933896 | tf_op jit(solution)/shard_map/ppermute | solution.py:78
  73.9 7.2 %collective-permute-start.21 = (f32[608,128]{1,0:T(8,128)S(1)}, f32[608,128]{1,0:T(8,128)S(1)}, u32[]{:S(2)}, u32[]{:S(2)}) collective-permute-start(f32[608,128]{1,0:T(8,128)S(1)} %pad_maximum_fusion.refs_0_), channel_id=1, source_target_pairs={{0,192},{1,35},{2,194},{3,33},{4,196},{5,39},{6,198},{7,37},{8,200... | collective-permute-start | bytes 933896 | tf_op jit(solution)/shard_map/ppermute | solution.py:78
  77.2 4.0 %collective-permute-start.27 = (f32[608,128]{1,0:T(8,128)S(1)}, f32[608,128]{1,0:T(8,128)S(1)}, u32[]{:S(2)}, u32[]{:S(2)}) collective-permute-start(f32[608,128]{1,0:T(8,128)S(1)} %collective-permute-done.26.refs_1_), channel_id=1, source_target_pairs={{0,1},{1,0},{2,3},{3,2},{4,5},{5,4},{6,7},{7,6},{8,9},{9,8},{10,11... | collective-permute-start | bytes 933896 | tf_op jit(solution)/shard_map/ppermute | solution.py:78
  (5 other events, 12.0 us)

commit v3 on v2

--- a/solution.py
+++ b/solution.py
@@ -57,6 +57,7 @@
 DEVICES = CORES * X_SIZE * Y_SIZE * Z_SIZE
 LANES = 128
 VMEM_LIMIT = 32 * 1024 * 1024
+COST = 16 * 1024 * 1024
 
 
 def place(dom, rep):
@@ -141,14 +142,11 @@
 
 def piece_at(half, x, y, r, s, piece):
     first, second = jnp.where(half == 0, x, y), jnp.where(half == 0, y, x)
-    block = half * X_SIZE + (first + r) % X_SIZE
-    return pl.multiple_of((block * Y_SIZE + (second + s) % Y_SIZE) * piece, 8)
+    return pl.multiple_of(((first + r) % X_SIZE * Y_SIZE + (second + s) % Y_SIZE) * piece, 8)
 
 
 def grad_kernel(counts_ref, left_ref, right_ref, rel_ref, src_ref, rid_ref, dst_ref, negl_ref, negr_ref, *refs):
-    send_refs, keep_refs = refs[:X_SIZE], refs[X_SIZE:2 * X_SIZE]
-    q_ref, p_ref, gr_ref, gl_ref, ds_ref, dt_ref, rows_ref, near_left_ref, near_right_ref, near_rel_ref, sems = refs[2 * X_SIZE:]
-    core, x, y, _ = here()
+    dw_ref, pick_ref, q_ref, p_ref, gr_ref, gl_ref, ds_ref, dt_ref, near_left_ref, near_right_ref, near_rel_ref, sems = refs
     fetches = []
     for n, pair in enumerate(((left_ref, near_left_ref), (right_ref, near_right_ref), (rel_ref, near_rel_ref))):
         fetches.append(pltpu.make_async_copy(*pair, sems.at[n]))
@@ -190,23 +188,32 @@
     dq, dp = halves(d_q), halves(d_p)
     a, b = adjoint(dq, s), adjoint(dp, t)
     d_w = jnp.concatenate([a[0] + b[0], a[1] - b[1]], axis=0)
-    d_relation = dot_picked(d_w, pick_rel, NT)
-    width = d_relation.shape[0]
-    block, piece = piece_rows(width * types)
-    pad = piece * Y_SIZE - block
-    if pad:
-        for k in range(CORES * X_SIZE):
-            rows_ref[(k + 1) * (block + pad) - pad:(k + 1) * (block + pad), :] = jnp.zeros((pad, LANES), F32)
-    for k, start, size, row in spans(width, types):
-        rows_ref[row:row + size, :] = d_relation[start:start + size, k * LANES:(k + 1) * LANES]
-    for out_refs, half in ((send_refs, 1 - core), (keep_refs, core)):
-        for r in range(X_SIZE):
-            for s in range(Y_SIZE):
-                out_refs[r][s * piece:(s + 1) * piece, :] = rows_ref[pl.ds(piece_at(half, x, y, r, s, piece), piece), :]
+    dw_ref[...], pick_ref[...] = d_w, pick_rel
     q_ref[...], p_ref[...] = q, p
     gr_ref[...], gl_ref[...] = g_right, g_left
     ds_ref[...] = jnp.concatenate(adjoint(dq, w), axis=0)
     dt_ref[...] = jnp.concatenate(product(dp, w), axis=0) + d_pos * q
+
+
+def blocks_kernel(mine, dw_ref, pick_ref, *refs):
+    out_refs, rows_ref = refs[:-1], refs[-1]
+    core, x, y, _ = here()
+    half = core if mine else 1 - core
+    width, types = dw_ref.shape[0], pick_ref.shape[0] // CORES
+    block, piece = piece_rows(width * types * CORES)
+    pad = piece * Y_SIZE - block
+    picks = pick_ref[pl.ds(pl.multiple_of(half * types, LANES), types), :]
+    grad = dot_picked(dw_ref[...], picks, NT)
+    if pad:
+        for k in range(X_SIZE):
+            rows_ref[(k + 1) * (block + pad) - pad:(k + 1) * (block + pad), :] = jnp.zeros((pad, LANES), F32)
+    for k, start, size, row in spans(width, types * CORES):
+        if k < types // LANES:
+            rows_ref[row:row + size, :] = grad[start:start + size, k * LANES:(k + 1) * LANES]
+    for r, out_ref in enumerate(out_refs):
+        for s in range(Y_SIZE):
+            at = piece_at(half, x, y, r, s, piece)
+            out_ref[s * piece:(s + 1) * piece, :] = rows_ref[pl.ds(at, piece), :]
 
 
 def rows_kernel(src_ref, dst_ref, q_ref, p_ref, gr_ref, gl_ref, ds_ref, dt_ref, send_ref, keep_ref):
@@ -236,14 +243,15 @@
     return pltpu.with_memory_space_constraint(value, pltpu.HBM)
 
 
-def call(kernel, specs, arrays, shapes, scratch=(), own=True):
+def call(kernel, specs, arrays, shapes, scratch=()):
     return pl.pallas_call(
         kernel,
-        out_shape=[pltpu.VMEM(shape, F32) if own else jax.ShapeDtypeStruct(shape, F32) for shape in shapes],
+        out_shape=[pltpu.VMEM(shape[0], shape[1]) if isinstance(shape[0], tuple) else pltpu.VMEM(shape, F32) for shape in shapes],
         in_specs=list(specs) + [WHOLE] * (len(arrays) - len(specs)),
         out_specs=[WHOLE] * len(shapes),
         scratch_shapes=list(scratch),
         compiler_params=pltpu.CompilerParams(vmem_limit_bytes=VMEM_LIMIT),
+        cost_estimate=pl.CostEstimate(flops=0, transcendentals=0, bytes_accessed=COST),
     )(*arrays)
 
 
@@ -263,70 +271,79 @@
         out_ref[width:, :] = jnp.broadcast_to(new_state, (8, half))
 
 
-def join_kernel(own_left_ref, other_left_ref, own_right_ref, other_right_ref, left_ref, left_state_ref, right_ref, right_state_ref):
-    first = here()[0] == 0
-    width = left_ref.shape[0]
-    half = own_left_ref.shape[1]
-    for own_ref, other_ref, rows_ref, state_ref in (
-        (own_left_ref, other_left_ref, left_ref, left_state_ref),
-        (own_right_ref, other_right_ref, right_ref, right_state_ref),
-    ):
-        own, other = own_ref[...], other_ref[...]
-        for at, value in ((0, jnp.where(first, own, other)), (half, jnp.where(first, other, own))):
-            rows_ref[:, at:at + half] = value[:width]
-            state_ref[:, at:at + half] = value[width:width + 1]
-
-
-def relation_kernel(steps, *refs):
-    count = 2 * len(steps)
-    in_refs, (out_ref, rows_ref, sems) = refs[-3 - count:-3], refs[-3:]
+def place_kernel(mine, *refs):
+    in_refs, (out_ref, new_rows_ref, new_state_ref) = refs[-X_SIZE - 9:-7], refs[-7:-4]
+    rows_ref, joined_ref, state_ref, sems = refs[-4:]
+    blocks, (own_ref, other_ref) = in_refs[:X_SIZE], in_refs[X_SIZE:]
     core, x, y, _ = here()
+    half = core if mine else 1 - core
     width, types = out_ref.shape
     block, piece = piece_rows(width * types)
     lanes_each = block * LANES // width
-    for n, in_ref in enumerate(in_refs):
-        half = core if n % 2 == 0 else 1 - core
-        second = jnp.where(half == 0, y, x)
+    mine_first, mine_second = jnp.where(half == 0, x, y), jnp.where(half == 0, y, x)
+    columns = own_ref.shape[1]
+    own, other = own_ref[...], other_ref[...]
+    for at, value in ((0, jnp.where(core == 0, own, other)), (columns, jnp.where(core == 0, other, own))):
+        joined_ref[:, at:at + columns] = value[:width]
+        state_ref[:, at:at + columns] = value[width:width + 1]
+    copies = [
+        pltpu.make_async_copy(joined_ref, new_rows_ref, sems.at[X_SIZE, 0]),
+        pltpu.make_async_copy(state_ref, new_state_ref, sems.at[X_SIZE, 1]),
+    ]
+    for copy in copies:
+        copy.start()
+
+    def move(n, begin):
+        first = (mine_first + n) % X_SIZE
+        for low in range(2):
+
+            @pl.when(first % 2 == low)
+            def _():
+                at = 0
+                for i, (k, start, size, _) in enumerate(block_spans(width, types, low)):
+                    lane = (half * X_SIZE + first - low) * lanes_each + k * LANES
+                    copy = pltpu.make_async_copy(
+                        rows_ref.at[n, pl.ds(at, size), :],
+                        out_ref.at[pl.ds(start, size), pl.ds(pl.multiple_of(lane, LANES), LANES)],
+                        sems.at[n, i],
+                    )
+                    if begin:
+                        copy.start()
+                    else:
+                        copy.wait()
+                    at += size
+
+    for n, in_ref in enumerate(blocks):
         for s in range(Y_SIZE):
-            to = pl.multiple_of((second + s) % Y_SIZE * piece, 8)
+            to = pl.multiple_of((mine_second + s) % Y_SIZE * piece, 8)
             rows_ref[n, pl.ds(to, piece), :] = in_ref[s * piece:(s + 1) * piece, :]
-    for begin in (True, False):
-        for n in range(count):
-            half = core if n % 2 == 0 else 1 - core
-            first = (jnp.where(half == 0, x, y) + steps[n // 2]) % X_SIZE
-            for low in range(2):
-
-                @pl.when(first % 2 == low)
-                def _():
-                    at = 0
-                    for i, (k, start, size, _) in enumerate(block_spans(width, types, low)):
-                        lane = (half * X_SIZE + first - low) * lanes_each + k * LANES
-                        copy = pltpu.make_async_copy(
-                            rows_ref.at[n, pl.ds(at, size), :],
-                            out_ref.at[pl.ds(start, size), pl.ds(pl.multiple_of(lane, LANES), LANES)],
-                            sems.at[n, i],
-                        )
-                        if begin:
-                            copy.start()
-                        else:
-                            copy.wait()
-                        at += size
-
-
-def put_relation(steps, blocks, sofar, width, types):
+        move(n, True)
+    for n in range(X_SIZE):
+        move(n, False)
+    for copy in copies:
+        copy.wait()
+
+
+def put(mine, blocks, sofar, rows, shapes):
+    width, types = shapes[0]
     piece = piece_rows(width * types)[1]
     anywhere = pl.BlockSpec(memory_space=pl.ANY)
     before = [] if sofar is None else [sofar]
-    count = len(blocks)
     return pl.pallas_call(
-        functools.partial(relation_kernel, steps),
-        out_shape=jax.ShapeDtypeStruct((width, types), F32),
-        in_specs=[anywhere] * len(before) + [WHOLE] * count,
-        out_specs=anywhere,
-        scratch_shapes=[pltpu.VMEM((count, piece * Y_SIZE, LANES), F32), pltpu.SemaphoreType.DMA((count, 2))],
+        functools.partial(place_kernel, mine),
+        out_shape=[jax.ShapeDtypeStruct(shape, F32) for shape in shapes],
+        in_specs=[anywhere] * len(before) + [WHOLE] * (X_SIZE + 2),
+        out_specs=[anywhere] * 3,
+        scratch_shapes=[
+            pltpu.VMEM((X_SIZE, piece * Y_SIZE, LANES), F32),
+            pltpu.VMEM(shapes[1], F32),
+            pltpu.VMEM(shapes[2], F32),
+            pltpu.SemaphoreType.DMA((X_SIZE + 1, 2)),
+        ],
         input_output_aliases={0: 0} if before else {},
         compiler_params=pltpu.CompilerParams(vmem_limit_bytes=VMEM_LIMIT),
-    )(*before, *[near(value) for value in blocks])
+        cost_estimate=pl.CostEstimate(flops=0, transcendentals=0, bytes_accessed=COST),
+    )(*before, *[near(value) for value in list(blocks) + list(rows)])
 
 
 def scatter(pieces, move):
@@ -354,10 +371,13 @@
         grad_kernel,
         [scalar] + [pl.BlockSpec(memory_space=pl.ANY)] * 3,
         [edge_counts] + [far(value) for value in (left, right, relation, sources, relation_ids, destinations, negatives_left[0], negatives_right[0])],
-        [block] * (2 * X_SIZE) + [(width, edges)] * 2 + [(rows, edges)] * 2 + [(width, edges)] * 2,
-        [pltpu.VMEM((CORES * X_SIZE * block[0], LANES), F32), pltpu.VMEM(left.shape, F32), pltpu.VMEM(right.shape, F32), pltpu.VMEM(relation.shape, F32), pltpu.SemaphoreType.DMA((3,))],
+        [(width, edges), ((types, edges), BF16)] + [(width, edges)] * 2 + [(rows, edges)] * 2 + [(width, edges)] * 2,
+        [pltpu.VMEM(left.shape, F32), pltpu.VMEM(right.shape, F32), pltpu.VMEM(relation.shape, F32), pltpu.SemaphoreType.DMA((3,))],
     )
-    rel_send, rel_keep, saved = found[:X_SIZE], found[X_SIZE:2 * X_SIZE], found[2 * X_SIZE:]
+    by_relation, saved = [near(value) for value in found[:2]], found[2:]
+    staging = [pltpu.VMEM((X_SIZE * block[0], LANES), F32)]
+    rel_send = call(functools.partial(blocks_kernel, False), [], by_relation, [block] * X_SIZE, staging)
+    rel_keep = call(functools.partial(blocks_kernel, True), [], by_relation, [block] * X_SIZE, staging)
 
     blocks = {}
     for r in (2, 1, 3, 0):
@@ -378,7 +398,9 @@
     mine, lr_sum = after(mine, lr_sum)
     lr_other = to_y(lr_sum, 2)
     opposite = to_z(mine, lambda z: z ^ 5)
-    opposite, lr_sum, lr_other = after(opposite, lr_sum, lr_other)
+    mine = (mine + opposite) + (to_z(mine, lambda z: z + 2) + to_z(mine, lambda z: z - 2))
+    found = gather(mine, Y_SIZE, to_second)
+    found[2], lr_sum, lr_other = after(found[2], lr_sum, lr_other)
     packed = (width + 8, rows // CORES)
     new_left, new_right = call(
         adagrad_kernel,
@@ -386,28 +408,16 @@
         [near(lr_sum), near(lr_other)] + [far(value) for value in (left, right, left_state[None], right_state[None])],
         [packed, packed],
     )
+    *found, new_left, new_right = after(*found, new_left, new_right)
     new_right = to_bucket_before(new_right)
     other_left = to_core(new_left)
-    mine = (mine + opposite) + (to_z(mine, lambda z: z + 2) + to_z(mine, lambda z: z - 2))
-
-    mine = jnp.concatenate(gather(mine, Y_SIZE, to_second), axis=0)
-    mine, new_left, other_left, new_right = after(mine, new_left, other_left, new_right)
-    own = gather(mine, X_SIZE, to_first)
-    own[2], new_right = after(own[2], new_right)
-    left_next, left_state_next, right_next, right_state_next = call(
-        join_kernel,
-        [],
-        [near(value) for value in (new_left, other_left, new_right, to_core(new_right))],
-        [(width, rows), (1, rows), (width, rows), (1, rows)],
-        own=False,
-    )
-    relation_grad = put_relation((0, 2), [own[0], to_core(own[0]), own[2], to_core(own[2])], None, width, types)
-    last = own[1]
-    last, relation_grad, left_next, left_state_next, right_next, right_state_next = after(
-        last, relation_grad, left_next, left_state_next, right_next, right_state_next
-    )
-    relation_grad = put_relation((3,), [own[3], to_core(own[3])], relation_grad, width, types)
-    relation_grad = put_relation((1,), [last, to_core(last)], relation_grad, width, types)
+    *found, other_left = after(*found, other_left)
+    own = gather(jnp.concatenate(found, axis=0), X_SIZE, to_first)
+    other_right = to_core(new_right)
+    other = [to_core(value) for value in own]
+    shapes = [(width, types), (width, rows), (1, rows)]
+    relation_grad, left_next, left_state_next = put(True, own, None, [new_left, other_left], shapes)
+    relation_grad, right_next, right_state_next = put(False, other, relation_grad, [new_right, other_right], shapes)
     return left_next.T, left_state_next[0], right_next.T, right_state_next[0], relation_grad.T
 
 

time: 84 us -> 80.9 us (0.963)
  waiting for transfers between devices: 18.2 us -> 16.8 us
  Pallas kernels: 15.3 us -> 14.3 us
    ppermute x28, starting transfers between devices: 45.1 us -> 41.3 us  [send(): return lax.ppermute(value, ('dom', 'rep'), pairs)]
    ppermute x1, starting transfers between devices: 3.3 us -> 6.23 us  [to_bucket_before(): return lax.ppermute(value, ('dom', 'rep'), pairs)]
    ppermute x28, waiting for transfers between devices: 18.2 us -> 16.8 us  [send(): return lax.ppermute(value, ('dom', 'rep'), pairs)]
    pallas_call x7, Pallas kernels: 15.3 us -> 14.3 us  [the longest x5 11.6 us: call(): pl.pallas_call(kernel, out_shape=[pltpu.VMEM(shape[0], shape[1]) if isins...]
  transfers between devices with their start and end apart: 29 -> 29, of which waited for: 14 -> 10; matrix products, arithmetic and copies ran while one was open for 0% -> 0% of each run, Pallas kernels for 8% -> 7%
where the time goes in v3:
time: 80.9 us; the launch traced here: 80.6 us
  starting transfers between devices  47.6 us (59%)
  waiting for transfers between devices  16.8 us (21%)
  Pallas kernels  14.3 us (18%)
  between operations  1.61 us (2%)
    ppermute x28, starting transfers between devices, send(): return lax.ppermute(value, ('dom', 'rep'), pairs)  41.3 us
    ppermute x28, waiting for transfers between devices, send(): return lax.ppermute(value, ('dom', 'rep'), pairs)  16.8 us
    pallas_call x5, Pallas kernels, call(): pl.pallas_call(kernel, out_shape=[pltpu.VMEM(shape[0], shape[1]) if isins...  11.6 us
    ppermute x1, starting transfers between devices, to_bucket_before(): return lax.ppermute(value, ('dom', 'rep'), pairs)  6.23 us
    pallas_call x2, Pallas kernels, put(): pl.pallas_call(functools.partial(place_kernel, mine), out_shape=[jax.Shap...  2.69 us
  transfers between devices with their start and end apart: 29, of which 10 were waited for; matrix products, arithmetic and copies ran while one was open for 0% of the time, Pallas kernels for 7%

profile of v3, /device:TPU:1, one launch (start us, length us, event | category | flops | bytes accessed | tf_op | source)
XLA Modules:
  0.0 80.6 jit_solution(8484659157443778376)
XLA Ops:
  1.3 6.5 %shard_map.146 = (f32[400,512]{1,0:T(8,128)S(1)}, bf16[1536,512]{1,0:T(8,128)(2,1)S(1)}, f32[400,512]{1,0:T(8,128)S(1)}, f32[400,512]{1,0:T(8,128)S(1)}, f32[256...) custom-call(s32[1]{0:T(128)S(6)} %copy.21.counts_ref, ...), custom_call_target="tpu_custom_call" | custom-call | bytes 16777216 | tf_op jit(solution)/shard_map/pallas_call | solution.py:247
  8.8 3.3 %collective-permute-start.1 = (f32[608,128]{1,0:T(8,128)S(1)}, f32[608,128]{1,0:T(8,128)S(1)}, u32[]{:S(2)}, u32[]{:S(2)}) collective-permute-start(f32[608,128]{1,0:T(8,128)S(1)} %get-tuple-element.59), channel_id=1, source_target_pairs={{0,1},{1,0},{2,3},{3,2},{4,5},{5,4},{6,7},{7,6},{8,9},{9,8},{10,11... | collective-permute-start | bytes 933896 | tf_op jit(solution)/shard_map/ppermute | solution.py:79
  13.7 1.3 %collective-permute-start.2 = (f32[608,128]{1,0:T(8,128)S(1)}, f32[608,128]{1,0:T(8,128)S(1)}, u32[]{:S(2)}, u32[]{:S(2)}) collective-permute-start(f32[608,128]{1,0:T(8,128)S(1)} %add.46), channel_id=1, source_target_pairs={{0,128},{1,3},{2,130},{3,1},{4,132},{5,7},{6,134},{7,5},{8,136},{9... | collective-permute-start | bytes 933896 | tf_op jit(solution)/shard_map/ppermute | solution.py:79
  15.5 2.4 %collective-permute-start.6 = (f32[608,128]{1,0:T(8,128)S(1)}, f32[608,128]{1,0:T(8,128)S(1)}, u32[]{:S(2)}, u32[]{:S(2)}) collective-permute-start(f32[608,128]{1,0:T(8,128)S(1)} %add.50), channel_id=1, source_target_pairs={{0,192},{1,35},{2,194},{3,33},{4,196},{5,39},{6,198},{7,37},{8,200... | collective-permute-start | bytes 933896 | tf_op jit(solution)/shard_map/ppermute | solution.py:79
  17.9 2.0 %shard_map.149 = (f32[800,128]{1,0:T(8,128)S(1)}, f32[800,128]{1,0:T(8,128)S(1)}) custom-call(s32[1,512]{1,0:T(1,128)} %src_ref.3, s32[1,512]{1,0:T(1,128)} %dst_ref.3, f32[400,512]{1,0:T(8,128)S(1)} %get-tuple-element.71.q_ref, f32[400,512]{1,0:T(8,128)S(1)} %get-tuple-element.72.p_ref, f32[256,512]{1,0:T(8,128)S(1)} %get-tuple-element.73.gr_ref, ...), custom_call_target="tpu_custom_call" | custom-call | bytes 16777216 | tf_op jit(solution)/shard_map/pallas_call | solution.py:247
  19.8 1.3 %collective-permute-start.11 = (f32[800,128]{1,0:T(8,128)S(1)}, f32[800,128]{1,0:T(8,128)S(1)}, u32[]{:S(2)}, u32[]{:S(2)}) collective-permute-start(f32[800,128]{1,0:T(8,128)S(1)} %get-tuple-element.78), channel_id=1, source_target_pairs={{0,1},{1,0},{2,3},{3,2},{4,5},{5,4},{6,7},{7,6},{8,9},{9,8},{10,11... | collective-permute-start | bytes 1228808 | tf_op jit(solution)/shard_map/ppermute | solution.py:79
  21.4 3.3 %collective-permute-done.4 = f32[608,128]{1,0:T(8,128)S(1)} collective-permute-done((f32[608,128]{1,0:T(8,128)S(1)}, f32[608,128]{1,0:T(8,128)S(1)}, u32[]{:S(2)}, u32[]{:S(2)}) %collective-permute-start.4) | collective-permute-done | bytes 311328 | tf_op jit(solution)/shard_map/ppermute | solution.py:79
  24.8 1.4 %collective-permute-start.7 = (f32[152,128]{1,0:T(8,128)S(1)}, f32[152,128]{1,0:T(8,128)S(1)}, u32[]{:S(2)}, u32[]{:S(2)}) collective-permute-start(f32[152,128]{1,0:T(8,128)S(1)} %get-tuple-element.103), channel_id=1, source_target_pairs={{0,2},{1,129},{2,0},{3,131},{4,6},{5,133},{6,4},{7,135},{8,10},{9,... | collective-permute-start | bytes 233480 | tf_op jit(solution)/shard_map/ppermute | solution.py:79
  27.6 1.9 %collective-permute-done.7 = f32[152,128]{1,0:T(8,128)S(1)} collective-permute-done((f32[152,128]{1,0:T(8,128)S(1)}, f32[152,128]{1,0:T(8,128)S(1)}, u32[]{:S(2)}, u32[]{:S(2)}) %collective-permute-start.7) | collective-permute-done | bytes 77856 | tf_op jit(solution)/shard_map/ppermute | solution.py:79
  29.6 2.0 %collective-permute-done.8 = f32[152,128]{1,0:T(8,128)S(1)} collective-permute-done((f32[152,128]{1,0:T(8,128)S(1)}, f32[152,128]{1,0:T(8,128)S(1)}, u32[]{:S(2)}, u32[]{:S(2)}) %collective-permute-start.8) | collective-permute-done | bytes 77856 | tf_op jit(solution)/shard_map/ppermute | solution.py:79
  31.6 1.6 %collective-permute-start.10 = (f32[152,128]{1,0:T(8,128)S(1)}, f32[152,128]{1,0:T(8,128)S(1)}, u32[]{:S(2)}, u32[]{:S(2)}) collective-permute-start(f32[152,128]{1,0:T(8,128)S(1)} %fusion.1), channel_id=1, source_target_pairs={{0,4},{1,5},{2,6},{3,7},{4,0},{5,1},{6,2},{7,3},{8,12},{9,13},{10,... | collective-permute-start | bytes 233480 | tf_op jit(solution)/shard_map/ppermute | solution.py:79
  33.3 1.7 %collective-permute-done.10 = f32[152,128]{1,0:T(8,128)S(1)} collective-permute-done((f32[152,128]{1,0:T(8,128)S(1)}, f32[152,128]{1,0:T(8,128)S(1)}, u32[]{:S(2)}, u32[]{:S(2)}) %collective-permute-start.10) | collective-permute-done | bytes 77856 | tf_op jit(solution)/shard_map/ppermute | solution.py:79
  35.1 2.0 %collective-permute-start.17 = (f32[800,128]{1,0:T(8,128)S(1)}, f32[800,128]{1,0:T(8,128)S(1)}, u32[]{:S(2)}, u32[]{:S(2)}) collective-permute-start(f32[800,128]{1,0:T(8,128)S(1)} %add.56.kept_ref), channel_id=1, source_target_pairs={{0,2},{1,3},{2,0},{3,1},{4,6},{5,7},{6,4},{7,5},{8,10},{9,11},{10,... | collective-permute-start | bytes 1228808 | tf_op jit(solution)/shard_map/ppermute | solution.py:79
  37.1 5.8 %collective-permute-start.14 = (f32[152,128]{1,0:T(8,128)S(1)}, f32[152,128]{1,0:T(8,128)S(1)}, u32[]{:S(2)}, u32[]{:S(2)}) collective-permute-start(f32[152,128]{1,0:T(8,128)S(1)} %add.55), channel_id=1, source_target_pairs={{0,24},{1,25},{2,26},{3,27},{4,28},{5,29},{6,30},{7,31},{8,0},{9,1... | collective-permute-start | bytes 233480 | tf_op jit(solution)/shard_map/ppermute | solution.py:79
  42.9 2.8 %collective-permute-start.12 = (f32[152,128]{1,0:T(8,128)S(1)}, f32[152,128]{1,0:T(8,128)S(1)}, u32[]{:S(2)}, u32[]{:S(2)}) collective-permute-start(f32[152,128]{1,0:T(8,128)S(1)} %add.55), channel_id=1, source_target_pairs={{0,20},{1,21},{2,22},{3,23},{4,16},{5,17},{6,18},{7,19},{8,28},{9,... | collective-permute-start | bytes 233480 | tf_op jit(solution)/shard_map/ppermute | solution.py:79
  45.7 3.7 %collective-permute-done.13 = f32[152,128]{1,0:T(8,128)S(1)} collective-permute-done((f32[152,128]{1,0:T(8,128)S(1)}, f32[152,128]{1,0:T(8,128)S(1)}, u32[]{:S(2)}, u32[]{:S(2)}) %collective-permute-start.13) | collective-permute-done | bytes 77856 | tf_op jit(solution)/shard_map/ppermute | solution.py:79
  50.4 2.4 %collective-permute-start.15 = (f32[152,128]{1,0:T(8,128)S(1)}, f32[152,128]{1,0:T(8,128)S(1)}, u32[]{:S(2)}, u32[]{:S(2)}) collective-permute-start(f32[152,128]{1,0:T(8,128)S(1)} %add_add_fusion.1), channel_id=1, source_target_pairs={{0,34},{1,193},{2,32},{3,195},{4,38},{5,197},{6,36},{7,199},{8,42}... | collective-permute-start | bytes 233480 | tf_op jit(solution)/shard_map/ppermute | solution.py:79
  52.7 1.6 %collective-permute-done.16 = f32[152,128]{1,0:T(8,128)S(1)} collective-permute-done((f32[152,128]{1,0:T(8,128)S(1)}, f32[152,128]{1,0:T(8,128)S(1)}, u32[]{:S(2)}, u32[]{:S(2)}) %collective-permute-start.16) | collective-permute-done | bytes 77856 | tf_op jit(solution)/shard_map/ppermute | solution.py:79
  54.3 1.3 %shard_map.150 = (f32[408,128]{1,0:T(8,128)S(1)}, f32[408,128]{1,0:T(8,128)S(1)}) custom-call(f32[800,128]{1,0:T(8,128)S(1)} %add.56.kept_ref, f32[800,128]{1,0:T(8,128)S(1)} %collective-permute-done.17.got_ref, f32[400,256]{1,0:T(8,128)} %bitcast.15, f32[400,256]{1,0:T(8,128)} %bitcast.17, f32[1,256]{1,0:T(1,128)} %bitcast.20, f32[1,256]{1,0:T(1,128)} %bitcast.21), custom_call_target="tpu_custom_call" | custom-call | bytes 16777216 | tf_op jit(solution)/shard_map/pallas_call | solution.py:247
  55.6 7.1 %collective-permute-start.19 = (f32[408,128]{1,0:T(8,128)S(1)}, f32[408,128]{1,0:T(8,128)S(1)}, u32[]{:S(2)}, u32[]{:S(2)}) collective-permute-start(f32[408,128]{1,0:T(8,128)S(1)} %get-tuple-element.90.refs_4_), channel_id=1, source_target_pairs={{0,1},{1,0},{2,3},{3,2},{4,5},{5,4},{6,7},{7,6},{8,9},{9,8},{10,11... | collective-permute-start | bytes 626696 | tf_op jit(solution)/shard_map/ppermute | solution.py:79
  63.9 4.1 %collective-permute-start.21 = (f32[608,128]{1,0:T(8,128)S(1)}, f32[608,128]{1,0:T(8,128)S(1)}, u32[]{:S(2)}, u32[]{:S(2)}) collective-permute-start(f32[608,128]{1,0:T(8,128)S(1)} %constant_dynamic-update-slice_fusion.refs_0_), channel_id=1, source_target_pairs={{0,128},{1,3},{2,130},{3,1},{4,132},{5,7},{6,134},{7,5},{8,136},{9... | collective-permute-start | bytes 933896 | tf_op jit(solution)/shard_map/ppermute | solution.py:79
  68.1 6.2 %collective-permute-start.27 = (f32[408,128]{1,0:T(8,128)S(1)}, f32[408,128]{1,0:T(8,128)S(1)}, u32[]{:S(2)}, u32[]{:S(2)}) collective-permute-start(f32[408,128]{1,0:T(8,128)S(1)} %get-tuple-element.99), channel_id=1, source_target_pairs={{0,252},{1,253},{2,254},{3,255},{4,0},{5,1},{6,2},{7,3},{8,4},{9,5... | collective-permute-start | bytes 626696 | tf_op jit(solution)/shard_map/ppermute | solution.py:112
  77.6 1.3 %shard_map.151 = (f32[400,1536]{1,0:T(8,128)}, f32[400,256]{1,0:T(8,128)}, f32[1,256]{1,0:T(1,128)}) custom-call(f32[608,128]{1,0:T(8,128)S(1)} %constant_dynamic-update-slice_fusion.refs_0_, f32[608,128]{1,0:T(8,128)S(1)} %collective-permute-done.20.refs_1_, f32[608,128]{1,0:T(8,128)S(1)} %collective-permute-done.21.refs_2_, ...), custom_call_target="tpu_custom_call" | custom-call | bytes 16777216 | tf_op jit(solution)/shard_map/pallas_call | solution.py:332
  79.1 1.3 %shard_map.152 = (f32[400,1536]{1,0:T(8,128)}, f32[400,256]{1,0:T(8,128)}, f32[1,256]{1,0:T(1,128)}) custom-call(f32[400,1536]{1,0:T(8,128)} %get-tuple-element.98.refs_0_, f32[608,128]{1,0:T(8,128)S(1)} %collective-permute-done.23.refs_1_, f32[608,128]{1,0:T(8,128)S(1)} %collective-permute-done.24.refs_2_, ...), custom_call_target="tpu_custom_call", output_to_operand_aliasing={{0}: (0, {})} | custom-call | bytes 16777216 | tf_op jit(solution)/shard_map/pallas_call | solution.py:332
  (54 shorter events, 10.5 us)
Async XLA Ops:
  8.8 4.9 %collective-permute-start.1 = (f32[608,128]{1,0:T(8,128)S(1)}, f32[608,128]{1,0:T(8,128)S(1)}, u32[]{:S(2)}, u32[]{:S(2)}) collective-permute-start(f32[608,128]{1,0:T(8,128)S(1)} %get-tuple-element.59), channel_id=1, source_target_pairs={{0,1},{1,0},{2,3},{3,2},{4,5},{5,4},{6,7},{7,6},{8,9},{9,8},{10,11... | collective-permute-start | bytes 933896 | tf_op jit(solution)/shard_map/ppermute | solution.py:79
  12.6 8.6 %collective-permute-start = (f32[608,128]{1,0:T(8,128)S(1)}, f32[608,128]{1,0:T(8,128)S(1)}, u32[]{:S(2)}, u32[]{:S(2)}) collective-permute-start(f32[608,128]{1,0:T(8,128)S(1)} %get-tuple-element.57), channel_id=1, source_target_pairs={{0,1},{1,0},{2,3},{3,2},{4,5},{5,4},{6,7},{7,6},{8,9},{9,8},{10,11... | collective-permute-start | bytes 933896 | tf_op jit(solution)/shard_map/ppermute | solution.py:79
  13.7 7.7 %collective-permute-start.2 = (f32[608,128]{1,0:T(8,128)S(1)}, f32[608,128]{1,0:T(8,128)S(1)}, u32[]{:S(2)}, u32[]{:S(2)}) collective-permute-start(f32[608,128]{1,0:T(8,128)S(1)} %add.46), channel_id=1, source_target_pairs={{0,128},{1,3},{2,130},{3,1},{4,132},{5,7},{6,134},{7,5},{8,136},{9... | collective-permute-start | bytes 933896 | tf_op jit(solution)/shard_map/ppermute | solution.py:79
  15.0 9.7 %collective-permute-start.4 = (f32[608,128]{1,0:T(8,128)S(1)}, f32[608,128]{1,0:T(8,128)S(1)}, u32[]{:S(2)}, u32[]{:S(2)}) collective-permute-start(f32[608,128]{1,0:T(8,128)S(1)} %add.48), channel_id=1, source_target_pairs={{0,64},{1,33},{2,66},{3,35},{4,68},{5,37},{6,70},{7,39},{8,72},{9,... | collective-permute-start | bytes 933896 | tf_op jit(solution)/shard_map/ppermute | solution.py:79
  15.5 9.1 %collective-permute-start.6 = (f32[608,128]{1,0:T(8,128)S(1)}, f32[608,128]{1,0:T(8,128)S(1)}, u32[]{:S(2)}, u32[]{:S(2)}) collective-permute-start(f32[608,128]{1,0:T(8,128)S(1)} %add.50), channel_id=1, source_target_pairs={{0,192},{1,35},{2,194},{3,33},{4,196},{5,39},{6,198},{7,37},{8,200... | collective-permute-start | bytes 933896 | tf_op jit(solution)/shard_map/ppermute | solution.py:79
  19.8 13.4 %collective-permute-start.11 = (f32[800,128]{1,0:T(8,128)S(1)}, f32[800,128]{1,0:T(8,128)S(1)}, u32[]{:S(2)}, u32[]{:S(2)}) collective-permute-start(f32[800,128]{1,0:T(8,128)S(1)} %get-tuple-element.78), channel_id=1, source_target_pairs={{0,1},{1,0},{2,3},{3,2},{4,5},{5,4},{6,7},{7,6},{8,9},{9,8},{10,11... | collective-permute-start | bytes 1228808 | tf_op jit(solution)/shard_map/ppermute | solution.py:79
  24.8 4.8 %collective-permute-start.7 = (f32[152,128]{1,0:T(8,128)S(1)}, f32[152,128]{1,0:T(8,128)S(1)}, u32[]{:S(2)}, u32[]{:S(2)}) collective-permute-start(f32[152,128]{1,0:T(8,128)S(1)} %get-tuple-element.103), channel_id=1, source_target_pairs={{0,2},{1,129},{2,0},{3,131},{4,6},{5,133},{6,4},{7,135},{8,10},{9,... | collective-permute-start | bytes 233480 | tf_op jit(solution)/shard_map/ppermute | solution.py:79
  26.2 3.4 %collective-permute-start.9 = (f32[152,128]{1,0:T(8,128)S(1)}, f32[152,128]{1,0:T(8,128)S(1)}, u32[]{:S(2)}, u32[]{:S(2)}) collective-permute-start(f32[152,128]{1,0:T(8,128)S(1)} %get-tuple-element.104), channel_id=1, source_target_pairs={{0,34},{1,193},{2,32},{3,195},{4,38},{5,197},{6,36},{7,199},{8,42}... | collective-permute-start | bytes 233480 | tf_op jit(solution)/shard_map/ppermute | solution.py:79
  27.0 4.6 %collective-permute-start.8 = (f32[152,128]{1,0:T(8,128)S(1)}, f32[152,128]{1,0:T(8,128)S(1)}, u32[]{:S(2)}, u32[]{:S(2)}) collective-permute-start(f32[152,128]{1,0:T(8,128)S(1)} %get-tuple-element.105), channel_id=1, source_target_pairs={{0,32},{1,65},{2,34},{3,67},{4,36},{5,69},{6,38},{7,71},{8,40},{9,... | collective-permute-start | bytes 233480 | tf_op jit(solution)/shard_map/ppermute | solution.py:79
  31.6 3.4 %collective-permute-start.10 = (f32[152,128]{1,0:T(8,128)S(1)}, f32[152,128]{1,0:T(8,128)S(1)}, u32[]{:S(2)}, u32[]{:S(2)}) collective-permute-start(f32[152,128]{1,0:T(8,128)S(1)} %fusion.1), channel_id=1, source_target_pairs={{0,4},{1,5},{2,6},{3,7},{4,0},{5,1},{6,2},{7,3},{8,12},{9,13},{10,... | collective-permute-start | bytes 233480 | tf_op jit(solution)/shard_map/ppermute | solution.py:79
  35.1 19.3 %collective-permute-start.17 = (f32[800,128]{1,0:T(8,128)S(1)}, f32[800,128]{1,0:T(8,128)S(1)}, u32[]{:S(2)}, u32[]{:S(2)}) collective-permute-start(f32[800,128]{1,0:T(8,128)S(1)} %add.56.kept_ref), channel_id=1, source_target_pairs={{0,2},{1,3},{2,0},{3,1},{4,6},{5,7},{6,4},{7,5},{8,10},{9,11},{10,... | collective-permute-start | bytes 1228808 | tf_op jit(solution)/shard_map/ppermute | solution.py:79
  37.1 8.7 %collective-permute-start.14 = (f32[152,128]{1,0:T(8,128)S(1)}, f32[152,128]{1,0:T(8,128)S(1)}, u32[]{:S(2)}, u32[]{:S(2)}) collective-permute-start(f32[152,128]{1,0:T(8,128)S(1)} %add.55), channel_id=1, source_target_pairs={{0,24},{1,25},{2,26},{3,27},{4,28},{5,29},{6,30},{7,31},{8,0},{9,1... | collective-permute-start | bytes 233480 | tf_op jit(solution)/shard_map/ppermute | solution.py:79
  42.9 6.5 %collective-permute-start.13 = (f32[152,128]{1,0:T(8,128)S(1)}, f32[152,128]{1,0:T(8,128)S(1)}, u32[]{:S(2)}, u32[]{:S(2)}) collective-permute-start(f32[152,128]{1,0:T(8,128)S(1)} %add.55), channel_id=1, source_target_pairs={{0,8},{1,9},{2,10},{3,11},{4,12},{5,13},{6,14},{7,15},{8,16},{9,17... | collective-permute-start | bytes 233480 | tf_op jit(solution)/shard_map/ppermute | solution.py:79
  42.9 6.5 %collective-permute-start.12 = (f32[152,128]{1,0:T(8,128)S(1)}, f32[152,128]{1,0:T(8,128)S(1)}, u32[]{:S(2)}, u32[]{:S(2)}) collective-permute-start(f32[152,128]{1,0:T(8,128)S(1)} %add.55), channel_id=1, source_target_pairs={{0,20},{1,21},{2,22},{3,23},{4,16},{5,17},{6,18},{7,19},{8,28},{9,... | collective-permute-start | bytes 233480 | tf_op jit(solution)/shard_map/ppermute | solution.py:79
  49.4 4.9 %collective-permute-start.16 = (f32[152,128]{1,0:T(8,128)S(1)}, f32[152,128]{1,0:T(8,128)S(1)}, u32[]{:S(2)}, u32[]{:S(2)}) collective-permute-start(f32[152,128]{1,0:T(8,128)S(1)} %add_add_fusion.1), channel_id=1, source_target_pairs={{0,2},{1,129},{2,0},{3,131},{4,6},{5,133},{6,4},{7,135},{8,10},{9,... | collective-permute-start | bytes 233480 | tf_op jit(solution)/shard_map/ppermute | solution.py:79
  50.1 5.6 %collective-permute-start.18 = (f32[152,128]{1,0:T(8,128)S(1)}, f32[152,128]{1,0:T(8,128)S(1)}, u32[]{:S(2)}, u32[]{:S(2)}) collective-permute-start(f32[152,128]{1,0:T(8,128)S(1)} %add_add_fusion.1), channel_id=1, source_target_pairs={{0,32},{1,65},{2,34},{3,67},{4,36},{5,69},{6,38},{7,71},{8,40},{9,... | collective-permute-start | bytes 233480 | tf_op jit(solution)/shard_map/ppermute | solution.py:79
  50.4 5.2 %collective-permute-start.15 = (f32[152,128]{1,0:T(8,128)S(1)}, f32[152,128]{1,0:T(8,128)S(1)}, u32[]{:S(2)}, u32[]{:S(2)}) collective-permute-start(f32[152,128]{1,0:T(8,128)S(1)} %add_add_fusion.1), channel_id=1, source_target_pairs={{0,34},{1,193},{2,32},{3,195},{4,38},{5,197},{6,36},{7,199},{8,42}... | collective-permute-start | bytes 233480 | tf_op jit(solution)/shard_map/ppermute | solution.py:79
  55.6 8.2 %collective-permute-start.19 = (f32[408,128]{1,0:T(8,128)S(1)}, f32[408,128]{1,0:T(8,128)S(1)}, u32[]{:S(2)}, u32[]{:S(2)}) collective-permute-start(f32[408,128]{1,0:T(8,128)S(1)} %get-tuple-element.90.refs_4_), channel_id=1, source_target_pairs={{0,1},{1,0},{2,3},{3,2},{4,5},{5,4},{6,7},{7,6},{8,9},{9,8},{10,11... | collective-permute-start | bytes 626696 | tf_op jit(solution)/shard_map/ppermute | solution.py:79
  63.9 10.5 %collective-permute-start.22 = (f32[608,128]{1,0:T(8,128)S(1)}, f32[608,128]{1,0:T(8,128)S(1)}, u32[]{:S(2)}, u32[]{:S(2)}) collective-permute-start(f32[608,128]{1,0:T(8,128)S(1)} %constant_dynamic-update-slice_fusion.refs_0_), channel_id=1, source_target_pairs={{0,64},{1,33},{2,66},{3,35},{4,68},{5,37},{6,70},{7,39},{8,72},{9,... | collective-permute-start | bytes 933896 | tf_op jit(solution)/shard_map/ppermute | solution.py:79
  63.9 12.0 %collective-permute-start.21 = (f32[608,128]{1,0:T(8,128)S(1)}, f32[608,128]{1,0:T(8,128)S(1)}, u32[]{:S(2)}, u32[]{:S(2)}) collective-permute-start(f32[608,128]{1,0:T(8,128)S(1)} %constant_dynamic-update-slice_fusion.refs_0_), channel_id=1, source_target_pairs={{0,128},{1,3},{2,130},{3,1},{4,132},{5,7},{6,134},{7,5},{8,136},{9... | collective-permute-start | bytes 933896 | tf_op jit(solution)/shard_map/ppermute | solution.py:79
  68.1 9.1 %collective-permute-start.20 = (f32[608,128]{1,0:T(8,128)S(1)}, f32[608,128]{1,0:T(8,128)S(1)}, u32[]{:S(2)}, u32[]{:S(2)}) collective-permute-start(f32[608,128]{1,0:T(8,128)S(1)} %constant_dynamic-update-slice_fusion.refs_0_), channel_id=1, source_target_pairs={{0,192},{1,35},{2,194},{3,33},{4,196},{5,39},{6,198},{7,37},{8,200... | collective-permute-start | bytes 933896 | tf_op jit(solution)/shard_map/ppermute | solution.py:79
  68.1 9.1 %collective-permute-start.27 = (f32[408,128]{1,0:T(8,128)S(1)}, f32[408,128]{1,0:T(8,128)S(1)}, u32[]{:S(2)}, u32[]{:S(2)}) collective-permute-start(f32[408,128]{1,0:T(8,128)S(1)} %get-tuple-element.99), channel_id=1, source_target_pairs={{0,252},{1,253},{2,254},{3,255},{4,0},{5,1},{6,2},{7,3},{8,4},{9,5... | collective-permute-start | bytes 626696 | tf_op jit(solution)/shard_map/ppermute | solution.py:112
  74.3 4.8 %collective-permute-start.23 = (f32[608,128]{1,0:T(8,128)S(1)}, f32[608,128]{1,0:T(8,128)S(1)}, u32[]{:S(2)}, u32[]{:S(2)}) collective-permute-start(f32[608,128]{1,0:T(8,128)S(1)} %constant_dynamic-update-slice_fusion.refs_0_), channel_id=1, source_target_pairs={{0,1},{1,0},{2,3},{3,2},{4,5},{5,4},{6,7},{7,6},{8,9},{9,8},{10,11... | collective-permute-start | bytes 933896 | tf_op jit(solution)/shard_map/ppermute | solution.py:79
  74.3 4.8 %collective-permute-start.26 = (f32[608,128]{1,0:T(8,128)S(1)}, f32[608,128]{1,0:T(8,128)S(1)}, u32[]{:S(2)}, u32[]{:S(2)}) collective-permute-start(f32[608,128]{1,0:T(8,128)S(1)} %collective-permute-done.22.refs_3_), channel_id=1, source_target_pairs={{0,1},{1,0},{2,3},{3,2},{4,5},{5,4},{6,7},{7,6},{8,9},{9,8},{10,11... | collective-permute-start | bytes 933896 | tf_op jit(solution)/shard_map/ppermute | solution.py:79
  (5 other events, 13.2 us)

commit v4 on v3

--- a/solution.py
+++ b/solution.py
@@ -145,31 +145,36 @@
     return pl.multiple_of(((first + r) % X_SIZE * Y_SIZE + (second + s) % Y_SIZE) * piece, 8)
 
 
-def grad_kernel(counts_ref, left_ref, right_ref, rel_ref, src_ref, rid_ref, dst_ref, negl_ref, negr_ref, *refs):
-    dw_ref, pick_ref, q_ref, p_ref, gr_ref, gl_ref, ds_ref, dt_ref, near_left_ref, near_right_ref, near_rel_ref, sems = refs
+def grad_kernel(counts_ref, *refs):
+    far_refs, near_refs, sems = refs[:8], refs[-9:-1], refs[-1]
+    dw_ref, pick_ref, q_ref, p_ref, gr_ref, gl_ref, ds_ref, dt_ref = refs[8:-9]
     fetches = []
-    for n, pair in enumerate(((left_ref, near_left_ref), (right_ref, near_right_ref), (rel_ref, near_rel_ref))):
-        fetches.append(pltpu.make_async_copy(*pair, sems.at[n]))
+    for n, (far_ref, near_ref) in enumerate(zip(far_refs, near_refs)):
+        fetches.append(pltpu.make_async_copy(far_ref, near_ref, sems.at[n]))
     for fetch in fetches:
         fetch.start()
+    src_ref, rid_ref, dst_ref, negl_ref, negr_ref, near_left_ref, near_right_ref, near_rel_ref = near_refs
+    left_ref, right_ref, rel_ref = near_left_ref, near_right_ref, near_rel_ref
     slots = src_ref.shape[1]
     rows = left_ref.shape[1]
     types = rel_ref.shape[1]
     negatives = negl_ref.shape[1]
+    for fetch in fetches[:5]:
+        fetch.wait()
     count_right = jnp.sum(one_hot(negr_ref[...], rows), axis=1, keepdims=True)
     count_left = jnp.sum(one_hot(negl_ref[...], rows), axis=1, keepdims=True)
     pick_src = one_hot(src_ref[...], rows).astype(BF16)
     pick_dst = one_hot(dst_ref[...], rows).astype(BF16)
     pick_rel = one_hot(rid_ref[...], types).astype(BF16)
-    fetches[0].wait()
+    fetches[5].wait()
     left = near_left_ref[...]
     source = dot_picked(left, pick_src, NN)
     left_parts, left_rows = parts(left), parts(left.T)
-    fetches[1].wait()
+    fetches[6].wait()
     right = near_right_ref[...]
     target = dot_picked(right, pick_dst, NN)
     right_parts, right_rows = parts(right), parts(right.T)
-    fetches[2].wait()
+    fetches[7].wait()
     weight = dot_picked(near_rel_ref[...], pick_rel, NN)
     s, t, w = halves(source), halves(target), halves(weight)
     q = jnp.concatenate(product(s, w), axis=0)
@@ -243,7 +248,7 @@
     return pltpu.with_memory_space_constraint(value, pltpu.HBM)
 
 
-def call(kernel, specs, arrays, shapes, scratch=()):
+def call(kernel, specs, arrays, shapes, scratch=(), cost=COST):
     return pl.pallas_call(
         kernel,
         out_shape=[pltpu.VMEM(shape[0], shape[1]) if isinstance(shape[0], tuple) else pltpu.VMEM(shape, F32) for shape in shapes],
@@ -251,7 +256,7 @@
         out_specs=[WHOLE] * len(shapes),
         scratch_shapes=list(scratch),
         compiler_params=pltpu.CompilerParams(vmem_limit_bytes=VMEM_LIMIT),
-        cost_estimate=pl.CostEstimate(flops=0, transcendentals=0, bytes_accessed=COST),
+        cost_estimate=pl.CostEstimate(flops=0, transcendentals=0, bytes_accessed=cost),
     )(*arrays)
 
 
@@ -367,12 +372,13 @@
     piece = piece_rows(width * types)[1]
     block = (piece * Y_SIZE, LANES)
     scalar = pl.BlockSpec(memory_space=pltpu.SMEM)
+    given = (sources, relation_ids, destinations, negatives_left[0], negatives_right[0], left, right, relation)
     found = call(
         grad_kernel,
-        [scalar] + [pl.BlockSpec(memory_space=pl.ANY)] * 3,
-        [edge_counts] + [far(value) for value in (left, right, relation, sources, relation_ids, destinations, negatives_left[0], negatives_right[0])],
+        [scalar] + [pl.BlockSpec(memory_space=pl.ANY)] * len(given),
+        [edge_counts] + [far(value) for value in given],
         [(width, edges), ((types, edges), BF16)] + [(width, edges)] * 2 + [(rows, edges)] * 2 + [(width, edges)] * 2,
-        [pltpu.VMEM(left.shape, F32), pltpu.VMEM(right.shape, F32), pltpu.VMEM(relation.shape, F32), pltpu.SemaphoreType.DMA((3,))],
+        [pltpu.VMEM(value.shape, value.dtype) for value in given] + [pltpu.SemaphoreType.DMA((len(given),))],
     )
     by_relation, saved = [near(value) for value in found[:2]], found[2:]
     staging = [pltpu.VMEM((X_SIZE * block[0], LANES), F32)]
@@ -398,7 +404,9 @@
     mine, lr_sum = after(mine, lr_sum)
     lr_other = to_y(lr_sum, 2)
     opposite = to_z(mine, lambda z: z ^ 5)
-    mine = (mine + opposite) + (to_z(mine, lambda z: z + 2) + to_z(mine, lambda z: z - 2))
+    nearer = to_z(mine, lambda z: z + 1 if z % 2 else z - 1)
+    other_side = to_z(mine, lambda z: z + 2 if z % 2 else z - 2)
+    mine = (mine + opposite) + (nearer + other_side)
     found = gather(mine, Y_SIZE, to_second)
     found[2], lr_sum, lr_other = after(found[2], lr_sum, lr_other)
     packed = (width + 8, rows // CORES)
@@ -407,6 +415,7 @@
         [],
         [near(lr_sum), near(lr_other)] + [far(value) for value in (left, right, left_state[None], right_state[None])],
         [packed, packed],
+        cost=0,
     )
     *found, new_left, new_right = after(*found, new_left, new_right)
     new_right = to_bucket_before(new_right)

time: 80.9 us -> 80.6 us (level)
  starting transfers between devices: 47.6 us -> 45.6 us
  waiting for transfers between devices: 16.8 us -> 18.1 us
    ppermute x28, starting transfers between devices: 41.3 us -> 38.6 us  [send(): return lax.ppermute(value, ('dom', 'rep'), pairs)]
  transfers between devices with their start and end apart: 29 -> 29, of which waited for: 10 -> 12; matrix products, arithmetic and copies ran while one was open for 0% -> 0% of each run, Pallas kernels for 7% -> 7%
where the time goes in v4:
time: 80.6 us; the launch traced here: 79.8 us
  starting transfers between devices  45.6 us (57%)
  waiting for transfers between devices  18.1 us (22%)
  Pallas kernels  14.2 us (18%)
  between operations  1.62 us (2%)
    ppermute x28, starting transfers between devices, send(): return lax.ppermute(value, ('dom', 'rep'), pairs)  38.6 us
    ppermute x28, waiting for transfers between devices, send(): return lax.ppermute(value, ('dom', 'rep'), pairs)  17.5 us
    pallas_call x5, Pallas kernels, call(): pl.pallas_call(kernel, out_shape=[pltpu.VMEM(shape[0], shape[1]) if isins...  11.5 us
    ppermute x1, starting transfers between devices, to_bucket_before(): return lax.ppermute(value, ('dom', 'rep'), pairs)  7 us
    pallas_call x2, Pallas kernels, put(): pl.pallas_call(functools.partial(place_kernel, mine), out_shape=[jax.Shap...  2.69 us
  transfers between devices with their start and end apart: 29, of which 12 were waited for; matrix products, arithmetic and copies ran while one was open for 0% of the time, Pallas kernels for 7%

profile of v4, /device:TPU:1, one launch (start us, length us, event | category | flops | bytes accessed | tf_op | source)
XLA Modules:
  0.0 79.8 jit_solution(10069974035161588715)
XLA Ops:
  1.3 6.4 %shard_map.146 = (f32[400,512]{1,0:T(8,128)S(1)}, bf16[1536,512]{1,0:T(8,128)(2,1)S(1)}, f32[400,512]{1,0:T(8,128)S(1)}, f32[400,512]{1,0:T(8,128)S(1)}, f32[256...) custom-call(s32[1]{0:T(128)S(6)} %copy.21.counts_ref, ...), custom_call_target="tpu_custom_call" | custom-call | bytes 16777216 | tf_op jit(solution)/shard_map/pallas_call | solution.py:252
  8.6 3.3 %collective-permute-start.1 = (f32[608,128]{1,0:T(8,128)S(1)}, f32[608,128]{1,0:T(8,128)S(1)}, u32[]{:S(2)}, u32[]{:S(2)}) collective-permute-start(f32[608,128]{1,0:T(8,128)S(1)} %get-tuple-element.59), channel_id=1, source_target_pairs={{0,1},{1,0},{2,3},{3,2},{4,5},{5,4},{6,7},{7,6},{8,9},{9,8},{10,11... | collective-permute-start | bytes 933896 | tf_op jit(solution)/shard_map/ppermute | solution.py:79
  15.4 2.4 %collective-permute-start.6 = (f32[608,128]{1,0:T(8,128)S(1)}, f32[608,128]{1,0:T(8,128)S(1)}, u32[]{:S(2)}, u32[]{:S(2)}) collective-permute-start(f32[608,128]{1,0:T(8,128)S(1)} %add.50), channel_id=1, source_target_pairs={{0,192},{1,35},{2,194},{3,33},{4,196},{5,39},{6,198},{7,37},{8,200... | collective-permute-start | bytes 933896 | tf_op jit(solution)/shard_map/ppermute | solution.py:79
  17.7 2.0 %shard_map.149 = (f32[800,128]{1,0:T(8,128)S(1)}, f32[800,128]{1,0:T(8,128)S(1)}) custom-call(s32[1,512]{1,0:T(1,128)} %src_ref.1, s32[1,512]{1,0:T(1,128)} %dst_ref.1, f32[400,512]{1,0:T(8,128)S(1)} %get-tuple-element.71.q_ref, f32[400,512]{1,0:T(8,128)S(1)} %get-tuple-element.72.p_ref, f32[256,512]{1,0:T(8,128)S(1)} %get-tuple-element.73.gr_ref, ...), custom_call_target="tpu_custom_call" | custom-call | bytes 16777216 | tf_op jit(solution)/shard_map/pallas_call | solution.py:252
  19.7 1.3 %collective-permute-start.11 = (f32[800,128]{1,0:T(8,128)S(1)}, f32[800,128]{1,0:T(8,128)S(1)}, u32[]{:S(2)}, u32[]{:S(2)}) collective-permute-start(f32[800,128]{1,0:T(8,128)S(1)} %get-tuple-element.78), channel_id=1, source_target_pairs={{0,1},{1,0},{2,3},{3,2},{4,5},{5,4},{6,7},{7,6},{8,9},{9,8},{10,11... | collective-permute-start | bytes 1228808 | tf_op jit(solution)/shard_map/ppermute | solution.py:79
  21.2 3.3 %collective-permute-done.4 = f32[608,128]{1,0:T(8,128)S(1)} collective-permute-done((f32[608,128]{1,0:T(8,128)S(1)}, f32[608,128]{1,0:T(8,128)S(1)}, u32[]{:S(2)}, u32[]{:S(2)}) %collective-permute-start.4) | collective-permute-done | bytes 311328 | tf_op jit(solution)/shard_map/ppermute | solution.py:79
  24.6 1.4 %collective-permute-start.7 = (f32[152,128]{1,0:T(8,128)S(1)}, f32[152,128]{1,0:T(8,128)S(1)}, u32[]{:S(2)}, u32[]{:S(2)}) collective-permute-start(f32[152,128]{1,0:T(8,128)S(1)} %get-tuple-element.103), channel_id=1, source_target_pairs={{0,2},{1,129},{2,0},{3,131},{4,6},{5,133},{6,4},{7,135},{8,10},{9,... | collective-permute-start | bytes 233480 | tf_op jit(solution)/shard_map/ppermute | solution.py:79
  27.5 1.9 %collective-permute-done.7 = f32[152,128]{1,0:T(8,128)S(1)} collective-permute-done((f32[152,128]{1,0:T(8,128)S(1)}, f32[152,128]{1,0:T(8,128)S(1)}, u32[]{:S(2)}, u32[]{:S(2)}) %collective-permute-start.7) | collective-permute-done | bytes 77856 | tf_op jit(solution)/shard_map/ppermute | solution.py:79
  29.4 2.0 %collective-permute-done.8 = f32[152,128]{1,0:T(8,128)S(1)} collective-permute-done((f32[152,128]{1,0:T(8,128)S(1)}, f32[152,128]{1,0:T(8,128)S(1)}, u32[]{:S(2)}, u32[]{:S(2)}) %collective-permute-start.8) | collective-permute-done | bytes 77856 | tf_op jit(solution)/shard_map/ppermute | solution.py:79
  31.5 1.6 %collective-permute-start.10 = (f32[152,128]{1,0:T(8,128)S(1)}, f32[152,128]{1,0:T(8,128)S(1)}, u32[]{:S(2)}, u32[]{:S(2)}) collective-permute-start(f32[152,128]{1,0:T(8,128)S(1)} %fusion.1), channel_id=1, source_target_pairs={{0,4},{1,5},{2,6},{3,7},{4,0},{5,1},{6,2},{7,3},{8,12},{9,13},{10,... | collective-permute-start | bytes 233480 | tf_op jit(solution)/shard_map/ppermute | solution.py:79
  33.2 1.7 %collective-permute-done.10 = f32[152,128]{1,0:T(8,128)S(1)} collective-permute-done((f32[152,128]{1,0:T(8,128)S(1)}, f32[152,128]{1,0:T(8,128)S(1)}, u32[]{:S(2)}, u32[]{:S(2)}) %collective-permute-start.10) | collective-permute-done | bytes 77856 | tf_op jit(solution)/shard_map/ppermute | solution.py:79
  34.9 2.0 %collective-permute-start.17 = (f32[800,128]{1,0:T(8,128)S(1)}, f32[800,128]{1,0:T(8,128)S(1)}, u32[]{:S(2)}, u32[]{:S(2)}) collective-permute-start(f32[800,128]{1,0:T(8,128)S(1)} %add.56.kept_ref), channel_id=1, source_target_pairs={{0,2},{1,3},{2,0},{3,1},{4,6},{5,7},{6,4},{7,5},{8,10},{9,11},{10,... | collective-permute-start | bytes 1228808 | tf_op jit(solution)/shard_map/ppermute | solution.py:79
  36.9 5.8 %collective-permute-start.14 = (f32[152,128]{1,0:T(8,128)S(1)}, f32[152,128]{1,0:T(8,128)S(1)}, u32[]{:S(2)}, u32[]{:S(2)}) collective-permute-start(f32[152,128]{1,0:T(8,128)S(1)} %add.55), channel_id=1, source_target_pairs={{0,24},{1,25},{2,26},{3,27},{4,12},{5,13},{6,14},{7,15},{8,0},{9,1... | collective-permute-start | bytes 233480 | tf_op jit(solution)/shard_map/ppermute | solution.py:79
  42.8 2.4 %collective-permute-start.12 = (f32[152,128]{1,0:T(8,128)S(1)}, f32[152,128]{1,0:T(8,128)S(1)}, u32[]{:S(2)}, u32[]{:S(2)}) collective-permute-start(f32[152,128]{1,0:T(8,128)S(1)} %add.55), channel_id=1, source_target_pairs={{0,20},{1,21},{2,22},{3,23},{4,16},{5,17},{6,18},{7,19},{8,28},{9,... | collective-permute-start | bytes 233480 | tf_op jit(solution)/shard_map/ppermute | solution.py:79
  45.1 2.8 %collective-permute-done.13 = f32[152,128]{1,0:T(8,128)S(1)} collective-permute-done((f32[152,128]{1,0:T(8,128)S(1)}, f32[152,128]{1,0:T(8,128)S(1)}, u32[]{:S(2)}, u32[]{:S(2)}) %collective-permute-start.13) | collective-permute-done | bytes 77856 | tf_op jit(solution)/shard_map/ppermute | solution.py:79
  47.9 1.8 %collective-permute-done.12 = f32[152,128]{1,0:T(8,128)S(1)} collective-permute-done((f32[152,128]{1,0:T(8,128)S(1)}, f32[152,128]{1,0:T(8,128)S(1)}, u32[]{:S(2)}, u32[]{:S(2)}) %collective-permute-start.12) | collective-permute-done | bytes 77856 | tf_op jit(solution)/shard_map/ppermute | solution.py:79
  49.9 2.7 %collective-permute-start.15 = (f32[152,128]{1,0:T(8,128)S(1)}, f32[152,128]{1,0:T(8,128)S(1)}, u32[]{:S(2)}, u32[]{:S(2)}) collective-permute-start(f32[152,128]{1,0:T(8,128)S(1)} %add_add_fusion.1), channel_id=1, source_target_pairs={{0,34},{1,193},{2,32},{3,195},{4,38},{5,197},{6,36},{7,199},{8,42}... | collective-permute-start | bytes 233480 | tf_op jit(solution)/shard_map/ppermute | solution.py:79
  52.6 2.1 %collective-permute-done.16 = f32[152,128]{1,0:T(8,128)S(1)} collective-permute-done((f32[152,128]{1,0:T(8,128)S(1)}, f32[152,128]{1,0:T(8,128)S(1)}, u32[]{:S(2)}, u32[]{:S(2)}) %collective-permute-start.16) | collective-permute-done | bytes 77856 | tf_op jit(solution)/shard_map/ppermute | solution.py:79
  54.7 1.3 %shard_map.150 = (f32[408,128]{1,0:T(8,128)S(1)}, f32[408,128]{1,0:T(8,128)S(1)}) custom-call(f32[800,128]{1,0:T(8,128)S(1)} %add.56.kept_ref, f32[800,128]{1,0:T(8,128)S(1)} %collective-permute-done.17.got_ref, f32[400,256]{1,0:T(8,128)} %bitcast.15, f32[400,256]{1,0:T(8,128)} %bitcast.17, f32[1,256]{1,0:T(1,128)} %bitcast.20, f32[1,256]{1,0:T(1,128)} %bitcast.21), custom_call_target="tpu_custom_call" | custom-call | tf_op jit(solution)/shard_map/pallas_call | solution.py:252
  56.0 5.7 %collective-permute-start.19 = (f32[408,128]{1,0:T(8,128)S(1)}, f32[408,128]{1,0:T(8,128)S(1)}, u32[]{:S(2)}, u32[]{:S(2)}) collective-permute-start(f32[408,128]{1,0:T(8,128)S(1)} %get-tuple-element.90.refs_4_), channel_id=1, source_target_pairs={{0,1},{1,0},{2,3},{3,2},{4,5},{5,4},{6,7},{7,6},{8,9},{9,8},{10,11... | collective-permute-start | bytes 626696 | tf_op jit(solution)/shard_map/ppermute | solution.py:79
  63.0 4.1 %collective-permute-start.21 = (f32[608,128]{1,0:T(8,128)S(1)}, f32[608,128]{1,0:T(8,128)S(1)}, u32[]{:S(2)}, u32[]{:S(2)}) collective-permute-start(f32[608,128]{1,0:T(8,128)S(1)} %constant_dynamic-update-slice_fusion.refs_0_), channel_id=1, source_target_pairs={{0,128},{1,3},{2,130},{3,1},{4,132},{5,7},{6,134},{7,5},{8,136},{9... | collective-permute-start | bytes 933896 | tf_op jit(solution)/shard_map/ppermute | solution.py:79
  67.1 7.0 %collective-permute-start.27 = (f32[408,128]{1,0:T(8,128)S(1)}, f32[408,128]{1,0:T(8,128)S(1)}, u32[]{:S(2)}, u32[]{:S(2)}) collective-permute-start(f32[408,128]{1,0:T(8,128)S(1)} %get-tuple-element.99), channel_id=1, source_target_pairs={{0,252},{1,253},{2,254},{3,255},{4,0},{5,1},{6,2},{7,3},{8,4},{9,5... | collective-permute-start | bytes 626696 | tf_op jit(solution)/shard_map/ppermute | solution.py:112
  76.8 1.3 %shard_map.151 = (f32[400,1536]{1,0:T(8,128)}, f32[400,256]{1,0:T(8,128)}, f32[1,256]{1,0:T(1,128)}) custom-call(f32[608,128]{1,0:T(8,128)S(1)} %constant_dynamic-update-slice_fusion.refs_0_, f32[608,128]{1,0:T(8,128)S(1)} %collective-permute-done.20.refs_1_, f32[608,128]{1,0:T(8,128)S(1)} %collective-permute-done.21.refs_2_, ...), custom_call_target="tpu_custom_call" | custom-call | bytes 16777216 | tf_op jit(solution)/shard_map/pallas_call | solution.py:337
  78.3 1.3 %shard_map.152 = (f32[400,1536]{1,0:T(8,128)}, f32[400,256]{1,0:T(8,128)}, f32[1,256]{1,0:T(1,128)}) custom-call(f32[400,1536]{1,0:T(8,128)} %get-tuple-element.98.refs_0_, f32[608,128]{1,0:T(8,128)S(1)} %collective-permute-done.23.refs_1_, f32[608,128]{1,0:T(8,128)S(1)} %collective-permute-done.24.refs_2_, ...), custom_call_target="tpu_custom_call", output_to_operand_aliasing={{0}: (0, {})} | custom-call | bytes 16777216 | tf_op jit(solution)/shard_map/pallas_call | solution.py:337
  (54 shorter events, 10.4 us)
Async XLA Ops:
  8.6 4.9 %collective-permute-start.1 = (f32[608,128]{1,0:T(8,128)S(1)}, f32[608,128]{1,0:T(8,128)S(1)}, u32[]{:S(2)}, u32[]{:S(2)}) collective-permute-start(f32[608,128]{1,0:T(8,128)S(1)} %get-tuple-element.59), channel_id=1, source_target_pairs={{0,1},{1,0},{2,3},{3,2},{4,5},{5,4},{6,7},{7,6},{8,9},{9,8},{10,11... | collective-permute-start | bytes 933896 | tf_op jit(solution)/shard_map/ppermute | solution.py:79
  12.4 8.6 %collective-permute-start = (f32[608,128]{1,0:T(8,128)S(1)}, f32[608,128]{1,0:T(8,128)S(1)}, u32[]{:S(2)}, u32[]{:S(2)}) collective-permute-start(f32[608,128]{1,0:T(8,128)S(1)} %get-tuple-element.57), channel_id=1, source_target_pairs={{0,1},{1,0},{2,3},{3,2},{4,5},{5,4},{6,7},{7,6},{8,9},{9,8},{10,11... | collective-permute-start | bytes 933896 | tf_op jit(solution)/shard_map/ppermute | solution.py:79
  13.5 7.7 %collective-permute-start.2 = (f32[608,128]{1,0:T(8,128)S(1)}, f32[608,128]{1,0:T(8,128)S(1)}, u32[]{:S(2)}, u32[]{:S(2)}) collective-permute-start(f32[608,128]{1,0:T(8,128)S(1)} %add.46), channel_id=1, source_target_pairs={{0,128},{1,3},{2,130},{3,1},{4,132},{5,7},{6,134},{7,5},{8,136},{9... | collective-permute-start | bytes 933896 | tf_op jit(solution)/shard_map/ppermute | solution.py:79
  14.8 9.7 %collective-permute-start.4 = (f32[608,128]{1,0:T(8,128)S(1)}, f32[608,128]{1,0:T(8,128)S(1)}, u32[]{:S(2)}, u32[]{:S(2)}) collective-permute-start(f32[608,128]{1,0:T(8,128)S(1)} %add.48), channel_id=1, source_target_pairs={{0,64},{1,33},{2,66},{3,35},{4,68},{5,37},{6,70},{7,39},{8,72},{9,... | collective-permute-start | bytes 933896 | tf_op jit(solution)/shard_map/ppermute | solution.py:79
  15.4 9.1 %collective-permute-start.6 = (f32[608,128]{1,0:T(8,128)S(1)}, f32[608,128]{1,0:T(8,128)S(1)}, u32[]{:S(2)}, u32[]{:S(2)}) collective-permute-start(f32[608,128]{1,0:T(8,128)S(1)} %add.50), channel_id=1, source_target_pairs={{0,192},{1,35},{2,194},{3,33},{4,196},{5,39},{6,198},{7,37},{8,200... | collective-permute-start | bytes 933896 | tf_op jit(solution)/shard_map/ppermute | solution.py:79
  19.7 13.4 %collective-permute-start.11 = (f32[800,128]{1,0:T(8,128)S(1)}, f32[800,128]{1,0:T(8,128)S(1)}, u32[]{:S(2)}, u32[]{:S(2)}) collective-permute-start(f32[800,128]{1,0:T(8,128)S(1)} %get-tuple-element.78), channel_id=1, source_target_pairs={{0,1},{1,0},{2,3},{3,2},{4,5},{5,4},{6,7},{7,6},{8,9},{9,8},{10,11... | collective-permute-start | bytes 1228808 | tf_op jit(solution)/shard_map/ppermute | solution.py:79
  24.6 4.8 %collective-permute-start.7 = (f32[152,128]{1,0:T(8,128)S(1)}, f32[152,128]{1,0:T(8,128)S(1)}, u32[]{:S(2)}, u32[]{:S(2)}) collective-permute-start(f32[152,128]{1,0:T(8,128)S(1)} %get-tuple-element.103), channel_id=1, source_target_pairs={{0,2},{1,129},{2,0},{3,131},{4,6},{5,133},{6,4},{7,135},{8,10},{9,... | collective-permute-start | bytes 233480 | tf_op jit(solution)/shard_map/ppermute | solution.py:79
  26.0 3.4 %collective-permute-start.9 = (f32[152,128]{1,0:T(8,128)S(1)}, f32[152,128]{1,0:T(8,128)S(1)}, u32[]{:S(2)}, u32[]{:S(2)}) collective-permute-start(f32[152,128]{1,0:T(8,128)S(1)} %get-tuple-element.104), channel_id=1, source_target_pairs={{0,34},{1,193},{2,32},{3,195},{4,38},{5,197},{6,36},{7,199},{8,42}... | collective-permute-start | bytes 233480 | tf_op jit(solution)/shard_map/ppermute | solution.py:79
  26.9 4.6 %collective-permute-start.8 = (f32[152,128]{1,0:T(8,128)S(1)}, f32[152,128]{1,0:T(8,128)S(1)}, u32[]{:S(2)}, u32[]{:S(2)}) collective-permute-start(f32[152,128]{1,0:T(8,128)S(1)} %get-tuple-element.105), channel_id=1, source_target_pairs={{0,32},{1,65},{2,34},{3,67},{4,36},{5,69},{6,38},{7,71},{8,40},{9,... | collective-permute-start | bytes 233480 | tf_op jit(solution)/shard_map/ppermute | solution.py:79
  31.5 3.4 %collective-permute-start.10 = (f32[152,128]{1,0:T(8,128)S(1)}, f32[152,128]{1,0:T(8,128)S(1)}, u32[]{:S(2)}, u32[]{:S(2)}) collective-permute-start(f32[152,128]{1,0:T(8,128)S(1)} %fusion.1), channel_id=1, source_target_pairs={{0,4},{1,5},{2,6},{3,7},{4,0},{5,1},{6,2},{7,3},{8,12},{9,13},{10,... | collective-permute-start | bytes 233480 | tf_op jit(solution)/shard_map/ppermute | solution.py:79
  34.9 19.8 %collective-permute-start.17 = (f32[800,128]{1,0:T(8,128)S(1)}, f32[800,128]{1,0:T(8,128)S(1)}, u32[]{:S(2)}, u32[]{:S(2)}) collective-permute-start(f32[800,128]{1,0:T(8,128)S(1)} %add.56.kept_ref), channel_id=1, source_target_pairs={{0,2},{1,3},{2,0},{3,1},{4,6},{5,7},{6,4},{7,5},{8,10},{9,11},{10,... | collective-permute-start | bytes 1228808 | tf_op jit(solution)/shard_map/ppermute | solution.py:79
  36.9 8.2 %collective-permute-start.14 = (f32[152,128]{1,0:T(8,128)S(1)}, f32[152,128]{1,0:T(8,128)S(1)}, u32[]{:S(2)}, u32[]{:S(2)}) collective-permute-start(f32[152,128]{1,0:T(8,128)S(1)} %add.55), channel_id=1, source_target_pairs={{0,24},{1,25},{2,26},{3,27},{4,12},{5,13},{6,14},{7,15},{8,0},{9,1... | collective-permute-start | bytes 233480 | tf_op jit(solution)/shard_map/ppermute | solution.py:79
  42.8 5.2 %collective-permute-start.13 = (f32[152,128]{1,0:T(8,128)S(1)}, f32[152,128]{1,0:T(8,128)S(1)}, u32[]{:S(2)}, u32[]{:S(2)}) collective-permute-start(f32[152,128]{1,0:T(8,128)S(1)} %add.55), channel_id=1, source_target_pairs={{0,28},{1,29},{2,30},{3,31},{4,8},{5,9},{6,10},{7,11},{8,4},{9,5},... | collective-permute-start | bytes 233480 | tf_op jit(solution)/shard_map/ppermute | solution.py:79
  42.8 7.0 %collective-permute-start.12 = (f32[152,128]{1,0:T(8,128)S(1)}, f32[152,128]{1,0:T(8,128)S(1)}, u32[]{:S(2)}, u32[]{:S(2)}) collective-permute-start(f32[152,128]{1,0:T(8,128)S(1)} %add.55), channel_id=1, source_target_pairs={{0,20},{1,21},{2,22},{3,23},{4,16},{5,17},{6,18},{7,19},{8,28},{9,... | collective-permute-start | bytes 233480 | tf_op jit(solution)/shard_map/ppermute | solution.py:79
  49.8 4.9 %collective-permute-start.16 = (f32[152,128]{1,0:T(8,128)S(1)}, f32[152,128]{1,0:T(8,128)S(1)}, u32[]{:S(2)}, u32[]{:S(2)}) collective-permute-start(f32[152,128]{1,0:T(8,128)S(1)} %add_add_fusion.1), channel_id=1, source_target_pairs={{0,2},{1,129},{2,0},{3,131},{4,6},{5,133},{6,4},{7,135},{8,10},{9,... | collective-permute-start | bytes 233480 | tf_op jit(solution)/shard_map/ppermute | solution.py:79
  49.9 6.1 %collective-permute-start.18 = (f32[152,128]{1,0:T(8,128)S(1)}, f32[152,128]{1,0:T(8,128)S(1)}, u32[]{:S(2)}, u32[]{:S(2)}) collective-permute-start(f32[152,128]{1,0:T(8,128)S(1)} %add_add_fusion.1), channel_id=1, source_target_pairs={{0,32},{1,65},{2,34},{3,67},{4,36},{5,69},{6,38},{7,71},{8,40},{9,... | collective-permute-start | bytes 233480 | tf_op jit(solution)/shard_map/ppermute | solution.py:79
  49.9 6.1 %collective-permute-start.15 = (f32[152,128]{1,0:T(8,128)S(1)}, f32[152,128]{1,0:T(8,128)S(1)}, u32[]{:S(2)}, u32[]{:S(2)}) collective-permute-start(f32[152,128]{1,0:T(8,128)S(1)} %add_add_fusion.1), channel_id=1, source_target_pairs={{0,34},{1,193},{2,32},{3,195},{4,38},{5,197},{6,36},{7,199},{8,42}... | collective-permute-start | bytes 233480 | tf_op jit(solution)/shard_map/ppermute | solution.py:79
  56.0 6.8 %collective-permute-start.19 = (f32[408,128]{1,0:T(8,128)S(1)}, f32[408,128]{1,0:T(8,128)S(1)}, u32[]{:S(2)}, u32[]{:S(2)}) collective-permute-start(f32[408,128]{1,0:T(8,128)S(1)} %get-tuple-element.90.refs_4_), channel_id=1, source_target_pairs={{0,1},{1,0},{2,3},{3,2},{4,5},{5,4},{6,7},{7,6},{8,9},{9,8},{10,11... | collective-permute-start | bytes 626696 | tf_op jit(solution)/shard_map/ppermute | solution.py:79
  62.9 11.2 %collective-permute-start.22 = (f32[608,128]{1,0:T(8,128)S(1)}, f32[608,128]{1,0:T(8,128)S(1)}, u32[]{:S(2)}, u32[]{:S(2)}) collective-permute-start(f32[608,128]{1,0:T(8,128)S(1)} %constant_dynamic-update-slice_fusion.refs_0_), channel_id=1, source_target_pairs={{0,64},{1,33},{2,66},{3,35},{4,68},{5,37},{6,70},{7,39},{8,72},{9,... | collective-permute-start | bytes 933896 | tf_op jit(solution)/shard_map/ppermute | solution.py:79
  63.0 12.0 %collective-permute-start.21 = (f32[608,128]{1,0:T(8,128)S(1)}, f32[608,128]{1,0:T(8,128)S(1)}, u32[]{:S(2)}, u32[]{:S(2)}) collective-permute-start(f32[608,128]{1,0:T(8,128)S(1)} %constant_dynamic-update-slice_fusion.refs_0_), channel_id=1, source_target_pairs={{0,128},{1,3},{2,130},{3,1},{4,132},{5,7},{6,134},{7,5},{8,136},{9... | collective-permute-start | bytes 933896 | tf_op jit(solution)/shard_map/ppermute | solution.py:79
  67.1 9.1 %collective-permute-start.20 = (f32[608,128]{1,0:T(8,128)S(1)}, f32[608,128]{1,0:T(8,128)S(1)}, u32[]{:S(2)}, u32[]{:S(2)}) collective-permute-start(f32[608,128]{1,0:T(8,128)S(1)} %constant_dynamic-update-slice_fusion.refs_0_), channel_id=1, source_target_pairs={{0,192},{1,35},{2,194},{3,33},{4,196},{5,39},{6,198},{7,37},{8,200... | collective-permute-start | bytes 933896 | tf_op jit(solution)/shard_map/ppermute | solution.py:79
  67.1 9.7 %collective-permute-start.27 = (f32[408,128]{1,0:T(8,128)S(1)}, f32[408,128]{1,0:T(8,128)S(1)}, u32[]{:S(2)}, u32[]{:S(2)}) collective-permute-start(f32[408,128]{1,0:T(8,128)S(1)} %get-tuple-element.99), channel_id=1, source_target_pairs={{0,252},{1,253},{2,254},{3,255},{4,0},{5,1},{6,2},{7,3},{8,4},{9,5... | collective-permute-start | bytes 626696 | tf_op jit(solution)/shard_map/ppermute | solution.py:112
  74.1 4.2 %collective-permute-start.23 = (f32[608,128]{1,0:T(8,128)S(1)}, f32[608,128]{1,0:T(8,128)S(1)}, u32[]{:S(2)}, u32[]{:S(2)}) collective-permute-start(f32[608,128]{1,0:T(8,128)S(1)} %constant_dynamic-update-slice_fusion.refs_0_), channel_id=1, source_target_pairs={{0,1},{1,0},{2,3},{3,2},{4,5},{5,4},{6,7},{7,6},{8,9},{9,8},{10,11... | collective-permute-start | bytes 933896 | tf_op jit(solution)/shard_map/ppermute | solution.py:79
  74.1 4.2 %collective-permute-start.26 = (f32[608,128]{1,0:T(8,128)S(1)}, f32[608,128]{1,0:T(8,128)S(1)}, u32[]{:S(2)}, u32[]{:S(2)}) collective-permute-start(f32[608,128]{1,0:T(8,128)S(1)} %collective-permute-done.22.refs_3_), channel_id=1, source_target_pairs={{0,1},{1,0},{2,3},{3,2},{4,5},{5,4},{6,7},{7,6},{8,9},{9,8},{10,11... | collective-permute-start | bytes 933896 | tf_op jit(solution)/shard_map/ppermute | solution.py:79
  (5 other events, 13.1 us)

commit v5 on v4

--- a/solution.py
+++ b/solution.py
@@ -161,8 +161,6 @@
     negatives = negl_ref.shape[1]
     for fetch in fetches[:5]:
         fetch.wait()
-    count_right = jnp.sum(one_hot(negr_ref[...], rows), axis=1, keepdims=True)
-    count_left = jnp.sum(one_hot(negl_ref[...], rows), axis=1, keepdims=True)
     pick_src = one_hot(src_ref[...], rows).astype(BF16)
     pick_dst = one_hot(dst_ref[...], rows).astype(BF16)
     pick_rel = one_hot(rid_ref[...], types).astype(BF16)
@@ -176,6 +174,8 @@
     right_parts, right_rows = parts(right), parts(right.T)
     fetches[7].wait()
     weight = dot_picked(near_rel_ref[...], pick_rel, NN)
+    count_right = jnp.sum(one_hot(negr_ref[...], rows), axis=1, keepdims=True)
+    count_left = jnp.sum(one_hot(negl_ref[...], rows), axis=1, keepdims=True)
     s, t, w = halves(source), halves(target), halves(weight)
     q = jnp.concatenate(product(s, w), axis=0)
     p = jnp.concatenate(adjoint(t, w), axis=0)

time: 80.6 us -> 80.5 us (level)
  no operation moved by 1% of the time
where the time goes in v5:
time: 80.5 us; the launch traced here: 79.7 us
  starting transfers between devices  45.5 us (57%)
  waiting for transfers between devices  18.2 us (23%)
  Pallas kernels  14.1 us (18%)
  between operations  1.62 us (2%)
    ppermute x28, starting transfers between devices, send(): return lax.ppermute(value, ('dom', 'rep'), pairs)  38.5 us
    ppermute x28, waiting for transfers between devices, send(): return lax.ppermute(value, ('dom', 'rep'), pairs)  17.5 us
    pallas_call x5, Pallas kernels, call(): pl.pallas_call(kernel, out_shape=[pltpu.VMEM(shape[0], shape[1]) if isins...  11.4 us
    ppermute x1, starting transfers between devices, to_bucket_before(): return lax.ppermute(value, ('dom', 'rep'), pairs)  6.99 us
    pallas_call x2, Pallas kernels, put(): pl.pallas_call(functools.partial(place_kernel, mine), out_shape=[jax.Shap...  2.69 us
  transfers between devices with their start and end apart: 29, of which 12 were waited for; matrix products, arithmetic and copies ran while one was open for 0% of the time, Pallas kernels for 7%

profile of v5, /device:TPU:1, one launch (start us, length us, event | category | flops | bytes accessed | tf_op | source)
XLA Modules:
  0.0 79.7 jit_solution(3092240173195022155)
XLA Ops:
  1.3 6.3 %shard_map.146 = (f32[400,512]{1,0:T(8,128)S(1)}, bf16[1536,512]{1,0:T(8,128)(2,1)S(1)}, f32[400,512]{1,0:T(8,128)S(1)}, f32[400,512]{1,0:T(8,128)S(1)}, f32[256...) custom-call(s32[1]{0:T(128)S(6)} %copy.21.counts_ref, ...), custom_call_target="tpu_custom_call" | custom-call | bytes 16777216 | tf_op jit(solution)/shard_map/pallas_call | solution.py:252
  8.5 3.3 %collective-permute-start.1 = (f32[608,128]{1,0:T(8,128)S(1)}, f32[608,128]{1,0:T(8,128)S(1)}, u32[]{:S(2)}, u32[]{:S(2)}) collective-permute-start(f32[608,128]{1,0:T(8,128)S(1)} %get-tuple-element.59), channel_id=1, source_target_pairs={{0,1},{1,0},{2,3},{3,2},{4,5},{5,4},{6,7},{7,6},{8,9},{9,8},{10,11... | collective-permute-start | bytes 933896 | tf_op jit(solution)/shard_map/ppermute | solution.py:79
  15.2 2.4 %collective-permute-start.6 = (f32[608,128]{1,0:T(8,128)S(1)}, f32[608,128]{1,0:T(8,128)S(1)}, u32[]{:S(2)}, u32[]{:S(2)}) collective-permute-start(f32[608,128]{1,0:T(8,128)S(1)} %add.50), channel_id=1, source_target_pairs={{0,192},{1,35},{2,194},{3,33},{4,196},{5,39},{6,198},{7,37},{8,200... | collective-permute-start | bytes 933896 | tf_op jit(solution)/shard_map/ppermute | solution.py:79
  17.6 2.0 %shard_map.149 = (f32[800,128]{1,0:T(8,128)S(1)}, f32[800,128]{1,0:T(8,128)S(1)}) custom-call(s32[1,512]{1,0:T(1,128)} %src_ref.1, s32[1,512]{1,0:T(1,128)} %dst_ref.1, f32[400,512]{1,0:T(8,128)S(1)} %get-tuple-element.71.q_ref, f32[400,512]{1,0:T(8,128)S(1)} %get-tuple-element.72.p_ref, f32[256,512]{1,0:T(8,128)S(1)} %get-tuple-element.73.gr_ref, ...), custom_call_target="tpu_custom_call" | custom-call | bytes 16777216 | tf_op jit(solution)/shard_map/pallas_call | solution.py:252
  19.5 1.4 %collective-permute-start.11 = (f32[800,128]{1,0:T(8,128)S(1)}, f32[800,128]{1,0:T(8,128)S(1)}, u32[]{:S(2)}, u32[]{:S(2)}) collective-permute-start(f32[800,128]{1,0:T(8,128)S(1)} %get-tuple-element.78), channel_id=1, source_target_pairs={{0,1},{1,0},{2,3},{3,2},{4,5},{5,4},{6,7},{7,6},{8,9},{9,8},{10,11... | collective-permute-start | bytes 1228808 | tf_op jit(solution)/shard_map/ppermute | solution.py:79
  21.1 3.3 %collective-permute-done.4 = f32[608,128]{1,0:T(8,128)S(1)} collective-permute-done((f32[608,128]{1,0:T(8,128)S(1)}, f32[608,128]{1,0:T(8,128)S(1)}, u32[]{:S(2)}, u32[]{:S(2)}) %collective-permute-start.4) | collective-permute-done | bytes 311328 | tf_op jit(solution)/shard_map/ppermute | solution.py:79
  24.5 1.4 %collective-permute-start.7 = (f32[152,128]{1,0:T(8,128)S(1)}, f32[152,128]{1,0:T(8,128)S(1)}, u32[]{:S(2)}, u32[]{:S(2)}) collective-permute-start(f32[152,128]{1,0:T(8,128)S(1)} %get-tuple-element.103), channel_id=1, source_target_pairs={{0,2},{1,129},{2,0},{3,131},{4,6},{5,133},{6,4},{7,135},{8,10},{9,... | collective-permute-start | bytes 233480 | tf_op jit(solution)/shard_map/ppermute | solution.py:79
  27.4 1.9 %collective-permute-done.7 = f32[152,128]{1,0:T(8,128)S(1)} collective-permute-done((f32[152,128]{1,0:T(8,128)S(1)}, f32[152,128]{1,0:T(8,128)S(1)}, u32[]{:S(2)}, u32[]{:S(2)}) %collective-permute-start.7) | collective-permute-done | bytes 77856 | tf_op jit(solution)/shard_map/ppermute | solution.py:79
  29.3 2.0 %collective-permute-done.8 = f32[152,128]{1,0:T(8,128)S(1)} collective-permute-done((f32[152,128]{1,0:T(8,128)S(1)}, f32[152,128]{1,0:T(8,128)S(1)}, u32[]{:S(2)}, u32[]{:S(2)}) %collective-permute-start.8) | collective-permute-done | bytes 77856 | tf_op jit(solution)/shard_map/ppermute | solution.py:79
  31.4 1.6 %collective-permute-start.10 = (f32[152,128]{1,0:T(8,128)S(1)}, f32[152,128]{1,0:T(8,128)S(1)}, u32[]{:S(2)}, u32[]{:S(2)}) collective-permute-start(f32[152,128]{1,0:T(8,128)S(1)} %fusion.1), channel_id=1, source_target_pairs={{0,4},{1,5},{2,6},{3,7},{4,0},{5,1},{6,2},{7,3},{8,12},{9,13},{10,... | collective-permute-start | bytes 233480 | tf_op jit(solution)/shard_map/ppermute | solution.py:79
  33.1 1.7 %collective-permute-done.10 = f32[152,128]{1,0:T(8,128)S(1)} collective-permute-done((f32[152,128]{1,0:T(8,128)S(1)}, f32[152,128]{1,0:T(8,128)S(1)}, u32[]{:S(2)}, u32[]{:S(2)}) %collective-permute-start.10) | collective-permute-done | bytes 77856 | tf_op jit(solution)/shard_map/ppermute | solution.py:79
  34.8 2.0 %collective-permute-start.17 = (f32[800,128]{1,0:T(8,128)S(1)}, f32[800,128]{1,0:T(8,128)S(1)}, u32[]{:S(2)}, u32[]{:S(2)}) collective-permute-start(f32[800,128]{1,0:T(8,128)S(1)} %add.56.kept_ref), channel_id=1, source_target_pairs={{0,2},{1,3},{2,0},{3,1},{4,6},{5,7},{6,4},{7,5},{8,10},{9,11},{10,... | collective-permute-start | bytes 1228808 | tf_op jit(solution)/shard_map/ppermute | solution.py:79
  36.8 5.8 %collective-permute-start.14 = (f32[152,128]{1,0:T(8,128)S(1)}, f32[152,128]{1,0:T(8,128)S(1)}, u32[]{:S(2)}, u32[]{:S(2)}) collective-permute-start(f32[152,128]{1,0:T(8,128)S(1)} %add.55), channel_id=1, source_target_pairs={{0,24},{1,25},{2,26},{3,27},{4,12},{5,13},{6,14},{7,15},{8,0},{9,1... | collective-permute-start | bytes 233480 | tf_op jit(solution)/shard_map/ppermute | solution.py:79
  42.6 2.4 %collective-permute-start.12 = (f32[152,128]{1,0:T(8,128)S(1)}, f32[152,128]{1,0:T(8,128)S(1)}, u32[]{:S(2)}, u32[]{:S(2)}) collective-permute-start(f32[152,128]{1,0:T(8,128)S(1)} %add.55), channel_id=1, source_target_pairs={{0,20},{1,21},{2,22},{3,23},{4,16},{5,17},{6,18},{7,19},{8,28},{9,... | collective-permute-start | bytes 233480 | tf_op jit(solution)/shard_map/ppermute | solution.py:79
  45.0 2.8 %collective-permute-done.13 = f32[152,128]{1,0:T(8,128)S(1)} collective-permute-done((f32[152,128]{1,0:T(8,128)S(1)}, f32[152,128]{1,0:T(8,128)S(1)}, u32[]{:S(2)}, u32[]{:S(2)}) %collective-permute-start.13) | collective-permute-done | bytes 77856 | tf_op jit(solution)/shard_map/ppermute | solution.py:79
  47.8 1.8 %collective-permute-done.12 = f32[152,128]{1,0:T(8,128)S(1)} collective-permute-done((f32[152,128]{1,0:T(8,128)S(1)}, f32[152,128]{1,0:T(8,128)S(1)}, u32[]{:S(2)}, u32[]{:S(2)}) %collective-permute-start.12) | collective-permute-done | bytes 77856 | tf_op jit(solution)/shard_map/ppermute | solution.py:79
  49.8 2.7 %collective-permute-start.15 = (f32[152,128]{1,0:T(8,128)S(1)}, f32[152,128]{1,0:T(8,128)S(1)}, u32[]{:S(2)}, u32[]{:S(2)}) collective-permute-start(f32[152,128]{1,0:T(8,128)S(1)} %add_add_fusion.1), channel_id=1, source_target_pairs={{0,34},{1,193},{2,32},{3,195},{4,38},{5,197},{6,36},{7,199},{8,42}... | collective-permute-start | bytes 233480 | tf_op jit(solution)/shard_map/ppermute | solution.py:79
  52.5 2.1 %collective-permute-done.16 = f32[152,128]{1,0:T(8,128)S(1)} collective-permute-done((f32[152,128]{1,0:T(8,128)S(1)}, f32[152,128]{1,0:T(8,128)S(1)}, u32[]{:S(2)}, u32[]{:S(2)}) %collective-permute-start.16) | collective-permute-done | bytes 77856 | tf_op jit(solution)/shard_map/ppermute | solution.py:79
  54.6 1.3 %shard_map.150 = (f32[408,128]{1,0:T(8,128)S(1)}, f32[408,128]{1,0:T(8,128)S(1)}) custom-call(f32[800,128]{1,0:T(8,128)S(1)} %add.56.kept_ref, f32[800,128]{1,0:T(8,128)S(1)} %collective-permute-done.17.got_ref, f32[400,256]{1,0:T(8,128)} %bitcast.15, f32[400,256]{1,0:T(8,128)} %bitcast.17, f32[1,256]{1,0:T(1,128)} %bitcast.20, f32[1,256]{1,0:T(1,128)} %bitcast.21), custom_call_target="tpu_custom_call" | custom-call | tf_op jit(solution)/shard_map/pallas_call | solution.py:252
  55.9 5.7 %collective-permute-start.19 = (f32[408,128]{1,0:T(8,128)S(1)}, f32[408,128]{1,0:T(8,128)S(1)}, u32[]{:S(2)}, u32[]{:S(2)}) collective-permute-start(f32[408,128]{1,0:T(8,128)S(1)} %get-tuple-element.90.refs_4_), channel_id=1, source_target_pairs={{0,1},{1,0},{2,3},{3,2},{4,5},{5,4},{6,7},{7,6},{8,9},{9,8},{10,11... | collective-permute-start | bytes 626696 | tf_op jit(solution)/shard_map/ppermute | solution.py:79
  62.9 4.1 %collective-permute-start.21 = (f32[608,128]{1,0:T(8,128)S(1)}, f32[608,128]{1,0:T(8,128)S(1)}, u32[]{:S(2)}, u32[]{:S(2)}) collective-permute-start(f32[608,128]{1,0:T(8,128)S(1)} %constant_dynamic-update-slice_fusion.refs_0_), channel_id=1, source_target_pairs={{0,128},{1,3},{2,130},{3,1},{4,132},{5,7},{6,134},{7,5},{8,136},{9... | collective-permute-start | bytes 933896 | tf_op jit(solution)/shard_map/ppermute | solution.py:79
  67.0 7.0 %collective-permute-start.27 = (f32[408,128]{1,0:T(8,128)S(1)}, f32[408,128]{1,0:T(8,128)S(1)}, u32[]{:S(2)}, u32[]{:S(2)}) collective-permute-start(f32[408,128]{1,0:T(8,128)S(1)} %get-tuple-element.99), channel_id=1, source_target_pairs={{0,252},{1,253},{2,254},{3,255},{4,0},{5,1},{6,2},{7,3},{8,4},{9,5... | collective-permute-start | bytes 626696 | tf_op jit(solution)/shard_map/ppermute | solution.py:112
  76.7 1.3 %shard_map.151 = (f32[400,1536]{1,0:T(8,128)}, f32[400,256]{1,0:T(8,128)}, f32[1,256]{1,0:T(1,128)}) custom-call(f32[608,128]{1,0:T(8,128)S(1)} %constant_dynamic-update-slice_fusion.refs_0_, f32[608,128]{1,0:T(8,128)S(1)} %collective-permute-done.20.refs_1_, f32[608,128]{1,0:T(8,128)S(1)} %collective-permute-done.21.refs_2_, ...), custom_call_target="tpu_custom_call" | custom-call | bytes 16777216 | tf_op jit(solution)/shard_map/pallas_call | solution.py:337
  78.2 1.3 %shard_map.152 = (f32[400,1536]{1,0:T(8,128)}, f32[400,256]{1,0:T(8,128)}, f32[1,256]{1,0:T(1,128)}) custom-call(f32[400,1536]{1,0:T(8,128)} %get-tuple-element.98.refs_0_, f32[608,128]{1,0:T(8,128)S(1)} %collective-permute-done.23.refs_1_, f32[608,128]{1,0:T(8,128)S(1)} %collective-permute-done.24.refs_2_, ...), custom_call_target="tpu_custom_call", output_to_operand_aliasing={{0}: (0, {})} | custom-call | bytes 16777216 | tf_op jit(solution)/shard_map/pallas_call | solution.py:337
  (54 shorter events, 10.4 us)
Async XLA Ops:
  8.5 4.9 %collective-permute-start.1 = (f32[608,128]{1,0:T(8,128)S(1)}, f32[608,128]{1,0:T(8,128)S(1)}, u32[]{:S(2)}, u32[]{:S(2)}) collective-permute-start(f32[608,128]{1,0:T(8,128)S(1)} %get-tuple-element.59), channel_id=1, source_target_pairs={{0,1},{1,0},{2,3},{3,2},{4,5},{5,4},{6,7},{7,6},{8,9},{9,8},{10,11... | collective-permute-start | bytes 933896 | tf_op jit(solution)/shard_map/ppermute | solution.py:79
  12.3 8.5 %collective-permute-start = (f32[608,128]{1,0:T(8,128)S(1)}, f32[608,128]{1,0:T(8,128)S(1)}, u32[]{:S(2)}, u32[]{:S(2)}) collective-permute-start(f32[608,128]{1,0:T(8,128)S(1)} %get-tuple-element.57), channel_id=1, source_target_pairs={{0,1},{1,0},{2,3},{3,2},{4,5},{5,4},{6,7},{7,6},{8,9},{9,8},{10,11... | collective-permute-start | bytes 933896 | tf_op jit(solution)/shard_map/ppermute | solution.py:79
  13.4 7.7 %collective-permute-start.2 = (f32[608,128]{1,0:T(8,128)S(1)}, f32[608,128]{1,0:T(8,128)S(1)}, u32[]{:S(2)}, u32[]{:S(2)}) collective-permute-start(f32[608,128]{1,0:T(8,128)S(1)} %add.46), channel_id=1, source_target_pairs={{0,128},{1,3},{2,130},{3,1},{4,132},{5,7},{6,134},{7,5},{8,136},{9... | collective-permute-start | bytes 933896 | tf_op jit(solution)/shard_map/ppermute | solution.py:79
  14.7 9.7 %collective-permute-start.4 = (f32[608,128]{1,0:T(8,128)S(1)}, f32[608,128]{1,0:T(8,128)S(1)}, u32[]{:S(2)}, u32[]{:S(2)}) collective-permute-start(f32[608,128]{1,0:T(8,128)S(1)} %add.48), channel_id=1, source_target_pairs={{0,64},{1,33},{2,66},{3,35},{4,68},{5,37},{6,70},{7,39},{8,72},{9,... | collective-permute-start | bytes 933896 | tf_op jit(solution)/shard_map/ppermute | solution.py:79
  15.2 9.2 %collective-permute-start.6 = (f32[608,128]{1,0:T(8,128)S(1)}, f32[608,128]{1,0:T(8,128)S(1)}, u32[]{:S(2)}, u32[]{:S(2)}) collective-permute-start(f32[608,128]{1,0:T(8,128)S(1)} %add.50), channel_id=1, source_target_pairs={{0,192},{1,35},{2,194},{3,33},{4,196},{5,39},{6,198},{7,37},{8,200... | collective-permute-start | bytes 933896 | tf_op jit(solution)/shard_map/ppermute | solution.py:79
  19.5 13.5 %collective-permute-start.11 = (f32[800,128]{1,0:T(8,128)S(1)}, f32[800,128]{1,0:T(8,128)S(1)}, u32[]{:S(2)}, u32[]{:S(2)}) collective-permute-start(f32[800,128]{1,0:T(8,128)S(1)} %get-tuple-element.78), channel_id=1, source_target_pairs={{0,1},{1,0},{2,3},{3,2},{4,5},{5,4},{6,7},{7,6},{8,9},{9,8},{10,11... | collective-permute-start | bytes 1228808 | tf_op jit(solution)/shard_map/ppermute | solution.py:79
  24.5 4.8 %collective-permute-start.7 = (f32[152,128]{1,0:T(8,128)S(1)}, f32[152,128]{1,0:T(8,128)S(1)}, u32[]{:S(2)}, u32[]{:S(2)}) collective-permute-start(f32[152,128]{1,0:T(8,128)S(1)} %get-tuple-element.103), channel_id=1, source_target_pairs={{0,2},{1,129},{2,0},{3,131},{4,6},{5,133},{6,4},{7,135},{8,10},{9,... | collective-permute-start | bytes 233480 | tf_op jit(solution)/shard_map/ppermute | solution.py:79
  25.9 3.4 %collective-permute-start.9 = (f32[152,128]{1,0:T(8,128)S(1)}, f32[152,128]{1,0:T(8,128)S(1)}, u32[]{:S(2)}, u32[]{:S(2)}) collective-permute-start(f32[152,128]{1,0:T(8,128)S(1)} %get-tuple-element.104), channel_id=1, source_target_pairs={{0,34},{1,193},{2,32},{3,195},{4,38},{5,197},{6,36},{7,199},{8,42}... | collective-permute-start | bytes 233480 | tf_op jit(solution)/shard_map/ppermute | solution.py:79
  26.8 4.6 %collective-permute-start.8 = (f32[152,128]{1,0:T(8,128)S(1)}, f32[152,128]{1,0:T(8,128)S(1)}, u32[]{:S(2)}, u32[]{:S(2)}) collective-permute-start(f32[152,128]{1,0:T(8,128)S(1)} %get-tuple-element.105), channel_id=1, source_target_pairs={{0,32},{1,65},{2,34},{3,67},{4,36},{5,69},{6,38},{7,71},{8,40},{9,... | collective-permute-start | bytes 233480 | tf_op jit(solution)/shard_map/ppermute | solution.py:79
  31.4 3.4 %collective-permute-start.10 = (f32[152,128]{1,0:T(8,128)S(1)}, f32[152,128]{1,0:T(8,128)S(1)}, u32[]{:S(2)}, u32[]{:S(2)}) collective-permute-start(f32[152,128]{1,0:T(8,128)S(1)} %fusion.1), channel_id=1, source_target_pairs={{0,4},{1,5},{2,6},{3,7},{4,0},{5,1},{6,2},{7,3},{8,12},{9,13},{10,... | collective-permute-start | bytes 233480 | tf_op jit(solution)/shard_map/ppermute | solution.py:79
  34.8 19.8 %collective-permute-start.17 = (f32[800,128]{1,0:T(8,128)S(1)}, f32[800,128]{1,0:T(8,128)S(1)}, u32[]{:S(2)}, u32[]{:S(2)}) collective-permute-start(f32[800,128]{1,0:T(8,128)S(1)} %add.56.kept_ref), channel_id=1, source_target_pairs={{0,2},{1,3},{2,0},{3,1},{4,6},{5,7},{6,4},{7,5},{8,10},{9,11},{10,... | collective-permute-start | bytes 1228808 | tf_op jit(solution)/shard_map/ppermute | solution.py:79
  36.8 8.2 %collective-permute-start.14 = (f32[152,128]{1,0:T(8,128)S(1)}, f32[152,128]{1,0:T(8,128)S(1)}, u32[]{:S(2)}, u32[]{:S(2)}) collective-permute-start(f32[152,128]{1,0:T(8,128)S(1)} %add.55), channel_id=1, source_target_pairs={{0,24},{1,25},{2,26},{3,27},{4,12},{5,13},{6,14},{7,15},{8,0},{9,1... | collective-permute-start | bytes 233480 | tf_op jit(solution)/shard_map/ppermute | solution.py:79
  42.6 5.2 %collective-permute-start.13 = (f32[152,128]{1,0:T(8,128)S(1)}, f32[152,128]{1,0:T(8,128)S(1)}, u32[]{:S(2)}, u32[]{:S(2)}) collective-permute-start(f32[152,128]{1,0:T(8,128)S(1)} %add.55), channel_id=1, source_target_pairs={{0,28},{1,29},{2,30},{3,31},{4,8},{5,9},{6,10},{7,11},{8,4},{9,5},... | collective-permute-start | bytes 233480 | tf_op jit(solution)/shard_map/ppermute | solution.py:79
  42.6 7.0 %collective-permute-start.12 = (f32[152,128]{1,0:T(8,128)S(1)}, f32[152,128]{1,0:T(8,128)S(1)}, u32[]{:S(2)}, u32[]{:S(2)}) collective-permute-start(f32[152,128]{1,0:T(8,128)S(1)} %add.55), channel_id=1, source_target_pairs={{0,20},{1,21},{2,22},{3,23},{4,16},{5,17},{6,18},{7,19},{8,28},{9,... | collective-permute-start | bytes 233480 | tf_op jit(solution)/shard_map/ppermute | solution.py:79
  49.6 4.9 %collective-permute-start.16 = (f32[152,128]{1,0:T(8,128)S(1)}, f32[152,128]{1,0:T(8,128)S(1)}, u32[]{:S(2)}, u32[]{:S(2)}) collective-permute-start(f32[152,128]{1,0:T(8,128)S(1)} %add_add_fusion.1), channel_id=1, source_target_pairs={{0,2},{1,129},{2,0},{3,131},{4,6},{5,133},{6,4},{7,135},{8,10},{9,... | collective-permute-start | bytes 233480 | tf_op jit(solution)/shard_map/ppermute | solution.py:79
  49.7 6.1 %collective-permute-start.18 = (f32[152,128]{1,0:T(8,128)S(1)}, f32[152,128]{1,0:T(8,128)S(1)}, u32[]{:S(2)}, u32[]{:S(2)}) collective-permute-start(f32[152,128]{1,0:T(8,128)S(1)} %add_add_fusion.1), channel_id=1, source_target_pairs={{0,32},{1,65},{2,34},{3,67},{4,36},{5,69},{6,38},{7,71},{8,40},{9,... | collective-permute-start | bytes 233480 | tf_op jit(solution)/shard_map/ppermute | solution.py:79
  49.8 6.1 %collective-permute-start.15 = (f32[152,128]{1,0:T(8,128)S(1)}, f32[152,128]{1,0:T(8,128)S(1)}, u32[]{:S(2)}, u32[]{:S(2)}) collective-permute-start(f32[152,128]{1,0:T(8,128)S(1)} %add_add_fusion.1), channel_id=1, source_target_pairs={{0,34},{1,193},{2,32},{3,195},{4,38},{5,197},{6,36},{7,199},{8,42}... | collective-permute-start | bytes 233480 | tf_op jit(solution)/shard_map/ppermute | solution.py:79
  55.9 6.8 %collective-permute-start.19 = (f32[408,128]{1,0:T(8,128)S(1)}, f32[408,128]{1,0:T(8,128)S(1)}, u32[]{:S(2)}, u32[]{:S(2)}) collective-permute-start(f32[408,128]{1,0:T(8,128)S(1)} %get-tuple-element.90.refs_4_), channel_id=1, source_target_pairs={{0,1},{1,0},{2,3},{3,2},{4,5},{5,4},{6,7},{7,6},{8,9},{9,8},{10,11... | collective-permute-start | bytes 626696 | tf_op jit(solution)/shard_map/ppermute | solution.py:79
  62.8 11.2 %collective-permute-start.22 = (f32[608,128]{1,0:T(8,128)S(1)}, f32[608,128]{1,0:T(8,128)S(1)}, u32[]{:S(2)}, u32[]{:S(2)}) collective-permute-start(f32[608,128]{1,0:T(8,128)S(1)} %constant_dynamic-update-slice_fusion.refs_0_), channel_id=1, source_target_pairs={{0,64},{1,33},{2,66},{3,35},{4,68},{5,37},{6,70},{7,39},{8,72},{9,... | collective-permute-start | bytes 933896 | tf_op jit(solution)/shard_map/ppermute | solution.py:79
  62.9 12.0 %collective-permute-start.21 = (f32[608,128]{1,0:T(8,128)S(1)}, f32[608,128]{1,0:T(8,128)S(1)}, u32[]{:S(2)}, u32[]{:S(2)}) collective-permute-start(f32[608,128]{1,0:T(8,128)S(1)} %constant_dynamic-update-slice_fusion.refs_0_), channel_id=1, source_target_pairs={{0,128},{1,3},{2,130},{3,1},{4,132},{5,7},{6,134},{7,5},{8,136},{9... | collective-permute-start | bytes 933896 | tf_op jit(solution)/shard_map/ppermute | solution.py:79
  67.0 9.1 %collective-permute-start.20 = (f32[608,128]{1,0:T(8,128)S(1)}, f32[608,128]{1,0:T(8,128)S(1)}, u32[]{:S(2)}, u32[]{:S(2)}) collective-permute-start(f32[608,128]{1,0:T(8,128)S(1)} %constant_dynamic-update-slice_fusion.refs_0_), channel_id=1, source_target_pairs={{0,192},{1,35},{2,194},{3,33},{4,196},{5,39},{6,198},{7,37},{8,200... | collective-permute-start | bytes 933896 | tf_op jit(solution)/shard_map/ppermute | solution.py:79
  67.0 9.7 %collective-permute-start.27 = (f32[408,128]{1,0:T(8,128)S(1)}, f32[408,128]{1,0:T(8,128)S(1)}, u32[]{:S(2)}, u32[]{:S(2)}) collective-permute-start(f32[408,128]{1,0:T(8,128)S(1)} %get-tuple-element.99), channel_id=1, source_target_pairs={{0,252},{1,253},{2,254},{3,255},{4,0},{5,1},{6,2},{7,3},{8,4},{9,5... | collective-permute-start | bytes 626696 | tf_op jit(solution)/shard_map/ppermute | solution.py:112
  74.0 4.2 %collective-permute-start.23 = (f32[608,128]{1,0:T(8,128)S(1)}, f32[608,128]{1,0:T(8,128)S(1)}, u32[]{:S(2)}, u32[]{:S(2)}) collective-permute-start(f32[608,128]{1,0:T(8,128)S(1)} %constant_dynamic-update-slice_fusion.refs_0_), channel_id=1, source_target_pairs={{0,1},{1,0},{2,3},{3,2},{4,5},{5,4},{6,7},{7,6},{8,9},{9,8},{10,11... | collective-permute-start | bytes 933896 | tf_op jit(solution)/shard_map/ppermute | solution.py:79
  74.0 4.2 %collective-permute-start.26 = (f32[608,128]{1,0:T(8,128)S(1)}, f32[608,128]{1,0:T(8,128)S(1)}, u32[]{:S(2)}, u32[]{:S(2)}) collective-permute-start(f32[608,128]{1,0:T(8,128)S(1)} %collective-permute-done.22.refs_3_), channel_id=1, source_target_pairs={{0,1},{1,0},{2,3},{3,2},{4,5},{5,4},{6,7},{7,6},{8,9},{9,8},{10,11... | collective-permute-start | bytes 933896 | tf_op jit(solution)/shard_map/ppermute | solution.py:79
  (5 other events, 13.0 us)
